TPU v7x, 512 devices: a whole 4x4x16 slice. The times are simulated.
512 devices in a mesh: row: 16 (over y, x), col: 32 (over z, core).
Axes of the slice: x: 4, y: 4, z: 16, core: 2. Of those that a mesh axis runs over, the one named last changes fastest.
Arguments:
- rhs_own: float32 [2, 2048, 512], P(None, 'row'), may hold values from -6 to 6
- inverse: bfloat16 [4096, 512], P('col'), as said below
- offdiag: bfloat16 [12288, 4096], P('row', 'col'), may hold values from -0.125 to 0.125
- pattern: int32 [8, 96], P(None, 'row'), may hold values from 0 to 9, as said below
- rhs_ext: float32 [16384, 512], P(('row', 'col')), may hold values from -6 to 6
Outputs:
- solution: bfloat16 [4096, 512], P('col')
- remainder: float32 [16384, 512], P(('row', 'col'))
Inputs may be any that keep to these rules, and one draw needn't show every extreme that they name: `pattern`: within one supernode and row group the 6 slots are distinct; a slot l < 2 of row group r appears for supernode s only when window tile l * 16 + r belongs to a supernode after s. `inverse`: each block of 512 rows is lower triangular with a positive diagonal.
All inputs are finite; a program needn't handle non-finite values.
Results may differ from a plain program's by a relative error of at most 0.0065.
Values may be sent and summed in bfloat16 or wider, within the bound.
No kernel may reach another device: no remote copies, remote signals or barrier semaphores. Data moves between devices by JAX's collectives and lax.ppermute only.
A program may use at most 64 MiB of HBM per device.

v0:
```python
import jax
import jax.numpy as jnp
from jax import lax
from jax.sharding import PartitionSpec as P


def local(rhs_own, inverse, offdiag, pattern, rhs_ext):
    groups = lax.axis_size("row")
    columns = lax.axis_size("col")
    row_id = lax.axis_index("row")
    col_id = lax.axis_index("col")
    tile_rows = offdiag.shape[1]
    node_width = inverse.shape[1]
    per_node = node_width // tile_rows
    supers = columns // per_node
    own_count = rhs_own.shape[0]
    rhs_cols = rhs_own.shape[2]
    blocks_count = offdiag.shape[0] // tile_rows
    ext_count = rhs_ext.shape[0] * columns // tile_rows
    slot_count = own_count + ext_count
    my_node = col_id // per_node
    my_pattern = lax.dynamic_index_in_dim(pattern, my_node, 0, keepdims=False)
    partial_value = jnp.zeros((slot_count, tile_rows, rhs_cols), jnp.float32)
    solution = jnp.zeros((tile_rows, rhs_cols), jnp.bfloat16)
    for section in range(supers):
        first_tile = per_node * section
        offset = (row_id - first_tile) % groups
        holder = offset < per_node
        slot_index = (first_tile + offset) // groups
        if section > 0:
            carried = lax.dynamic_index_in_dim(partial_value, slot_index, 0, keepdims=False)
            summed_updates = lax.psum(carried, "col")
        else:
            summed_updates = jnp.zeros((tile_rows, rhs_cols), jnp.float32)
        current = lax.dynamic_index_in_dim(rhs_own, slot_index, 0, keepdims=False) - summed_updates
        current_bf = current.astype(jnp.bfloat16)
        active = my_node == section

        def term_solve():
            col_slice = lax.dynamic_slice_in_dim(
                inverse, jnp.minimum(offset, per_node - 1) * tile_rows, tile_rows, 1
            )
            return jnp.dot(col_slice, current_bf, preferred_element_type=jnp.float32)

        term_part = lax.cond(
            active & holder, term_solve, lambda: jnp.zeros((tile_rows, rhs_cols), jnp.float32)
        )
        solved_sum = lax.psum(term_part, "row")
        solved = solved_sum.astype(jnp.bfloat16)
        solution = jnp.where(active, solved, solution)

        def apply_blocks():
            products = jnp.dot(offdiag, solved, preferred_element_type=jnp.float32)
            return partial_value.at[my_pattern].add(
                products.reshape(blocks_count, tile_rows, rhs_cols)
            )

        partial_value = lax.cond(active, apply_blocks, lambda: partial_value)
    ext_flat = partial_value[own_count:].reshape(ext_count * tile_rows, rhs_cols)
    below = lax.psum_scatter(ext_flat, "col", scatter_dimension=0, tiled=True)
    return (solution, rhs_ext - below)


def solution(mesh):
    return jax.shard_map(
        local,
        mesh=mesh,
        in_specs=(
            P(None, "row", None),
            P("col", None),
            P("row", "col"),
            P(None, "row"),
            P(("row", "col"), None),
        ),
        out_specs=(P("col", None), P(("row", "col"), None)),
        check_vma=False,
    )
```

profile of v0, /device:TPU:24, one launch (start us, length us, event | category | flops | bytes accessed | tf_op | source)
XLA Modules:
  0.0 2184.9 jit_solution(10662890306993543803)
XLA Ops:
  7.3 71.9 %all-reduce.29 = bf16[128,512]{1,0:T(8,128)(2,1)S(1)} all-reduce(f32[128,512]{1,0:T(8,128)S(1)} %get-tuple-element.325), channel_id=1, replica_groups=mesh['row'=16,'col'=32] {'row'}, use_global_device_ids=true, to_apply=%region_2.3 | all-reduce | flops 65536 | bytes 393216 | tf_op jit(solution)/shard_map/psum | solution.py:48
  79.3 7.1 conditional.17
  80.7 1.8 broadcast_in_dim.23
  82.5 3.9 scatter_fusion
  86.5 1.7 dynamic-slice_bitcast_fusion.6
  88.3 205.7 %all-reduce.16.cloned.1.call-done = f32[128,512]{1,0:T(8,128)} async-done(((f32[128,512]{1,0:T(8,128)}), f32[128,512]{1,0:T(8,128)}) %all-reduce.16.cloned.1.call-update) | async-done | bytes 262160 | tf_op jit(solution)/shard_map/psum | solution.py:32
  295.1 70.8 %all-reduce.30 = bf16[128,512]{1,0:T(8,128)(2,1)S(1)} all-reduce(f32[128,512]{1,0:T(8,128)S(1)} %get-tuple-element.327), channel_id=1, replica_groups=mesh['row'=16,'col'=32] {'row'}, use_global_device_ids=true, to_apply=%region_9.10 | all-reduce | flops 65536 | bytes 393216 | tf_op jit(solution)/shard_map/psum | solution.py:48
  365.9 1.7 dynamic-slice_bitcast_fusion.5
  367.8 207.8 %all-reduce.18.cloned.1.call-done = f32[128,512]{1,0:T(8,128)} async-done(((f32[128,512]{1,0:T(8,128)}), f32[128,512]{1,0:T(8,128)}) %all-reduce.18.cloned.1.call-update) | async-done | bytes 262160 | tf_op jit(solution)/shard_map/psum | solution.py:32
  576.6 70.8 %all-reduce.31 = bf16[128,512]{1,0:T(8,128)(2,1)S(1)} all-reduce(f32[128,512]{1,0:T(8,128)S(1)} %get-tuple-element.329), channel_id=1, replica_groups=mesh['row'=16,'col'=32] {'row'}, use_global_device_ids=true, to_apply=%region_16.17 | all-reduce | flops 65536 | bytes 393216 | tf_op jit(solution)/shard_map/psum | solution.py:48
  647.4 1.7 dynamic-slice_bitcast_fusion.4
  649.2 207.8 %all-reduce.20.cloned.1.call-done = f32[128,512]{1,0:T(8,128)} async-done(((f32[128,512]{1,0:T(8,128)}), f32[128,512]{1,0:T(8,128)}) %all-reduce.20.cloned.1.call-update) | async-done | bytes 262160 | tf_op jit(solution)/shard_map/psum | solution.py:32
  858.1 70.8 %all-reduce.32 = bf16[128,512]{1,0:T(8,128)(2,1)S(1)} all-reduce(f32[128,512]{1,0:T(8,128)S(1)} %get-tuple-element.331), channel_id=1, replica_groups=mesh['row'=16,'col'=32] {'row'}, use_global_device_ids=true, to_apply=%region_23.24 | all-reduce | flops 65536 | bytes 393216 | tf_op jit(solution)/shard_map/psum | solution.py:48
  928.9 1.7 dynamic-slice_bitcast_fusion.3
  930.7 210.1 %all-reduce.22.cloned.1.call-done = f32[128,512]{1,0:T(8,128)} async-done(((f32[128,512]{1,0:T(8,128)}), f32[128,512]{1,0:T(8,128)}) %all-reduce.22.cloned.1.call-update) | async-done | bytes 262160 | tf_op jit(solution)/shard_map/psum | solution.py:32
  1141.8 70.8 %all-reduce.33 = bf16[128,512]{1,0:T(8,128)(2,1)S(1)} all-reduce(f32[128,512]{1,0:T(8,128)S(1)} %get-tuple-element.333), channel_id=1, replica_groups=mesh['row'=16,'col'=32] {'row'}, use_global_device_ids=true, to_apply=%region_30.31 | all-reduce | flops 65536 | bytes 393216 | tf_op jit(solution)/shard_map/psum | solution.py:48
  1214.5 212.1 %all-reduce.24.cloned.1.call-done = f32[128,512]{1,0:T(8,128)} async-done(((f32[128,512]{1,0:T(8,128)}), f32[128,512]{1,0:T(8,128)}) %all-reduce.24.cloned.1.call-update) | async-done | bytes 262160 | tf_op jit(solution)/shard_map/psum | solution.py:32
  1427.6 70.8 %all-reduce.34 = bf16[128,512]{1,0:T(8,128)(2,1)S(1)} all-reduce(f32[128,512]{1,0:T(8,128)S(1)} %get-tuple-element.335), channel_id=1, replica_groups=mesh['row'=16,'col'=32] {'row'}, use_global_device_ids=true, to_apply=%region_37.38 | all-reduce | flops 65536 | bytes 393216 | tf_op jit(solution)/shard_map/psum | solution.py:48
  1500.2 207.9 %all-reduce.26.cloned.1.call-done = f32[128,512]{1,0:T(8,128)} async-done(((f32[128,512]{1,0:T(8,128)}), f32[128,512]{1,0:T(8,128)}) %all-reduce.26.cloned.1.call-update) | async-done | bytes 262160 | tf_op jit(solution)/shard_map/psum | solution.py:32
  1709.1 70.8 %all-reduce.35 = bf16[128,512]{1,0:T(8,128)(2,1)S(1)} all-reduce(f32[128,512]{1,0:T(8,128)S(1)} %get-tuple-element.337), channel_id=1, replica_groups=mesh['row'=16,'col'=32] {'row'}, use_global_device_ids=true, to_apply=%region_44.45 | all-reduce | flops 65536 | bytes 393216 | tf_op jit(solution)/shard_map/psum | solution.py:48
  1781.7 207.9 %all-reduce.28.cloned.1.call-done = f32[128,512]{1,0:T(8,128)} async-done(((f32[128,512]{1,0:T(8,128)}), f32[128,512]{1,0:T(8,128)}) %all-reduce.28.cloned.1.call-update) | async-done | bytes 262160 | tf_op jit(solution)/shard_map/psum | solution.py:32
  1990.6 70.8 %all-reduce.36 = bf16[128,512]{1,0:T(8,128)(2,1)S(1)} all-reduce(f32[128,512]{1,0:T(8,128)S(1)} %get-tuple-element.339), channel_id=1, replica_groups=mesh['row'=16,'col'=32] {'row'}, use_global_device_ids=true, to_apply=%region_51.52 | all-reduce | flops 65536 | bytes 393216 | tf_op jit(solution)/shard_map/psum | solution.py:48
  2061.4 3.1 slice.4
  2065.2 111.3 %reduce-scatter.2.cloned.1.call-done = f32[32,512]{1,0:T(8,128)} async-done(((f32[1024,512]{1,0:T(8,128)}), f32[32,512]{1,0:T(8,128)}) %reduce-scatter.2.cloned.1.call-update) | async-done | bytes 65552 | tf_op jit(solution)/shard_map/reduce_scatter | solution.py:60
  (64 shorter events, 16.6 us)
Async XLA Ops:
  7.2 72.1 %copy-start = (s32[8,6]{1,0:T(8,128)S(1)}, s32[8,6]{1,0:T(8,128)}, u32[]{:S(2)}) copy-start(s32[8,6]{1,0:T(8,128)} %param.40) | copy-start | bytes 580
  7.2 286.9 %all-reduce.16.cloned.1.call-start = ((), (), s32[]{:S(2)}) async-start(), calls=%async_computation.1 | async-start | bytes 524288 | tf_op jit(solution)/shard_map/psum | solution.py:32
  79.3 214.7 %copy-start.2 = (f32[2,128,512]{2,1,0:T(8,128)S(1)}, f32[2,128,512]{2,1,0:T(8,128)}, u32[]{:S(2)}) copy-start(f32[2,128,512]{2,1,0:T(8,128)} %param.37) | copy-start | bytes 1572868
  79.3 215.7 %copy-start.3 = (bf16[128,512]{1,0:T(8,128)(2,1)S(1)}, bf16[128,512]{1,0:T(8,128)(2,1)}, u32[]{:S(2)}) copy-start(bf16[128,512]{1,0:T(8,128)(2,1)} %param.38) | copy-start | bytes 393220
  86.5 279.4 %copy-start.1 = (bf16[768,128]{1,0:T(8,128)(2,1)S(1)}, bf16[768,128]{1,0:T(8,128)(2,1)}, u32[]{:S(2)}) copy-start(bf16[768,128]{1,0:T(8,128)(2,1)} %param.39) | copy-start | bytes 589828
  88.2 487.4 %all-reduce.18.cloned.1.call-start = ((), (), s32[]{:S(2)}) async-start(), calls=%async_computation.2 | async-start | bytes 524288 | tf_op jit(solution)/shard_map/psum | solution.py:32
  367.6 489.4 %all-reduce.20.cloned.1.call-start = ((), (), s32[]{:S(2)}) async-start(), calls=%async_computation.3 | async-start | bytes 524288 | tf_op jit(solution)/shard_map/psum | solution.py:32
  649.1 491.7 %all-reduce.22.cloned.1.call-start = ((), (), s32[]{:S(2)}) async-start(), calls=%async_computation.4 | async-start | bytes 524288 | tf_op jit(solution)/shard_map/psum | solution.py:32
  930.6 495.9 %all-reduce.24.cloned.1.call-start = ((), (), s32[]{:S(2)}) async-start(), calls=%async_computation.5 | async-start | bytes 524288 | tf_op jit(solution)/shard_map/psum | solution.py:32
  1214.4 493.7 %all-reduce.26.cloned.1.call-start = ((), (), s32[]{:S(2)}) async-start(), calls=%async_computation.6 | async-start | bytes 524288 | tf_op jit(solution)/shard_map/psum | solution.py:32
  1500.1 489.5 %all-reduce.28.cloned.1.call-start = ((), (), s32[]{:S(2)}) async-start(), calls=%async_computation.7 | async-start | bytes 524288 | tf_op jit(solution)/shard_map/psum | solution.py:32
  1781.7 394.9 %reduce-scatter.2.cloned.1.call-start = ((), (), s32[]{:S(2)}) async-start(), calls=%async_computation.8 | async-start | bytes 2162688 | tf_op jit(solution)/shard_map/reduce_scatter | solution.py:60
  2064.5 112.0 %copy-start.4 = (f32[32,512]{1,0:T(8,128)S(1)}, f32[32,512]{1,0:T(8,128)}, u32[]{:S(2)}) copy-start(f32[32,512]{1,0:T(8,128)} %param.41) | copy-start | bytes 196612
Sparse Core Ops, SparseCore 0:
  88.3 205.6 all-reduce.15
  367.8 207.7 all-reduce.17
  649.3 207.7 all-reduce.19
  930.7 210.0 all-reduce.21
  1214.5 211.9 all-reduce.23
  1500.2 207.8 all-reduce.25
  1781.8 207.7 all-reduce.27
  2064.7 111.8 reduce-scatter.1
where the time goes:
time: 2190 us; the launch traced here: 2180 us
  waiting for transfers between devices  1570 us (72%)
  blocking collectives  567 us (26%)
    psum x7, waiting for transfers between devices, local(): summed_updates = lax.psum(carried, 'col')  1460 us
    psum x8, blocking collectives, local(): solved_sum = lax.psum(term_part, 'row')  567 us
    reduce_scatter x1, waiting for transfers between devices, local(): below = lax.psum_scatter(ext_flat, 'col', scatter_dimension=0, tiled=True)  111 us
  transfers between devices with their start and end apart: 8, of which 8 were waited for; matrix products, arithmetic and copies ran while one was open for 0% of the time, Pallas kernels for 0%

commit v1 on v0

v1 whole, which is shorter than its diff:
```python
import jax
import jax.numpy as jnp
from jax import lax
from jax.experimental import pallas as pl
from jax.experimental.pallas import tpu as pltpu
from jax.sharding import PartitionSpec as P

AXES = ("row", "col")
NX, NY, NZ, NC = 4, 4, 16, 2
TILE = 128
SUPER = 8
TPS = 4
NZ_DEV = 6
OWN = 2
RHS = 512
RZ = RHS // NZ
KEEP = 14
CHUNK = KEEP + 1
HALF = 8
INV0 = NZ_DEV * TILE
BLOB = INV0 + TPS * TILE
F32 = jnp.float32
BF = jnp.bfloat16
VMEM = 60 * 1024 * 1024


def dev(y, x, z, k):
    return ((y % NY) * NX + x % NX) * (NZ * NC) + (z % NZ) * NC + k % NC


def every():
    for y in range(NY):
        for x in range(NX):
            for z in range(NZ):
                for k in range(NC):
                    yield y, x, z, k


def home(slot, y, z):
    if slot == 0:
        return y, z + KEEP - 2 * y
    if y == 3 and z >= 8:
        return 0, z
    if y == 2 and z >= 10:
        return 1, z
    return y, z


def balance_pairs():
    pairs = []
    for y, x, z, k in every():
        for slot in range(OWN):
            if z < 8 * slot + 2 * y:
                to = home(slot, y, z)
                if to != (y, z):
                    pairs.append((dev(y, x, z, k), dev(to[0], x, to[1], k)))
    return pairs


def ring_pairs(stage, step):
    pairs = []
    for y, x, z, k in every():
        along_x = (k == 0) == (stage == 0)
        to = dev(y, x + step, z, k) if along_x else dev(y + step, x, z, k)
        pairs.append((dev(y, x, z, k), to))
    return pairs


def swap_pairs():
    return [(dev(y, x, z, k), dev(y, x, z, 1 - k)) for y, x, z, k in every()]


def move(value, pairs):
    return lax.ppermute(value, AXES, pairs)


def nt(a, b):
    return lax.dot_general(a, b, (((1,), (1,)), ((), ())), preferred_element_type=F32)


def prep_kernel(meta, off, inv, rhs, blob, send, keep, btile, flat):
    blob[:INV0] = off[...]
    for j in range(TPS):
        blob[INV0 + j * TILE : INV0 + (j + 1) * TILE] = inv[:, j * TILE : (j + 1) * TILE]
    tiles = []
    for slot in range(OWN):
        tile = jnp.zeros((TILE, TILE), F32)
        for k in range(NZ_DEV):
            block = off[k * TILE : (k + 1) * TILE].astype(F32)
            tile = jnp.where(meta[k] == slot, block, tile)
        tiles.append(tile)
    keep[...] = tiles[1].astype(BF)
    send[...] = jnp.where(meta[6] == 0, tiles[0], tiles[1]).astype(BF)
    start = pl.multiple_of(meta[7], RZ)
    for slot in range(OWN):
        flat[...] = rhs[slot].T
        part = flat[pl.ds(start, RZ), :]
        high = part.astype(BF)
        btile[slot * 2 * RZ : slot * 2 * RZ + RZ] = high
        btile[slot * 2 * RZ + RZ : (slot + 1) * 2 * RZ] = (part - high.astype(F32)).astype(BF)


def prep(meta, off, inv, rhs):
    tile = jax.ShapeDtypeStruct((TILE, TILE), BF)
    vm = pl.BlockSpec(memory_space=pltpu.VMEM)
    return pl.pallas_call(
        prep_kernel,
        out_shape=(jax.ShapeDtypeStruct((BLOB, TILE), BF), tile, tile, tile),
        in_specs=[pl.BlockSpec(memory_space=pltpu.SMEM), vm, vm, vm],
        out_specs=(vm, vm, vm, vm),
        scratch_shapes=[pltpu.VMEM((RHS, TILE), F32)],
        compiler_params=pltpu.CompilerParams(vmem_limit_bytes=VMEM),
    )(meta, off, inv, rhs)


PIECES = ((0, 4), (4, 4), (8, 2), (10, 2), (12, 4))


def solve_kernel(meta, pattern, *refs):
    pieces = refs[:10]
    blobs, out, factor, blob, upd, ext, sol, sems, bsems = refs[10:]
    core = meta[32]
    copies = []
    for h in range(2):
        for p, (first, count) in enumerate(PIECES):
            copies.append(
                pltpu.make_async_copy(
                    pieces[h * 5 + p], factor.at[h, pl.ds(first, count)], sems.at[h * 5 + p]
                )
            )
    loads = [
        pltpu.make_async_copy(
            blobs.at[pl.ds(s * TPS, TPS)], blob.at[pl.ds(s * TPS, TPS)], bsems.at[s]
        )
        for s in range(SUPER)
    ]
    for c in copies:
        c.start()
    for c in loads:
        c.start()
    upd[...] = jnp.zeros_like(upd)
    ext[...] = jnp.zeros_like(ext)
    for c in copies:
        c.wait()

    def block(parity, y, x, place):
        return factor[parity ^ core, meta[parity * 16 + y * NX + x], place]

    def rhs_tile(t):
        slot, r = t // 16, t % 16
        where = jnp.where(core == 0, meta[r], meta[16 + r])
        base = slot * 2 * RZ
        high = factor[0, where, KEEP, base : base + RZ].astype(F32)
        low = factor[0, where, KEEP, base + RZ : base + 2 * RZ].astype(F32)
        return high + low

    for s in range(SUPER):
        loads[s].wait()
        current = jnp.concatenate(
            [(rhs_tile(t) - upd[t]).astype(BF) for t in range(s * TPS, (s + 1) * TPS)], axis=1
        )
        solved = []
        for i in range(TPS):
            c = s * TPS + i
            rows = jnp.concatenate(
                [blob[c, INV0 + j * TILE : INV0 + (j + 1) * TILE] for j in range(i + 1)], axis=1
            )
            x_i = nt(current[:, : (i + 1) * TILE], rows).astype(BF)
            sol[c] = x_i
            solved.append(x_i)
        x_s = jnp.concatenate(solved, axis=1)
        for t in range((s + 1) * TPS, SUPER * TPS):
            slot, y, x = t // 16, t % 16 // NX, t % NX
            parts = []
            for j in range(TPS):
                at_y, place = home(slot, y, 2 * s + j // 2)
                parts.append(block(j % 2, at_y, x, place))
            upd[t] += nt(x_s, jnp.concatenate(parts, axis=1))
        for k in range(NZ_DEV):
            row0 = pl.multiple_of(k * TILE + core * 32, 32)
            row1 = pl.multiple_of(k * TILE + core * 32 + 64, 32)
            tops = [blob[s * TPS + j, pl.ds(row0, 32)] for j in range(TPS)]
            lows = [blob[s * TPS + j, pl.ds(row1, 32)] for j in range(TPS)]
            rows = jnp.concatenate(
                [jnp.concatenate(tops, axis=1), jnp.concatenate(lows, axis=1)], axis=0
            )
            ext[pattern[s * NZ_DEV + k]] += nt(x_s, rows)
    for z in range(NZ):
        out[z, :RZ] = sol[2 * z + core]
        part = ext[OWN + z // 2][:, (z % 2) * 32 : (z % 2) * 32 + 32]
        high = part.astype(BF)
        low = (part - high.astype(F32)).astype(BF)
        out[z, RZ:] = jnp.concatenate(
            [high, low, jnp.zeros((RZ, TILE - 64), BF)], axis=1
        )


def solve(meta, pattern, pieces, blobs):
    sm = pl.BlockSpec(memory_space=pltpu.SMEM)
    hbm = pl.BlockSpec(memory_space=pl.ANY)
    return pl.pallas_call(
        solve_kernel,
        out_shape=jax.ShapeDtypeStruct((NZ, 2 * RZ, TILE), BF),
        in_specs=[sm, sm] + [hbm] * 11,
        out_specs=pl.BlockSpec(memory_space=pltpu.VMEM),
        scratch_shapes=[
            pltpu.VMEM((2, 16, CHUNK, TILE, TILE), BF),
            pltpu.VMEM((SUPER * TPS, BLOB, TILE), BF),
            pltpu.VMEM((SUPER * TPS, RZ, TILE), F32),
            pltpu.VMEM((10, RZ, 64), F32),
            pltpu.VMEM((SUPER * TPS, RZ, TILE), BF),
            pltpu.SemaphoreType.DMA((10,)),
            pltpu.SemaphoreType.DMA((SUPER,)),
        ],
        compiler_params=pltpu.CompilerParams(vmem_limit_bytes=VMEM),
    )(meta, pattern, *pieces, blobs)


def finish_kernel(got, rhs_ext, solution, remainder):
    x = jnp.concatenate([got[z, :RZ].astype(F32) for z in range(NZ)], axis=0)
    solution[...] = x.T.astype(BF)
    tail = jnp.concatenate([got[z, RZ:].astype(F32) for z in range(NZ)], axis=0).T
    remainder[...] = rhs_ext[...] - (tail[:32] + tail[32:64])


def finish(got, rhs_ext):
    return pl.pallas_call(
        finish_kernel,
        out_shape=(
            jax.ShapeDtypeStruct((TILE, RHS), BF),
            jax.ShapeDtypeStruct((32, RHS), F32),
        ),
        compiler_params=pltpu.CompilerParams(vmem_limit_bytes=VMEM),
    )(got, rhs_ext)


def local(rhs_own, inverse, offdiag, pattern, rhs_ext):
    row, col = lax.axis_index("row"), lax.axis_index("col")
    y, x, z, core = row // NX, row % NX, col // NC, col % NC
    groups = [[NC * i + k for i in range(NZ)] for k in range(NC)]
    mine = lax.dynamic_index_in_dim(pattern, col // TPS, 0, keepdims=False)
    sends_first = z < 2 * y
    meta = jnp.concatenate(
        [mine, jnp.stack([jnp.where(sends_first, 0, 1), z * RZ]).astype(jnp.int32)]
    )
    blob, send, keep, btile = prep(meta, offdiag, inverse, rhs_own)
    blobs = lax.all_gather(blob, "col")
    got = move(send, balance_pairs())
    gets = (z < KEEP) & (z >= jnp.where((y == 0) | (y == 3), 8, 10))
    one = jnp.where(gets, got, keep)
    line = lax.all_gather(one, "col", axis_index_groups=groups)
    chunk = jnp.concatenate([line[:KEEP], btile[None]], axis=0)

    right = move(chunk, ring_pairs(0, -1))
    left = move(chunk, ring_pairs(0, 1))
    far = jnp.concatenate(
        [move(right[:HALF], ring_pairs(0, -1)), move(left[HALF:], ring_pairs(0, 1))], axis=0
    )
    first = jnp.stack([chunk, right, far, left])
    right = move(first, ring_pairs(1, -1))
    left = move(first, ring_pairs(1, 1))
    far_a = move(right[:2], ring_pairs(1, -1))
    far_b = move(left[2:], ring_pairs(1, 1))
    pieces = [first, right, far_a, far_b, left]
    pieces += [move(p, swap_pairs()) for p in pieces]

    places = []
    for parity in range(2):
        for r in range(16):
            dy, dx = (r // NX - y) % NY, (r % NX - x) % NX
            places.append(dy * 4 + dx if parity == 0 else dx * 4 + dy)
    table = jnp.stack(places + [core]).astype(jnp.int32)
    packed = solve(table, pattern.reshape(-1), pieces, blobs)
    home_again = lax.all_to_all(packed, "col", 0, 0, tiled=True, axis_index_groups=groups)
    return finish(home_again, rhs_ext)


def solution(mesh):
    return jax.shard_map(
        local,
        mesh=mesh,
        in_specs=(
            P(None, "row", None),
            P("col", None),
            P("row", "col"),
            P(None, "row"),
            P(("row", "col"), None),
        ),
        out_specs=(P("col", None), P(("row", "col"), None)),
        check_vma=False,
    )
```

time: 2190 us -> 206 us (0.09)
  waiting for transfers between devices: 1570 us -> 44.6 us
  blocking collectives: 567 us -> 65.8 us
  starting transfers between devices: 0.32 us -> 51.7 us
    psum x7 -> x0, waiting for transfers between devices: 1460 us -> none  [local(): summed_updates = lax.psum(carried, 'col')]
    psum x8 -> x0, blocking collectives: 567 us -> none  [local(): solved_sum = lax.psum(term_part, 'row')]
    reduce_scatter x1 -> x0, waiting for transfers between devices: 111 us -> none  [local(): below = lax.psum_scatter(ext_flat, 'col', scatter_dimension=0, tiled=True)]
    ppermute x0 -> x14, starting transfers between devices: none -> 51.7 us  [move(): return lax.ppermute(value, AXES, pairs)]
    ppermute x0 -> x14, waiting for transfers between devices: none -> 44.6 us  [move(): return lax.ppermute(value, AXES, pairs)]
    all_gather x0 -> x1, blocking collectives: none -> 37.8 us  [local(): line = lax.all_gather(one, 'col', axis_index_groups=groups)]
    all_to_all x0 -> x1, blocking collectives: none -> 27.9 us  [local(): lax.all_to_all(packed, 'col', 0, 0, tiled=True, axis_index_groups=groups)]
    pallas_call x0 -> x3, Pallas kernels: none -> 21.9 us  [the longest x1 18.1 us: solve(): pl.pallas_call(solve_kernel, out_shape=jax.ShapeDtypeStruct((NZ, 2 * RZ,...]
  transfers between devices with their start and end apart: 8 -> 15, of which waited for: 8 -> 7; matrix products, arithmetic and copies ran while one was open for 0% -> 3% of each run, Pallas kernels for 0% -> 0%
where the time goes in v1:
time: 206 us
  blocking collectives  65.8 us (32%)
  starting transfers between devices  51.7 us (25%)
  waiting for transfers between devices  44.6 us (22%)
  Pallas kernels  21.9 us (11%)
  between operations  14.5 us (7%)
  local copies, waits for them, and re-layouts  4.58 us (2%)
  other arithmetic  2.48 us (1%)
    ppermute x14, starting transfers between devices, move(): return lax.ppermute(value, AXES, pairs)  51.7 us
    ppermute x14, waiting for transfers between devices, move(): return lax.ppermute(value, AXES, pairs)  44.6 us
    all_gather x1, blocking collectives, local(): line = lax.all_gather(one, 'col', axis_index_groups=groups)  37.8 us
    all_to_all x1, blocking collectives, local(): lax.all_to_all(packed, 'col', 0, 0, tiled=True, axis_index_groups=groups)  27.9 us
    pallas_call x1, Pallas kernels, solve(): pl.pallas_call(solve_kernel, out_shape=jax.ShapeDtypeStruct((NZ, 2 * RZ,...  18.1 us
  transfers between devices with their start and end apart: 15, of which 7 were waited for; matrix products, arithmetic and copies ran while one was open for 3% of the time, Pallas kernels for 0%

profile of v1, /device:TPU:24, one launch (start us, length us, event | category | flops | bytes accessed | tf_op | source)
XLA Modules:
  0.0 205.5 jit_solution(8073939831255875566)
XLA Ops:
  8.6 2.1 %shard_map.68 = (bf16[1280,128]{1,0:T(8,128)(2,1)}, bf16[128,128]{1,0:T(8,128)(2,1)}, bf16[128,128]{1,0:T(8,128)(2,1)}, bf16[128,128]{1,0:T(8,128)(2,1)}) custom-call(s32[8]{0:T(128)} %pad_add_fusion.meta, bf16[768,128]{1,0:T(8,128)(2,1)} %off.1, bf16[128,512]{1,0:T(8,128)(2,1)} %inv.1, f32[2,128,512]{2,1,0:T(8,128)} %rhs.1), custom_call_target="tpu_custom_call" | custom-call | tf_op jit(solution)/shard_map/pallas_call | solution.py:106
  10.7 15.7 %collective-permute-start = (bf16[128,128]{1,0:T(8,128)(2,1)}, bf16[128,128]{1,0:T(8,128)(2,1)S(1)}, u32[]{:S(2)}, u32[]{:S(2)}) collective-permute-start(bf16[128,128]{1,0:T(8,128)(2,1)} %get-tuple-element.6), channel_id=1, source_target_pairs={{128,152},{129,153},{130,154},{131,155},{160,184},{161,185},{162,1... | collective-permute-start | bytes 98312 | tf_op jit(solution)/shard_map/ppermute | solution.py:74
  26.5 1.9 collective-permute-done
  29.1 37.8 %all-gather = bf16[2048,128]{1,0:T(8,128)(2,1)S(1)} all-gather(bf16[128,128]{1,0:T(8,128)(2,1)S(1)} %broadcast_select_fusion), channel_id=2, replica_groups={{0,2,4,6,8,10,12,14,16,18,20,22,24,26,28,30},{1,3,5,7,9,11,13,15,17,19,..., dimensions={0}, use_global_device_ids=true | all-gather | bytes 557056 | tf_op jit(solution)/shard_map/all_gather | solution.py:251
  67.8 4.7 %collective-permute-start.1 = (bf16[15,128,128]{2,1,0:T(8,128)(2,1)S(1)}, bf16[15,128,128]{2,1,0:T(8,128)(2,1)S(1)}, u32[]{:S(2)}, u32[]{:S(2)}) collective-permute-start(bf16[15,128,128]{2,1,0:T(8,128)(2,1)S(1)} %get-tuple-element.11), channel_id=1, source_target_pairs={{0,96},{1,385},{2,98},{3,387},{4,100},{5,389},{6,102},{7,391},{8,1... | collective-permute-start | bytes 1474568 | tf_op jit(solution)/shard_map/ppermute | solution.py:74
  72.5 1.9 collective-permute-start.3
  74.4 4.4 %collective-permute-done.1 = bf16[15,128,128]{2,1,0:T(8,128)(2,1)S(1)} collective-permute-done((bf16[15,128,128]{2,1,0:T(8,128)(2,1)S(1)}, bf16[15,128,128]{2,1,0:T(8,128)(2,1)S(1)}, u32[]{:S(2)}, u32[]{:S(2)}) %collective-permute-start.1) | collective-permute-done | bytes 491552 | tf_op jit(solution)/shard_map/ppermute | solution.py:74
  78.8 5.6 %collective-permute-start.2 = (bf16[8,128,128]{2,1,0:T(8,128)(2,1)S(1)}, bf16[8,128,128]{2,1,0:T(8,128)(2,1)S(1)}, u32[]{:S(2)}, u32[]{:S(2)}) collective-permute-start(bf16[8,128,128]{2,1,0:T(8,128)(2,1)S(1)} %slice.22), channel_id=1, source_target_pairs={{0,96},{1,385},{2,98},{3,387},{4,100},{5,389},{6,102},{7,391},{8,1... | collective-permute-start | bytes 786440 | tf_op jit(solution)/shard_map/ppermute | solution.py:74
  84.5 1.9 collective-permute-start.4
  86.4 9.7 %collective-permute-done.4 = bf16[7,128,128]{2,1,0:T(8,128)(2,1)S(1)} collective-permute-done((bf16[7,128,128]{2,1,0:T(8,128)(2,1)S(1)}, bf16[7,128,128]{2,1,0:T(8,128)(2,1)S(1)}, u32[]{:S(2)}, u32[]{:S(2)}) %collective-permute-start.4) | collective-permute-done | bytes 229408 | tf_op jit(solution)/shard_map/ppermute | solution.py:74
  96.4 2.1 collective-permute-start.7
  98.5 3.9 %collective-permute-start.5 = (bf16[4,15,128,128]{3,2,1,0:T(8,128)(2,1)S(1)}, bf16[4,15,128,128]{3,2,1,0:T(8,128)(2,1)}, u32[]{:S(2)}, u32[]{:S(2)}) collective-permute-start(bf16[4,15,128,128]{3,2,1,0:T(8,128)(2,1)S(1)} %pad_maximum_fusion.refs_0_), channel_id=1, source_target_pairs={{0,384},{1,97},{2,386},{3,99},{4,388},{5,101},{6,390},{7,103},{8,3... | collective-permute-start | bytes 5898248 | tf_op jit(solution)/shard_map/ppermute | solution.py:74
  102.4 1.9 collective-permute-start.9
  104.4 18.8 %collective-permute-done.7.refs_4_ = bf16[4,15,128,128]{3,2,1,0:T(8,128)(2,1)} collective-permute-done((bf16[4,15,128,128]{3,2,1,0:T(8,128)(2,1)S(1)}, bf16[4,15,128,128]{3,2,1,0:T(8,128)(2,1)}, u32[]{:S(2)}, u32[]{:S(2)}) %collective-permute-start.7) | collective-permute-done | bytes 1966112 | tf_op jit(solution)/shard_map/ppermute | solution.py:74
  124.5 3.1 %collective-permute-start.8 = (bf16[2,15,128,128]{3,2,1,0:T(8,128)(2,1)S(1)}, bf16[2,15,128,128]{3,2,1,0:T(8,128)(2,1)S(1)}, u32[]{:S(2)}, u32[]{:S(2)}) collective-permute-start(bf16[2,15,128,128]{3,2,1,0:T(8,128)(2,1)S(1)} %slice.25), channel_id=1, source_target_pairs={{0,128},{1,33},{2,130},{3,35},{4,132},{5,37},{6,134},{7,39},{8,136... | collective-permute-start | bytes 2949128 | tf_op jit(solution)/shard_map/ppermute | solution.py:74
  128.9 2.7 %collective-permute-start.6 = (bf16[2,15,128,128]{3,2,1,0:T(8,128)(2,1)S(1)}, bf16[2,15,128,128]{3,2,1,0:T(8,128)(2,1)}, u32[]{:S(2)}, u32[]{:S(2)}) collective-permute-start(bf16[2,15,128,128]{3,2,1,0:T(8,128)(2,1)S(1)} %slice.24), channel_id=1, source_target_pairs={{0,384},{1,97},{2,386},{3,99},{4,388},{5,101},{6,390},{7,103},{8,3... | collective-permute-start | bytes 2949128 | tf_op jit(solution)/shard_map/ppermute | solution.py:74
  131.6 1.9 collective-permute-start.13
  133.5 2.4 %collective-permute-start.10 = (bf16[4,15,128,128]{3,2,1,0:T(8,128)(2,1)}, bf16[4,15,128,128]{3,2,1,0:T(8,128)(2,1)}, u32[]{:S(2)}, u32[]{:S(2)}) collective-permute-start(bf16[4,15,128,128]{3,2,1,0:T(8,128)(2,1)} %collective-permute-done.5.refs_1_), channel_id=1, source_target_pairs={{0,1},{1,0},{2,3},{3,2},{4,5},{5,4},{6,7},{7,6},{8,9},{9,8},{10,11... | collective-permute-start | bytes 5898248 | tf_op jit(solution)/shard_map/ppermute | solution.py:74
  135.9 4.5 %collective-permute-done.8.refs_3_ = bf16[2,15,128,128]{3,2,1,0:T(8,128)(2,1)S(1)} collective-permute-done((bf16[2,15,128,128]{3,2,1,0:T(8,128)(2,1)S(1)}, bf16[2,15,128,128]{3,2,1,0:T(8,128)(2,1)S(1)}, u32[]{:S(2)}, u32[]{:S(2)}) %collective-permute-start.8) | collective-permute-done | bytes 983072 | tf_op jit(solution)/shard_map/ppermute | solution.py:74
  140.5 1.9 collective-permute-start.12
  142.4 3.8 %collective-permute-done.6.refs_2_ = bf16[2,15,128,128]{3,2,1,0:T(8,128)(2,1)} collective-permute-done((bf16[2,15,128,128]{3,2,1,0:T(8,128)(2,1)S(1)}, bf16[2,15,128,128]{3,2,1,0:T(8,128)(2,1)}, u32[]{:S(2)}, u32[]{:S(2)}) %collective-permute-start.6) | collective-permute-done | bytes 983072 | tf_op jit(solution)/shard_map/ppermute | solution.py:74
  146.2 1.9 collective-permute-start.11
  151.0 18.1 %shard_map.69 = bf16[16,64,128]{2,1,0:T(8,128)(2,1)} custom-call(s32[33]{0:T(128)} %stack.156.meta, s32[48]{0:T(128)} %reshape.7.pattern, bf16[4,15,128,128]{3,2,1,0:T(8,128)(2,1)} %copy-done, bf16[4,15,128,128]{3,2,1,0:T(8,128)(2,1)} %collective-permute-done.5.refs_1_, bf16[2,15,128,128]{3,2,1,0:T(8,128)(2,1)} %collective-permute-done.6.refs_2_, ...), custom_call_target="tpu_custom_call" | custom-call | tf_op jit(solution)/shard_map/pallas_call | solution.py:201
  169.1 27.9 %all_to_all.5.got = bf16[16,64,128]{2,1,0:T(8,128)(2,1)} all-to-all(bf16[16,64,128]{2,1,0:T(8,128)(2,1)} %shard_map.69), channel_id=1, replica_groups={{0,2,4,6,8,10,12,14,16,18,20,22,24,26,28,30},{1,3,5,7,9,11,13,15,17,19,..., dimensions={0} | all-to-all | bytes 524288 | tf_op jit(solution)/shard_map/all_to_all | solution.py:274
  (31 shorter events, 10.3 us)
Async XLA Ops:
  7.2 143.8 %all-gather.4.cloned.1.call-start = ((), (), s32[]{:S(2)}) async-start(), calls=%async_computation.1 | async-start | bytes 10813440 | tf_op jit(solution)/shard_map/all_gather | solution.py:247
  10.7 17.6 %collective-permute-start = (bf16[128,128]{1,0:T(8,128)(2,1)}, bf16[128,128]{1,0:T(8,128)(2,1)S(1)}, u32[]{:S(2)}, u32[]{:S(2)}) collective-permute-start(bf16[128,128]{1,0:T(8,128)(2,1)} %get-tuple-element.6), channel_id=1, source_target_pairs={{128,152},{129,153},{130,154},{131,155},{160,184},{161,185},{162,1... | collective-permute-start | bytes 98312 | tf_op jit(solution)/shard_map/ppermute | solution.py:74
  67.8 11.0 %collective-permute-start.1 = (bf16[15,128,128]{2,1,0:T(8,128)(2,1)S(1)}, bf16[15,128,128]{2,1,0:T(8,128)(2,1)S(1)}, u32[]{:S(2)}, u32[]{:S(2)}) collective-permute-start(bf16[15,128,128]{2,1,0:T(8,128)(2,1)S(1)} %get-tuple-element.11), channel_id=1, source_target_pairs={{0,96},{1,385},{2,98},{3,387},{4,100},{5,389},{6,102},{7,391},{8,1... | collective-permute-start | bytes 1474568 | tf_op jit(solution)/shard_map/ppermute | solution.py:74
  72.5 12.0 %collective-permute-start.3 = (bf16[15,128,128]{2,1,0:T(8,128)(2,1)S(1)}, bf16[15,128,128]{2,1,0:T(8,128)(2,1)S(1)}, u32[]{:S(2)}, u32[]{:S(2)}) collective-permute-start(bf16[15,128,128]{2,1,0:T(8,128)(2,1)S(1)} %get-tuple-element.11), channel_id=1, source_target_pairs={{0,32},{1,129},{2,34},{3,131},{4,36},{5,133},{6,38},{7,135},{8,40}... | collective-permute-start | bytes 1474568 | tf_op jit(solution)/shard_map/ppermute | solution.py:74
  78.8 17.3 %collective-permute-start.2 = (bf16[8,128,128]{2,1,0:T(8,128)(2,1)S(1)}, bf16[8,128,128]{2,1,0:T(8,128)(2,1)S(1)}, u32[]{:S(2)}, u32[]{:S(2)}) collective-permute-start(bf16[8,128,128]{2,1,0:T(8,128)(2,1)S(1)} %slice.22), channel_id=1, source_target_pairs={{0,96},{1,385},{2,98},{3,387},{4,100},{5,389},{6,102},{7,391},{8,1... | collective-permute-start | bytes 786440 | tf_op jit(solution)/shard_map/ppermute | solution.py:74
  84.5 11.6 %collective-permute-start.4 = (bf16[7,128,128]{2,1,0:T(8,128)(2,1)S(1)}, bf16[7,128,128]{2,1,0:T(8,128)(2,1)S(1)}, u32[]{:S(2)}, u32[]{:S(2)}) collective-permute-start(bf16[7,128,128]{2,1,0:T(8,128)(2,1)S(1)} %slice.23), channel_id=1, source_target_pairs={{0,32},{1,129},{2,34},{3,131},{4,36},{5,133},{6,38},{7,135},{8,40}... | collective-permute-start | bytes 688136 | tf_op jit(solution)/shard_map/ppermute | solution.py:74
  96.4 51.7 %copy-start = (bf16[4,15,128,128]{3,2,1,0:T(8,128)(2,1)}, bf16[4,15,128,128]{3,2,1,0:T(8,128)(2,1)S(1)}, u32[]{:S(2)}) copy-start(bf16[4,15,128,128]{3,2,1,0:T(8,128)(2,1)S(1)} %pad_maximum_fusion.refs_0_) | copy-start | bytes 5898244
  96.4 51.9 %copy-start.2 = (s32[8,6]{1,0:T(8,128)S(1)}, s32[8,6]{1,0:T(8,128)}, u32[]{:S(2)}) copy-start(s32[8,6]{1,0:T(8,128)} %param.8) | copy-start | bytes 580
  96.4 26.8 %collective-permute-start.7 = (bf16[4,15,128,128]{3,2,1,0:T(8,128)(2,1)S(1)}, bf16[4,15,128,128]{3,2,1,0:T(8,128)(2,1)}, u32[]{:S(2)}, u32[]{:S(2)}) collective-permute-start(bf16[4,15,128,128]{3,2,1,0:T(8,128)(2,1)S(1)} %pad_maximum_fusion.refs_0_), channel_id=1, source_target_pairs={{0,128},{1,33},{2,130},{3,35},{4,132},{5,37},{6,134},{7,39},{8,136... | collective-permute-start | bytes 5898248 | tf_op jit(solution)/shard_map/ppermute | solution.py:74
  98.5 29.1 %collective-permute-start.5 = (bf16[4,15,128,128]{3,2,1,0:T(8,128)(2,1)S(1)}, bf16[4,15,128,128]{3,2,1,0:T(8,128)(2,1)}, u32[]{:S(2)}, u32[]{:S(2)}) collective-permute-start(bf16[4,15,128,128]{3,2,1,0:T(8,128)(2,1)S(1)} %pad_maximum_fusion.refs_0_), channel_id=1, source_target_pairs={{0,384},{1,97},{2,386},{3,99},{4,388},{5,101},{6,390},{7,103},{8,3... | collective-permute-start | bytes 5898248 | tf_op jit(solution)/shard_map/ppermute | solution.py:74
  102.4 47.1 %collective-permute-start.9 = (bf16[4,15,128,128]{3,2,1,0:T(8,128)(2,1)S(1)}, bf16[4,15,128,128]{3,2,1,0:T(8,128)(2,1)}, u32[]{:S(2)}, u32[]{:S(2)}) collective-permute-start(bf16[4,15,128,128]{3,2,1,0:T(8,128)(2,1)S(1)} %pad_maximum_fusion.refs_0_), channel_id=1, source_target_pairs={{0,1},{1,0},{2,3},{3,2},{4,5},{5,4},{6,7},{7,6},{8,9},{9,8},{10,11... | collective-permute-start | bytes 5898248 | tf_op jit(solution)/shard_map/ppermute | solution.py:74
  124.5 16.0 %collective-permute-start.8 = (bf16[2,15,128,128]{3,2,1,0:T(8,128)(2,1)S(1)}, bf16[2,15,128,128]{3,2,1,0:T(8,128)(2,1)S(1)}, u32[]{:S(2)}, u32[]{:S(2)}) collective-permute-start(bf16[2,15,128,128]{3,2,1,0:T(8,128)(2,1)S(1)} %slice.25), channel_id=1, source_target_pairs={{0,128},{1,33},{2,130},{3,35},{4,132},{5,37},{6,134},{7,39},{8,136... | collective-permute-start | bytes 2949128 | tf_op jit(solution)/shard_map/ppermute | solution.py:74
  128.9 17.3 %collective-permute-start.6 = (bf16[2,15,128,128]{3,2,1,0:T(8,128)(2,1)S(1)}, bf16[2,15,128,128]{3,2,1,0:T(8,128)(2,1)}, u32[]{:S(2)}, u32[]{:S(2)}) collective-permute-start(bf16[2,15,128,128]{3,2,1,0:T(8,128)(2,1)S(1)} %slice.24), channel_id=1, source_target_pairs={{0,384},{1,97},{2,386},{3,99},{4,388},{5,101},{6,390},{7,103},{8,3... | collective-permute-start | bytes 2949128 | tf_op jit(solution)/shard_map/ppermute | solution.py:74
  131.6 18.0 %collective-permute-start.13 = (bf16[4,15,128,128]{3,2,1,0:T(8,128)(2,1)}, bf16[4,15,128,128]{3,2,1,0:T(8,128)(2,1)}, u32[]{:S(2)}, u32[]{:S(2)}) collective-permute-start(bf16[4,15,128,128]{3,2,1,0:T(8,128)(2,1)} %collective-permute-done.7.refs_4_), channel_id=1, source_target_pairs={{0,1},{1,0},{2,3},{3,2},{4,5},{5,4},{6,7},{7,6},{8,9},{9,8},{10,11... | collective-permute-start | bytes 5898248 | tf_op jit(solution)/shard_map/ppermute | solution.py:74
  133.5 17.5 %collective-permute-start.10 = (bf16[4,15,128,128]{3,2,1,0:T(8,128)(2,1)}, bf16[4,15,128,128]{3,2,1,0:T(8,128)(2,1)}, u32[]{:S(2)}, u32[]{:S(2)}) collective-permute-start(bf16[4,15,128,128]{3,2,1,0:T(8,128)(2,1)} %collective-permute-done.5.refs_1_), channel_id=1, source_target_pairs={{0,1},{1,0},{2,3},{3,2},{4,5},{5,4},{6,7},{7,6},{8,9},{9,8},{10,11... | collective-permute-start | bytes 5898248 | tf_op jit(solution)/shard_map/ppermute | solution.py:74
  140.5 10.5 %copy-start.1 = (bf16[2,15,128,128]{3,2,1,0:T(8,128)(2,1)}, bf16[2,15,128,128]{3,2,1,0:T(8,128)(2,1)S(1)}, u32[]{:S(2)}) copy-start(bf16[2,15,128,128]{3,2,1,0:T(8,128)(2,1)S(1)} %collective-permute-done.8.refs_3_) | copy-start | bytes 2949124
  140.5 9.1 %collective-permute-start.12 = (bf16[2,15,128,128]{3,2,1,0:T(8,128)(2,1)S(1)}, bf16[2,15,128,128]{3,2,1,0:T(8,128)(2,1)}, u32[]{:S(2)}, u32[]{:S(2)}) collective-permute-start(bf16[2,15,128,128]{3,2,1,0:T(8,128)(2,1)S(1)} %collective-permute-done.8.refs_3_), channel_id=1, source_target_pairs={{0,1},{1,0},{2,3},{3,2},{4,5},{5,4},{6,7},{7,6},{8,9},{9,8},{10,11... | collective-permute-start | bytes 2949128 | tf_op jit(solution)/shard_map/ppermute | solution.py:74
  146.2 4.8 %collective-permute-start.11 = (bf16[2,15,128,128]{3,2,1,0:T(8,128)(2,1)}, bf16[2,15,128,128]{3,2,1,0:T(8,128)(2,1)}, u32[]{:S(2)}, u32[]{:S(2)}) collective-permute-start(bf16[2,15,128,128]{3,2,1,0:T(8,128)(2,1)} %collective-permute-done.6.refs_2_), channel_id=1, source_target_pairs={{0,1},{1,0},{2,3},{3,2},{4,5},{5,4},{6,7},{7,6},{8,9},{9,8},{10,11... | collective-permute-start | bytes 2949128 | tf_op jit(solution)/shard_map/ppermute | solution.py:74
Sparse Core Ops, SparseCore 0:
  10.8 89.6 all-gather.3

commit v2 on v1

v2 whole, which is shorter than its diff:
```python
import jax
import jax.numpy as jnp
from jax import lax
from jax.experimental import pallas as pl
from jax.experimental.pallas import tpu as pltpu
from jax.sharding import PartitionSpec as P

AXES = ("row", "col")
NX, NY, NZ, NC = 4, 4, 16, 2
TILE = 128
SUPER = 8
TPS = 4
NZ_DEV = 6
OWN = 2
RHS = 512
RZ = RHS // NZ
KEEP = 14
CHUNK = KEEP + 1
EARLY = 11
RHS_AT = 10
INV0 = NZ_DEV * TILE
BLOB = INV0 + TPS * TILE
BLOCKS = NZ_DEV + TPS
F32 = jnp.float32
BF = jnp.bfloat16
VMEM = 60 * 1024 * 1024


def dev(y, x, z, k):
    return ((y % NY) * NX + x % NX) * (NZ * NC) + (z % NZ) * NC + k % NC


def every():
    for y in range(NY):
        for x in range(NX):
            for z in range(NZ):
                for k in range(NC):
                    yield y, x, z, k


def home(slot, y, z):
    if slot == 0:
        return y, z + KEEP - 2 * y
    if y == 3 and z >= 8:
        return 0, z
    if y == 2 and z >= 10:
        return 1, z
    return y, z


def place_of(z):
    if z < 4:
        return z
    return z + 7 if z < 8 else z - 4


def balance_pairs():
    pairs = []
    for y, x, z, k in every():
        for slot in range(OWN):
            if z < 8 * slot + 2 * y:
                to = home(slot, y, z)
                if to != (y, z):
                    pairs.append((dev(y, x, z, k), dev(to[0], x, to[1], k)))
    return pairs


def first_groups():
    groups = []
    for z in range(NZ):
        for k in range(NC):
            for a in range(4):
                groups.append([dev(a, b, z, k) if k == 0 else dev(b, a, z, k) for b in range(4)])
    return groups


def ring_pairs(step):
    return [
        (dev(y, x, z, k), dev(y + step, x, z, k) if k == 0 else dev(y, x + step, z, k))
        for y, x, z, k in every()
    ]


def swap_pairs():
    return [(dev(y, x, z, k), dev(y, x, z, 1 - k)) for y, x, z, k in every()]


def move(value, pairs):
    return lax.ppermute(value, AXES, pairs)


def nt(a, b):
    return lax.dot_general(a, b, (((1,), (1,)), ((), ())), preferred_element_type=F32)


def coordinates():
    row, col = lax.axis_index("row"), lax.axis_index("col")
    return row >> 2, row & 3, col >> 1, col & 1


def prep_kernel(pattern, off, inv, rhs, blob, send, keep, btile, flat):
    y, _, z, _ = coordinates()
    blob[:INV0] = off[...]
    for j in range(TPS):
        blob[INV0 + j * TILE : INV0 + (j + 1) * TILE] = inv[:, j * TILE : (j + 1) * TILE]
    tiles = []
    for slot in range(OWN):
        tile = jnp.zeros((TILE, TILE), F32)
        for k in range(NZ_DEV):
            block = off[k * TILE : (k + 1) * TILE].astype(F32)
            tile = jnp.where(pattern[z >> 1, k] == slot, block, tile)
        tiles.append(tile)
    keep[...] = tiles[1].astype(BF)
    send[...] = jnp.where(z < 2 * y, tiles[0], tiles[1]).astype(BF)
    start = pl.multiple_of(z * RZ, RZ)
    for slot in range(OWN):
        flat[...] = rhs[slot].T
        part = flat[pl.ds(start, RZ), :]
        high = part.astype(BF)
        btile[slot * 2 * RZ : slot * 2 * RZ + RZ] = high
        btile[slot * 2 * RZ + RZ : (slot + 1) * 2 * RZ] = (part - high.astype(F32)).astype(BF)


def prep(pattern, off, inv, rhs):
    tile = jax.ShapeDtypeStruct((TILE, TILE), BF)
    vm = pl.BlockSpec(memory_space=pltpu.VMEM)
    return pl.pallas_call(
        prep_kernel,
        out_shape=(jax.ShapeDtypeStruct((BLOB, TILE), BF), tile, tile, tile),
        in_specs=[pl.BlockSpec(memory_space=pltpu.SMEM), vm, vm, vm],
        out_specs=(vm, vm, vm, vm),
        scratch_shapes=[pltpu.VMEM((RHS, TILE), F32)],
        compiler_params=pltpu.CompilerParams(vmem_limit_bytes=VMEM),
    )(pattern, off, inv, rhs)


PIECES = ((0, 4), (4, 4), (8, 2), (10, 2), (12, 4))


def solve_kernel(pattern, *refs):
    pieces = refs[:10]
    blobs, out, factor, invs, rows_ext, upd, ext, sol, early, late, isems, esems = refs[10:]
    my_y, my_x, _, core = coordinates()

    def load(first, count, sems):
        return [
            pltpu.make_async_copy(
                pieces[h * 5 + p].at[:, pl.ds(first, count)],
                factor.at[h, pl.ds(at, blocks), pl.ds(first, count)],
                sems.at[h * 5 + p],
            )
            for h in range(2)
            for p, (at, blocks) in enumerate(PIECES)
        ]

    first_loads = load(0, EARLY, early)
    last_loads = load(EARLY, CHUNK - EARLY, late)
    inv_loads, ext_loads = [], []
    for s in range(SUPER):
        four = pl.ds(s * TPS, TPS)
        inv_loads.append(
            pltpu.make_async_copy(
                blobs.at[four, pl.ds(NZ_DEV, TPS)], invs.at[four], isems.at[s]
            )
        )
        ext_loads.append(
            pltpu.make_async_copy(
                blobs.at[four, pl.ds(0, NZ_DEV), :, core], rows_ext.at[four], esems.at[s]
            )
        )
    for c in first_loads[:5] + inv_loads[:1] + first_loads[5:] + inv_loads[1:2] + last_loads:
        c.start()
    for c in inv_loads[2:] + ext_loads:
        c.start()
    upd[...] = jnp.zeros_like(upd)
    ext[...] = jnp.zeros_like(ext)
    for c in first_loads:
        c.wait()

    def position(parity, y, x):
        if parity == 0:
            return ((y - my_y) & 3) * 4 + x
        return ((x - my_x) & 3) * 4 + y

    def block(parity, y, x, place):
        return factor[parity ^ core, position(parity, y, x), place]

    def rhs_tile(t):
        slot, y, x = t // 16, t % 16 // NX, t % NX
        where = jnp.where(core == 0, position(0, y, x), position(1, y, x))
        base = slot * 2 * RZ
        high = factor[0, where, RHS_AT, base : base + RZ].astype(F32)
        low = factor[0, where, RHS_AT, base + RZ : base + 2 * RZ].astype(F32)
        return high + low

    for s in range(SUPER):
        inv_loads[s].wait()
        if s == 2:
            for c in last_loads:
                c.wait()
        current = jnp.concatenate(
            [(rhs_tile(t) - upd[t]).astype(BF) for t in range(s * TPS, (s + 1) * TPS)], axis=1
        )
        solved = []
        for i in range(TPS):
            c = s * TPS + i
            rows = jnp.concatenate(
                [invs[c, j].reshape(TILE, TILE) for j in range(i + 1)], axis=1
            )
            x_i = nt(current[:, : (i + 1) * TILE], rows).astype(BF)
            sol[c] = x_i
            solved.append(x_i)
        x_s = jnp.concatenate(solved, axis=1)
        for t in range((s + 1) * TPS, SUPER * TPS):
            slot, y, x = t // 16, t % 16 // NX, t % NX
            parts = []
            for j in range(TPS):
                at_y, plane = home(slot, y, 2 * s + j // 2)
                parts.append(block(j % 2, at_y, x, place_of(plane)))
            upd[t] += nt(x_s, jnp.concatenate(parts, axis=1))
    for s in range(SUPER):
        ext_loads[s].wait()
        x_s = jnp.concatenate([sol[s * TPS + j] for j in range(TPS)], axis=1)
        for k in range(NZ_DEV):
            rows = jnp.concatenate(
                [rows_ext[s * TPS + j, k].reshape(64, TILE) for j in range(TPS)], axis=1
            )
            ext[pattern[s, k]] += nt(x_s, rows)
    for z in range(NZ):
        out[z, :RZ] = sol[2 * z + core]
        part = ext[OWN + z // 2][:, (z % 2) * 32 : (z % 2) * 32 + 32]
        high = part.astype(BF)
        low = (part - high.astype(F32)).astype(BF)
        out[z, RZ:] = jnp.concatenate(
            [high, low, jnp.zeros((RZ, TILE - 64), BF)], axis=1
        )


def solve(pattern, pieces, blobs):
    hbm = pl.BlockSpec(memory_space=pl.ANY)
    return pl.pallas_call(
        solve_kernel,
        out_shape=jax.ShapeDtypeStruct((NZ, 2 * RZ, TILE), BF),
        in_specs=[pl.BlockSpec(memory_space=pltpu.SMEM)] + [hbm] * 11,
        out_specs=pl.BlockSpec(memory_space=pltpu.VMEM),
        scratch_shapes=[
            pltpu.VMEM((2, 16, CHUNK, TILE, TILE), BF),
            pltpu.VMEM((SUPER * TPS, TPS, 2, 2, 32, TILE), BF),
            pltpu.VMEM((SUPER * TPS, NZ_DEV, 2, 32, TILE), BF),
            pltpu.VMEM((SUPER * TPS, RZ, TILE), F32),
            pltpu.VMEM((10, RZ, 64), F32),
            pltpu.VMEM((SUPER * TPS, RZ, TILE), BF),
            pltpu.SemaphoreType.DMA((10,)),
            pltpu.SemaphoreType.DMA((10,)),
            pltpu.SemaphoreType.DMA((SUPER,)),
            pltpu.SemaphoreType.DMA((SUPER,)),
        ],
        compiler_params=pltpu.CompilerParams(vmem_limit_bytes=VMEM),
    )(pattern, *pieces, blobs)


def finish_kernel(got, rhs_ext, solution, remainder):
    x = jnp.concatenate([got[z, :RZ].astype(F32) for z in range(NZ)], axis=0)
    solution[...] = x.T.astype(BF)
    tail = jnp.concatenate([got[z, RZ:].astype(F32) for z in range(NZ)], axis=0).T
    remainder[...] = rhs_ext[...] - (tail[:32] + tail[32:64])


def finish(got, rhs_ext):
    return pl.pallas_call(
        finish_kernel,
        out_shape=(
            jax.ShapeDtypeStruct((TILE, RHS), BF),
            jax.ShapeDtypeStruct((32, RHS), F32),
        ),
        compiler_params=pltpu.CompilerParams(vmem_limit_bytes=VMEM),
    )(got, rhs_ext)


def local(rhs_own, inverse, offdiag, pattern, rhs_ext):
    y, _, z, _ = coordinates()
    groups = [[NC * i + k for i in range(NZ)] for k in range(NC)]
    blob, send, keep, btile = prep(pattern, offdiag, inverse, rhs_own)
    blobs = lax.all_gather(blob, "col")
    got = move(send, balance_pairs())
    gets = (z < KEEP) & (z >= jnp.where((y == 0) | (y == 3), 8, 10))
    one = jnp.where(gets, got, keep)
    line = lax.all_gather(one, "col", axis_index_groups=groups)
    chunk = jnp.concatenate([line[:4], line[8:KEEP], btile[None], line[4:8]], axis=0)
    four = jnp.broadcast_to(chunk[None], (4, CHUNK, TILE, TILE))
    first = lax.all_to_all(four, AXES, 0, 0, tiled=True, axis_index_groups=first_groups())
    right = move(first, ring_pairs(-1))
    left = move(first, ring_pairs(1))
    far_a = move(right[:2], ring_pairs(-1))
    far_b = move(left[2:], ring_pairs(1))
    pieces = [first, right, far_a, far_b, left]
    pieces += [move(p, swap_pairs()) for p in pieces]
    packed = solve(pattern, pieces, blobs.reshape(NZ * NC, BLOCKS, 2, 2, 32, TILE))
    home_again = lax.all_to_all(packed, "col", 0, 0, tiled=True, axis_index_groups=groups)
    return finish(home_again, rhs_ext)


def solution(mesh):
    return jax.shard_map(
        local,
        mesh=mesh,
        in_specs=(
            P(None, "row", None),
            P("col", None),
            P("row", "col"),
            P(None, "row"),
            P(("row", "col"), None),
        ),
        out_specs=(P("col", None), P(("row", "col"), None)),
        check_vma=False,
    )
```

time: 206 us -> 193 us (0.937)
  blocking collectives: 65.8 us -> 88.3 us
  starting transfers between devices: 51.7 us -> 37.5 us
  waiting for transfers between devices: 44.6 us -> 31.3 us
  Pallas kernels: 21.9 us -> 18.6 us
  local copies, waits for them, and re-layouts: 4.58 us -> 1.78 us
    all_to_all x0 -> x1, blocking collectives: none -> 23.8 us  [local(): lax.all_to_all(four, AXES, 0, 0, tiled=True, axis_index_groups=first_grou...]
    ppermute x14 -> x10, starting transfers between devices: 51.7 us -> 37.5 us  [move(): return lax.ppermute(value, AXES, pairs)]
    ppermute x14 -> x10, waiting for transfers between devices: 44.6 us -> 31.3 us  [move(): return lax.ppermute(value, AXES, pairs)]
    pallas_call x1, Pallas kernels: 18.1 us -> 14.7 us  [solve(): pl.pallas_call(solve_kernel, out_shape=jax.ShapeDtypeStruct((NZ, 2 * RZ,...]
    slice x5 -> x4, local copies, waits for them, and re-layouts: 2.6 us -> 0.22 us  [the longest x1 0.09 us: local(): far_a = move(right[:2], ring_pairs(-1))]
  transfers between devices with their start and end apart: 15 -> 11, of which waited for: 7 -> 5; matrix products, arithmetic and copies ran while one was open for 3% -> 1% of each run, Pallas kernels for 0% -> 0%
where the time goes in v2:
time: 193 us
  blocking collectives  88.3 us (46%)
  starting transfers between devices  37.5 us (19%)
  waiting for transfers between devices  31.3 us (16%)
  Pallas kernels  18.6 us (10%)
  between operations  14.3 us (7%)
    all_gather x1, blocking collectives, local(): line = lax.all_gather(one, 'col', axis_index_groups=groups)  37.6 us
    ppermute x10, starting transfers between devices, move(): return lax.ppermute(value, AXES, pairs)  37.5 us
    ppermute x10, waiting for transfers between devices, move(): return lax.ppermute(value, AXES, pairs)  31.3 us
    all_to_all x1, blocking collectives, local(): lax.all_to_all(packed, 'col', 0, 0, tiled=True, axis_index_groups=groups)  26.8 us
    all_to_all x1, blocking collectives, local(): lax.all_to_all(four, AXES, 0, 0, tiled=True, axis_index_groups=first_grou...  23.8 us
    pallas_call x1, Pallas kernels, solve(): pl.pallas_call(solve_kernel, out_shape=jax.ShapeDtypeStruct((NZ, 2 * RZ,...  14.7 us
  transfers between devices with their start and end apart: 11, of which 5 were waited for; matrix products, arithmetic and copies ran while one was open for 1% of the time, Pallas kernels for 0%

profile of v2, /device:TPU:24, one launch (start us, length us, event | category | flops | bytes accessed | tf_op | source)
XLA Modules:
  0.0 192.6 jit_solution(9685934084044421267)
XLA Ops:
  7.2 2.1 %shard_map.68 = (bf16[1280,128]{1,0:T(8,128)(2,1)}, bf16[128,128]{1,0:T(8,128)(2,1)}, bf16[128,128]{1,0:T(8,128)(2,1)}, bf16[128,128]{1,0:T(8,128)(2,1)}) custom-call(s32[8,6]{1,0:T(8,128)} %pattern.3, bf16[768,128]{1,0:T(8,128)(2,1)} %off.1, bf16[128,512]{1,0:T(8,128)(2,1)} %inv.1, f32[2,128,512]{2,1,0:T(8,128)} %rhs.1), custom_call_target="tpu_custom_call" | custom-call | tf_op jit(solution)/shard_map/pallas_call | solution.py:127
  9.4 15.7 %collective-permute-start = (bf16[128,128]{1,0:T(8,128)(2,1)}, bf16[128,128]{1,0:T(8,128)(2,1)S(1)}, u32[]{:S(2)}, u32[]{:S(2)}) collective-permute-start(bf16[128,128]{1,0:T(8,128)(2,1)} %get-tuple-element.6), channel_id=1, source_target_pairs={{128,152},{129,153},{130,154},{131,155},{160,184},{161,185},{162,1... | collective-permute-start | bytes 98312 | tf_op jit(solution)/shard_map/ppermute | solution.py:89
  25.1 1.9 collective-permute-done
  27.0 0.8 broadcast_select_fusion
  27.8 37.6 %all-gather = bf16[2048,128]{1,0:T(8,128)(2,1)S(1)} all-gather(bf16[128,128]{1,0:T(8,128)(2,1)S(1)} %broadcast_select_fusion), channel_id=2, replica_groups={{0,2,4,6,8,10,12,14,16,18,20,22,24,26,28,30},{1,3,5,7,9,11,13,15,17,19,..., dimensions={0}, use_global_device_ids=true | all-gather | bytes 557056 | tf_op jit(solution)/shard_map/all_gather | solution.py:288
  65.5 0.5 broadcast_in_dim.10
  66.0 23.8 %all_to_all.10.refs_0_ = bf16[4,15,128,128]{3,2,1,0:T(8,128)(2,1)S(1)} all-to-all(bf16[4,15,128,128]{3,2,1,0:T(8,128)(2,1)S(1)} %broadcast_in_dim.10), channel_id=1, replica_groups={{0,32,64,96},{128,160,192,224},{256,288,320,352},{384,416,448,480},{1,1..., dimensions={0} | all-to-all | bytes 3932160 | tf_op jit(solution)/shard_map/all_to_all | solution.py:291
  89.9 1.9 collective-permute-start.3
  91.8 3.9 %collective-permute-start.1 = (bf16[4,15,128,128]{3,2,1,0:T(8,128)(2,1)S(1)}, bf16[4,15,128,128]{3,2,1,0:T(8,128)(2,1)S(1)}, u32[]{:S(2)}, u32[]{:S(2)}) collective-permute-start(bf16[4,15,128,128]{3,2,1,0:T(8,128)(2,1)S(1)} %all_to_all.10.refs_0_), channel_id=1, source_target_pairs={{0,384},{1,97},{2,386},{3,99},{4,388},{5,101},{6,390},{7,103},{8,3... | collective-permute-start | bytes 5898248 | tf_op jit(solution)/shard_map/ppermute | solution.py:89
  95.7 1.9 collective-permute-start.5
  97.6 18.7 %collective-permute-done.3.refs_4_ = bf16[4,15,128,128]{3,2,1,0:T(8,128)(2,1)S(1)} collective-permute-done((bf16[4,15,128,128]{3,2,1,0:T(8,128)(2,1)S(1)}, bf16[4,15,128,128]{3,2,1,0:T(8,128)(2,1)S(1)}, u32[]{:S(2)}, u32[]{:S(2)}) %collective-permute-start.3) | collective-permute-done | bytes 1966112 | tf_op jit(solution)/shard_map/ppermute | solution.py:89
  116.5 3.1 %collective-permute-start.4 = (bf16[2,15,128,128]{3,2,1,0:T(8,128)(2,1)S(1)}, bf16[2,15,128,128]{3,2,1,0:T(8,128)(2,1)S(1)}, u32[]{:S(2)}, u32[]{:S(2)}) collective-permute-start(bf16[2,15,128,128]{3,2,1,0:T(8,128)(2,1)S(1)} %slice.27), channel_id=1, source_target_pairs={{0,128},{1,33},{2,130},{3,35},{4,132},{5,37},{6,134},{7,39},{8,136... | collective-permute-start | bytes 2949128 | tf_op jit(solution)/shard_map/ppermute | solution.py:89
  119.7 2.7 %collective-permute-start.2 = (bf16[2,15,128,128]{3,2,1,0:T(8,128)(2,1)S(1)}, bf16[2,15,128,128]{3,2,1,0:T(8,128)(2,1)S(1)}, u32[]{:S(2)}, u32[]{:S(2)}) collective-permute-start(bf16[2,15,128,128]{3,2,1,0:T(8,128)(2,1)S(1)} %slice.26), channel_id=1, source_target_pairs={{0,384},{1,97},{2,386},{3,99},{4,388},{5,101},{6,390},{7,103},{8,3... | collective-permute-start | bytes 2949128 | tf_op jit(solution)/shard_map/ppermute | solution.py:89
  122.4 1.9 collective-permute-start.9
  124.4 2.4 %collective-permute-start.6 = (bf16[4,15,128,128]{3,2,1,0:T(8,128)(2,1)S(1)}, bf16[4,15,128,128]{3,2,1,0:T(8,128)(2,1)}, u32[]{:S(2)}, u32[]{:S(2)}) collective-permute-start(bf16[4,15,128,128]{3,2,1,0:T(8,128)(2,1)S(1)} %collective-permute-done.1.refs_1_), channel_id=1, source_target_pairs={{0,1},{1,0},{2,3},{3,2},{4,5},{5,4},{6,7},{7,6},{8,9},{9,8},{10,11... | collective-permute-start | bytes 5898248 | tf_op jit(solution)/shard_map/ppermute | solution.py:89
  126.8 5.7 %collective-permute-done.4.refs_3_ = bf16[2,15,128,128]{3,2,1,0:T(8,128)(2,1)S(1)} collective-permute-done((bf16[2,15,128,128]{3,2,1,0:T(8,128)(2,1)S(1)}, bf16[2,15,128,128]{3,2,1,0:T(8,128)(2,1)S(1)}, u32[]{:S(2)}, u32[]{:S(2)}) %collective-permute-start.4) | collective-permute-done | bytes 983072 | tf_op jit(solution)/shard_map/ppermute | solution.py:89
  132.5 1.9 collective-permute-start.8
  134.4 2.5 %collective-permute-done.2.refs_2_ = bf16[2,15,128,128]{3,2,1,0:T(8,128)(2,1)S(1)} collective-permute-done((bf16[2,15,128,128]{3,2,1,0:T(8,128)(2,1)S(1)}, bf16[2,15,128,128]{3,2,1,0:T(8,128)(2,1)S(1)}, u32[]{:S(2)}, u32[]{:S(2)}) %collective-permute-start.2) | collective-permute-done | bytes 983072 | tf_op jit(solution)/shard_map/ppermute | solution.py:89
  136.9 1.9 collective-permute-start.7
  138.9 2.5 %collective-permute-done.7.refs_7_ = bf16[2,15,128,128]{3,2,1,0:T(8,128)(2,1)S(1)} collective-permute-done((bf16[2,15,128,128]{3,2,1,0:T(8,128)(2,1)S(1)}, bf16[2,15,128,128]{3,2,1,0:T(8,128)(2,1)S(1)}, u32[]{:S(2)}, u32[]{:S(2)}) %collective-permute-start.7) | collective-permute-done | bytes 983072 | tf_op jit(solution)/shard_map/ppermute | solution.py:89
  141.4 1.1 copy-done.8
  142.5 14.7 %shard_map.69 = bf16[16,64,128]{2,1,0:T(8,128)(2,1)} custom-call(s32[8,6]{1,0:T(8,128)} %pattern.3, bf16[4,15,128,128]{3,2,1,0:T(8,128)(2,1)} %copy-done, bf16[4,15,128,128]{3,2,1,0:T(8,128)(2,1)} %copy-done.2, bf16[2,15,128,128]{3,2,1,0:T(8,128)(2,1)} %copy-done.6, bf16[2,15,128,128]{3,2,1,0:T(8,128)(2,1)} %copy-done.5, ...), custom_call_target="tpu_custom_call" | custom-call | tf_op jit(solution)/shard_map/pallas_call | solution.py:241
  157.2 26.8 %all_to_all.11.got = bf16[16,64,128]{2,1,0:T(8,128)(2,1)} all-to-all(bf16[16,64,128]{2,1,0:T(8,128)(2,1)} %shard_map.69), channel_id=1, replica_groups={{0,2,4,6,8,10,12,14,16,18,20,22,24,26,28,30},{1,3,5,7,9,11,13,15,17,19,..., dimensions={0} | all-to-all | bytes 524288 | tf_op jit(solution)/shard_map/all_to_all | solution.py:299
  184.0 1.7 shard_map.70
  (32 shorter events, 0.4 us)
Async XLA Ops:
  7.2 135.3 %all-gather.4.cloned.1.call-start = ((), (), s32[]{:S(2)}) async-start(), calls=%async_computation.2 | async-start | bytes 10813440 | tf_op jit(solution)/shard_map/all_gather | solution.py:284
  9.4 56.1 %copy-start.9 = (bf16[128,128]{1,0:T(8,128)(2,1)S(1)}, bf16[128,128]{1,0:T(8,128)(2,1)}, u32[]{:S(2)}) copy-start(bf16[128,128]{1,0:T(8,128)(2,1)} %get-tuple-element.8) | copy-start | bytes 98308
  9.4 17.6 %collective-permute-start = (bf16[128,128]{1,0:T(8,128)(2,1)}, bf16[128,128]{1,0:T(8,128)(2,1)S(1)}, u32[]{:S(2)}, u32[]{:S(2)}) collective-permute-start(bf16[128,128]{1,0:T(8,128)(2,1)} %get-tuple-element.6), channel_id=1, source_target_pairs={{128,152},{129,153},{130,154},{131,155},{160,184},{161,185},{162,1... | collective-permute-start | bytes 98312 | tf_op jit(solution)/shard_map/ppermute | solution.py:89
  89.9 52.6 %copy-start = (bf16[4,15,128,128]{3,2,1,0:T(8,128)(2,1)}, bf16[4,15,128,128]{3,2,1,0:T(8,128)(2,1)S(1)}, u32[]{:S(2)}) copy-start(bf16[4,15,128,128]{3,2,1,0:T(8,128)(2,1)S(1)} %all_to_all.10.refs_0_) | copy-start | bytes 5898244
  89.9 26.5 %collective-permute-start.3 = (bf16[4,15,128,128]{3,2,1,0:T(8,128)(2,1)S(1)}, bf16[4,15,128,128]{3,2,1,0:T(8,128)(2,1)S(1)}, u32[]{:S(2)}, u32[]{:S(2)}) collective-permute-start(bf16[4,15,128,128]{3,2,1,0:T(8,128)(2,1)S(1)} %all_to_all.10.refs_0_), channel_id=1, source_target_pairs={{0,128},{1,33},{2,130},{3,35},{4,132},{5,37},{6,134},{7,39},{8,136... | collective-permute-start | bytes 5898248 | tf_op jit(solution)/shard_map/ppermute | solution.py:89
  91.8 27.8 %collective-permute-start.1 = (bf16[4,15,128,128]{3,2,1,0:T(8,128)(2,1)S(1)}, bf16[4,15,128,128]{3,2,1,0:T(8,128)(2,1)S(1)}, u32[]{:S(2)}, u32[]{:S(2)}) collective-permute-start(bf16[4,15,128,128]{3,2,1,0:T(8,128)(2,1)S(1)} %all_to_all.10.refs_0_), channel_id=1, source_target_pairs={{0,384},{1,97},{2,386},{3,99},{4,388},{5,101},{6,390},{7,103},{8,3... | collective-permute-start | bytes 5898248 | tf_op jit(solution)/shard_map/ppermute | solution.py:89
  95.7 43.1 %collective-permute-start.5 = (bf16[4,15,128,128]{3,2,1,0:T(8,128)(2,1)S(1)}, bf16[4,15,128,128]{3,2,1,0:T(8,128)(2,1)S(1)}, u32[]{:S(2)}, u32[]{:S(2)}) collective-permute-start(bf16[4,15,128,128]{3,2,1,0:T(8,128)(2,1)S(1)} %all_to_all.10.refs_0_), channel_id=1, source_target_pairs={{0,1},{1,0},{2,3},{3,2},{4,5},{5,4},{6,7},{7,6},{8,9},{9,8},{10,11... | collective-permute-start | bytes 5898248 | tf_op jit(solution)/shard_map/ppermute | solution.py:89
  116.4 22.5 %copy-start.1 = (bf16[4,15,128,128]{3,2,1,0:T(8,128)(2,1)}, bf16[4,15,128,128]{3,2,1,0:T(8,128)(2,1)S(1)}, u32[]{:S(2)}) copy-start(bf16[4,15,128,128]{3,2,1,0:T(8,128)(2,1)S(1)} %collective-permute-done.3.refs_4_) | copy-start | bytes 5898244
  116.5 16.0 %collective-permute-start.4 = (bf16[2,15,128,128]{3,2,1,0:T(8,128)(2,1)S(1)}, bf16[2,15,128,128]{3,2,1,0:T(8,128)(2,1)S(1)}, u32[]{:S(2)}, u32[]{:S(2)}) collective-permute-start(bf16[2,15,128,128]{3,2,1,0:T(8,128)(2,1)S(1)} %slice.27), channel_id=1, source_target_pairs={{0,128},{1,33},{2,130},{3,35},{4,132},{5,37},{6,134},{7,39},{8,136... | collective-permute-start | bytes 2949128 | tf_op jit(solution)/shard_map/ppermute | solution.py:89
  119.6 19.3 %copy-start.2 = (bf16[4,15,128,128]{3,2,1,0:T(8,128)(2,1)}, bf16[4,15,128,128]{3,2,1,0:T(8,128)(2,1)S(1)}, u32[]{:S(2)}) copy-start(bf16[4,15,128,128]{3,2,1,0:T(8,128)(2,1)S(1)} %collective-permute-done.1.refs_1_) | copy-start | bytes 5898244
  119.7 17.2 %collective-permute-start.2 = (bf16[2,15,128,128]{3,2,1,0:T(8,128)(2,1)S(1)}, bf16[2,15,128,128]{3,2,1,0:T(8,128)(2,1)S(1)}, u32[]{:S(2)}, u32[]{:S(2)}) collective-permute-start(bf16[2,15,128,128]{3,2,1,0:T(8,128)(2,1)S(1)} %slice.26), channel_id=1, source_target_pairs={{0,384},{1,97},{2,386},{3,99},{4,388},{5,101},{6,390},{7,103},{8,3... | collective-permute-start | bytes 2949128 | tf_op jit(solution)/shard_map/ppermute | solution.py:89
  122.4 16.5 %collective-permute-start.9 = (bf16[4,15,128,128]{3,2,1,0:T(8,128)(2,1)S(1)}, bf16[4,15,128,128]{3,2,1,0:T(8,128)(2,1)S(1)}, u32[]{:S(2)}, u32[]{:S(2)}) collective-permute-start(bf16[4,15,128,128]{3,2,1,0:T(8,128)(2,1)S(1)} %collective-permute-done.3.refs_4_), channel_id=1, source_target_pairs={{0,1},{1,0},{2,3},{3,2},{4,5},{5,4},{6,7},{7,6},{8,9},{9,8},{10,11... | collective-permute-start | bytes 5898248 | tf_op jit(solution)/shard_map/ppermute | solution.py:89
  124.4 18.1 %collective-permute-start.6 = (bf16[4,15,128,128]{3,2,1,0:T(8,128)(2,1)S(1)}, bf16[4,15,128,128]{3,2,1,0:T(8,128)(2,1)}, u32[]{:S(2)}, u32[]{:S(2)}) collective-permute-start(bf16[4,15,128,128]{3,2,1,0:T(8,128)(2,1)S(1)} %collective-permute-done.1.refs_1_), channel_id=1, source_target_pairs={{0,1},{1,0},{2,3},{3,2},{4,5},{5,4},{6,7},{7,6},{8,9},{9,8},{10,11... | collective-permute-start | bytes 5898248 | tf_op jit(solution)/shard_map/ppermute | solution.py:89
  132.5 10.0 %copy-start.5 = (bf16[2,15,128,128]{3,2,1,0:T(8,128)(2,1)}, bf16[2,15,128,128]{3,2,1,0:T(8,128)(2,1)S(1)}, u32[]{:S(2)}) copy-start(bf16[2,15,128,128]{3,2,1,0:T(8,128)(2,1)S(1)} %collective-permute-done.4.refs_3_) | copy-start | bytes 2949124
  132.5 6.4 %collective-permute-start.8 = (bf16[2,15,128,128]{3,2,1,0:T(8,128)(2,1)S(1)}, bf16[2,15,128,128]{3,2,1,0:T(8,128)(2,1)S(1)}, u32[]{:S(2)}, u32[]{:S(2)}) collective-permute-start(bf16[2,15,128,128]{3,2,1,0:T(8,128)(2,1)S(1)} %collective-permute-done.4.refs_3_), channel_id=1, source_target_pairs={{0,1},{1,0},{2,3},{3,2},{4,5},{5,4},{6,7},{7,6},{8,9},{9,8},{10,11... | collective-permute-start | bytes 2949128 | tf_op jit(solution)/shard_map/ppermute | solution.py:89
  136.9 4.5 %copy-start.6 = (bf16[2,15,128,128]{3,2,1,0:T(8,128)(2,1)}, bf16[2,15,128,128]{3,2,1,0:T(8,128)(2,1)S(1)}, u32[]{:S(2)}) copy-start(bf16[2,15,128,128]{3,2,1,0:T(8,128)(2,1)S(1)} %collective-permute-done.2.refs_2_) | copy-start | bytes 2949124
  136.9 4.4 %collective-permute-start.7 = (bf16[2,15,128,128]{3,2,1,0:T(8,128)(2,1)S(1)}, bf16[2,15,128,128]{3,2,1,0:T(8,128)(2,1)S(1)}, u32[]{:S(2)}, u32[]{:S(2)}) collective-permute-start(bf16[2,15,128,128]{3,2,1,0:T(8,128)(2,1)S(1)} %collective-permute-done.2.refs_2_), channel_id=1, source_target_pairs={{0,1},{1,0},{2,3},{3,2},{4,5},{5,4},{6,7},{7,6},{8,9},{9,8},{10,11... | collective-permute-start | bytes 2949128 | tf_op jit(solution)/shard_map/ppermute | solution.py:89
  138.9 2.5 %copy-start.3 = (bf16[4,15,128,128]{3,2,1,0:T(8,128)(2,1)}, bf16[4,15,128,128]{3,2,1,0:T(8,128)(2,1)S(1)}, u32[]{:S(2)}) copy-start(bf16[4,15,128,128]{3,2,1,0:T(8,128)(2,1)S(1)} %collective-permute-done.5.refs_5_) | copy-start | bytes 5898244
  138.9 2.5 %copy-start.7 = (bf16[2,15,128,128]{3,2,1,0:T(8,128)(2,1)}, bf16[2,15,128,128]{3,2,1,0:T(8,128)(2,1)S(1)}, u32[]{:S(2)}) copy-start(bf16[2,15,128,128]{3,2,1,0:T(8,128)(2,1)S(1)} %collective-permute-done.8.refs_8_) | copy-start | bytes 2949124
  138.9 2.5 %copy-start.4 = (bf16[4,15,128,128]{3,2,1,0:T(8,128)(2,1)}, bf16[4,15,128,128]{3,2,1,0:T(8,128)(2,1)S(1)}, u32[]{:S(2)}) copy-start(bf16[4,15,128,128]{3,2,1,0:T(8,128)(2,1)S(1)} %collective-permute-done.9.refs_9_) | copy-start | bytes 5898244
  141.4 1.1 copy-start.8
Sparse Core Ops, SparseCore 0:
  10.1 91.4 all-gather.3

commit v3 on v2

--- a/solution.py
+++ b/solution.py
@@ -14,8 +14,7 @@
 OWN = 2
 RHS = 512
 RZ = RHS // NZ
-KEEP = 14
-CHUNK = KEEP + 1
+CHUNK = 15
 EARLY = 11
 RHS_AT = 10
 INV0 = NZ_DEV * TILE
@@ -40,29 +39,36 @@
 
 def home(slot, y, z):
     if slot == 0:
-        return y, z + KEEP - 2 * y
-    if y == 3 and z >= 8:
-        return 0, z
-    if y == 2 and z >= 10:
-        return 1, z
-    return y, z
-
-
-def place_of(z):
+        if y == 1:
+            return 2, 8 + z
+        return 3 - y, 4 + z
     if z < 4:
-        return z
-    return z + 7 if z < 8 else z - 4
-
-
-def balance_pairs():
-    pairs = []
-    for y, x, z, k in every():
-        for slot in range(OWN):
-            if z < 8 * slot + 2 * y:
-                to = home(slot, y, z)
-                if to != (y, z):
-                    pairs.append((dev(y, x, z, k), dev(to[0], x, to[1], k)))
-    return pairs
+        return y, z
+    if z < 8:
+        return y, 7 + z
+    if y == 1:
+        return y, z
+    return y, z - 4
+
+
+def stride_groups():
+    return [
+        [dev(y, x, m + 4 * q, k) for y in pair for q in range(4)]
+        for x in range(NX)
+        for k in range(NC)
+        for pair in ((0, 3), (1, 2))
+        for m in range(4)
+    ]
+
+
+def near_groups():
+    return [
+        [dev(y, x, 4 * q + m, k) for m in range(4)]
+        for y in range(NY)
+        for x in range(NX)
+        for k in range(NC)
+        for q in range(4)
+    ]
 
 
 def first_groups():
@@ -89,6 +95,10 @@
     return lax.ppermute(value, AXES, pairs)
 
 
+def exchange(value, groups):
+    return lax.all_to_all(value, AXES, 0, 0, tiled=True, axis_index_groups=groups)
+
+
 def nt(a, b):
     return lax.dot_general(a, b, (((1,), (1,)), ((), ())), preferred_element_type=F32)
 
@@ -98,7 +108,7 @@
     return row >> 2, row & 3, col >> 1, col & 1
 
 
-def prep_kernel(pattern, off, inv, rhs, blob, send, keep, btile, flat):
+def prep_kernel(pattern, off, inv, rhs, blob, send, btile, flat):
     y, _, z, _ = coordinates()
     blob[:INV0] = off[...]
     for j in range(TPS):
@@ -110,8 +120,10 @@
             block = off[k * TILE : (k + 1) * TILE].astype(F32)
             tile = jnp.where(pattern[z >> 1, k] == slot, block, tile)
         tiles.append(tile)
-    keep[...] = tiles[1].astype(BF)
-    send[...] = jnp.where(z < 2 * y, tiles[0], tiles[1]).astype(BF)
+    for half in range(2):
+        tile = jnp.where((y >> 1) == half, tiles[1], tiles[0]).astype(BF)
+        for q in range(4):
+            send[half * 4 + q] = tile
     start = pl.multiple_of(z * RZ, RZ)
     for slot in range(OWN):
         flat[...] = rhs[slot].T
@@ -126,9 +138,13 @@
     vm = pl.BlockSpec(memory_space=pltpu.VMEM)
     return pl.pallas_call(
         prep_kernel,
-        out_shape=(jax.ShapeDtypeStruct((BLOB, TILE), BF), tile, tile, tile),
+        out_shape=(
+            jax.ShapeDtypeStruct((BLOB, TILE), BF),
+            jax.ShapeDtypeStruct((8, TILE, TILE), BF),
+            tile,
+        ),
         in_specs=[pl.BlockSpec(memory_space=pltpu.SMEM), vm, vm, vm],
-        out_specs=(vm, vm, vm, vm),
+        out_specs=(vm, vm, vm),
         scratch_shapes=[pltpu.VMEM((RHS, TILE), F32)],
         compiler_params=pltpu.CompilerParams(vmem_limit_bytes=VMEM),
     )(pattern, off, inv, rhs)
@@ -215,8 +231,8 @@
             slot, y, x = t // 16, t % 16 // NX, t % NX
             parts = []
             for j in range(TPS):
-                at_y, plane = home(slot, y, 2 * s + j // 2)
-                parts.append(block(j % 2, at_y, x, place_of(plane)))
+                at_y, place = home(slot, y, 2 * s + j // 2)
+                parts.append(block(j % 2, at_y, x, place))
             upd[t] += nt(x_s, jnp.concatenate(parts, axis=1))
     for s in range(SUPER):
         ext_loads[s].wait()
@@ -231,16 +247,15 @@
         part = ext[OWN + z // 2][:, (z % 2) * 32 : (z % 2) * 32 + 32]
         high = part.astype(BF)
         low = (part - high.astype(F32)).astype(BF)
-        out[z, RZ:] = jnp.concatenate(
-            [high, low, jnp.zeros((RZ, TILE - 64), BF)], axis=1
-        )
+        both = jnp.concatenate([high, low], axis=1)
+        out[z, RZ:] = jnp.concatenate([both[: RZ // 2], both[RZ // 2 :]], axis=1)
 
 
 def solve(pattern, pieces, blobs):
     hbm = pl.BlockSpec(memory_space=pl.ANY)
     return pl.pallas_call(
         solve_kernel,
-        out_shape=jax.ShapeDtypeStruct((NZ, 2 * RZ, TILE), BF),
+        out_shape=jax.ShapeDtypeStruct((NZ, RZ + RZ // 2, TILE), BF),
         in_specs=[pl.BlockSpec(memory_space=pltpu.SMEM)] + [hbm] * 11,
         out_specs=pl.BlockSpec(memory_space=pltpu.VMEM),
         scratch_shapes=[
@@ -262,8 +277,12 @@
 def finish_kernel(got, rhs_ext, solution, remainder):
     x = jnp.concatenate([got[z, :RZ].astype(F32) for z in range(NZ)], axis=0)
     solution[...] = x.T.astype(BF)
-    tail = jnp.concatenate([got[z, RZ:].astype(F32) for z in range(NZ)], axis=0).T
-    remainder[...] = rhs_ext[...] - (tail[:32] + tail[32:64])
+    parts = []
+    for z in range(NZ):
+        both = got[z, RZ:].astype(F32)
+        parts.append(both[:, :32] + both[:, 32:64])
+        parts.append(both[:, 64:96] + both[:, 96:])
+    remainder[...] = rhs_ext[...] - jnp.concatenate(parts, axis=0).T
 
 
 def finish(got, rhs_ext):
@@ -278,17 +297,27 @@
 
 
 def local(rhs_own, inverse, offdiag, pattern, rhs_ext):
-    y, _, z, _ = coordinates()
+    y, _, _, _ = coordinates()
     groups = [[NC * i + k for i in range(NZ)] for k in range(NC)]
-    blob, send, keep, btile = prep(pattern, offdiag, inverse, rhs_own)
+    blob, send, btile = prep(pattern, offdiag, inverse, rhs_own)
     blobs = lax.all_gather(blob, "col")
-    got = move(send, balance_pairs())
-    gets = (z < KEEP) & (z >= jnp.where((y == 0) | (y == 3), 8, 10))
-    one = jnp.where(gets, got, keep)
-    line = lax.all_gather(one, "col", axis_index_groups=groups)
-    chunk = jnp.concatenate([line[:4], line[8:KEEP], btile[None], line[4:8]], axis=0)
+    got = exchange(send, stride_groups())
+    low = y < 2
+    last = jnp.where(low, jnp.where(y == 0, got[5], got[2]), jnp.where(y == 2, got[0], got[7]))
+    quad = jnp.stack(
+        [
+            jnp.where(low, got[0], got[4]),
+            jnp.where(low, got[1], got[5]),
+            jnp.where(low, got[4], got[6]),
+            last,
+        ]
+    )
+    line = exchange(jnp.broadcast_to(quad[None], (4, 4, TILE, TILE)), near_groups())
+    chunk = jnp.concatenate(
+        [line[:, 0], line[:, 2], line[:2, 3], btile[None], line[:, 1]], axis=0
+    )
     four = jnp.broadcast_to(chunk[None], (4, CHUNK, TILE, TILE))
-    first = lax.all_to_all(four, AXES, 0, 0, tiled=True, axis_index_groups=first_groups())
+    first = exchange(four, first_groups())
     right = move(first, ring_pairs(-1))
     left = move(first, ring_pairs(1))
     far_a = move(right[:2], ring_pairs(-1))

time: 193 us -> 194 us (level)
  blocking collectives: 88.3 us -> 68.6 us
  waiting for transfers between devices: 31.3 us -> 46.5 us
  starting transfers between devices: 37.5 us -> 42.3 us
    all_gather x1 -> x0, blocking collectives: 37.6 us -> none  [local(): line = lax.all_gather(one, 'col', axis_index_groups=groups)]
    all_to_all x1 -> x2, blocking collectives: 23.8 us -> 48.4 us  [exchange(): lax.all_to_all(value, AXES, 0, 0, tiled=True, axis_index_groups=groups)]
    all_to_all x0 -> x1, starting transfers between devices: none -> 17.8 us  [exchange(): lax.all_to_all(value, AXES, 0, 0, tiled=True, axis_index_groups=groups)]
    all_to_all x0 -> x1, waiting for transfers between devices: none -> 16.8 us  [exchange(): lax.all_to_all(value, AXES, 0, 0, tiled=True, axis_index_groups=groups)]
    ppermute x10 -> x9, starting transfers between devices: 37.5 us -> 24.5 us  [move(): return lax.ppermute(value, AXES, pairs)]
    all_to_all x1, blocking collectives: 26.8 us -> 20.2 us  [local(): lax.all_to_all(packed, 'col', 0, 0, tiled=True, axis_index_groups=groups)]
    ppermute x10 -> x9, waiting for transfers between devices: 31.3 us -> 29.7 us  [move(): return lax.ppermute(value, AXES, pairs)]
  transfers between devices with their start and end apart: 11 -> 11, of which waited for: 5 -> 5; matrix products, arithmetic and copies ran while one was open for 1% -> 0% of each run, Pallas kernels for 0% -> 0%
where the time goes in v3:
time: 194 us; the launch traced here: 193 us
  blocking collectives  68.6 us (35%)
  waiting for transfers between devices  46.5 us (24%)
  starting transfers between devices  42.3 us (22%)
  Pallas kernels  18.8 us (10%)
  between operations  14.3 us (7%)
    all_to_all x2, blocking collectives, exchange(): lax.all_to_all(value, AXES, 0, 0, tiled=True, axis_index_groups=groups)  48.4 us
    ppermute x9, waiting for transfers between devices, move(): return lax.ppermute(value, AXES, pairs)  29.7 us
    ppermute x9, starting transfers between devices, move(): return lax.ppermute(value, AXES, pairs)  24.5 us
    all_to_all x1, blocking collectives, local(): lax.all_to_all(packed, 'col', 0, 0, tiled=True, axis_index_groups=groups)  20.2 us
    all_to_all x1, starting transfers between devices, exchange(): lax.all_to_all(value, AXES, 0, 0, tiled=True, axis_index_groups=groups)  17.8 us
    all_to_all x1, waiting for transfers between devices, exchange(): lax.all_to_all(value, AXES, 0, 0, tiled=True, axis_index_groups=groups)  16.8 us
    pallas_call x1, Pallas kernels, solve(): pl.pallas_call(solve_kernel, out_shape=jax.ShapeDtypeStruct((NZ, RZ + RZ...  14.7 us
  transfers between devices with their start and end apart: 11, of which 5 were waited for; matrix products, arithmetic and copies ran while one was open for 0% of the time, Pallas kernels for 0%

profile of v3, /device:TPU:24, one launch (start us, length us, event | category | flops | bytes accessed | tf_op | source)
XLA Modules:
  0.0 192.5 jit_solution(7861994907689208274)
XLA Ops:
  7.2 2.2 %shard_map.68 = (bf16[1280,128]{1,0:T(8,128)(2,1)}, bf16[8,128,128]{2,1,0:T(8,128)(2,1)}, bf16[128,128]{1,0:T(8,128)(2,1)}) custom-call(s32[8,6]{1,0:T(8,128)} %pattern.3, bf16[768,128]{1,0:T(8,128)(2,1)} %off.1, bf16[128,512]{1,0:T(8,128)(2,1)} %inv.1, f32[2,128,512]{2,1,0:T(8,128)} %rhs.1), custom_call_target="tpu_custom_call" | custom-call | tf_op jit(solution)/shard_map/pallas_call | solution.py:139
  9.4 17.8 %all-to-all-start = ((bf16[8,128,128]{2,1,0:T(8,128)(2,1)}), bf16[8,128,128]{2,1,0:T(8,128)(2,1)S(1)}, u32[]{:S(2)}, u32[]{:S(2)}) async-start(bf16[8,128,128]{2,1,0:T(8,128)(2,1)} %get-tuple-element.5), calls=%async_computation | async-start | bytes 524288 | tf_op jit(solution)/shard_map/all_to_all | solution.py:99
  27.2 16.8 %all-to-all-done = bf16[8,128,128]{2,1,0:T(8,128)(2,1)S(1)} async-done(((bf16[8,128,128]{2,1,0:T(8,128)(2,1)}), bf16[8,128,128]{2,1,0:T(8,128)(2,1)S(1)}, u32[]{:S(2)}, u32[]{:S(2)}) %all-to-all-start) | async-done | bytes 262176 | tf_op jit(solution)/shard_map/all_to_all | solution.py:99
  44.1 0.1 broadcast_in_dim.6
  44.2 28.5 %all_to_all.20 = bf16[4,4,128,128]{3,2,1,0:T(8,128)(2,1)S(1)} all-to-all(bf16[4,4,128,128]{3,2,1,0:T(8,128)(2,1)S(1)} %broadcast_in_dim.6), channel_id=1, replica_groups={{0,2,4,6},{8,10,12,14},{16,18,20,22},{24,26,28,30},{1,3,5,7},{9,11,13,1..., dimensions={0} | all-to-all | bytes 1048576 | tf_op jit(solution)/shard_map/all_to_all | solution.py:99
  72.7 0.5 broadcast_in_dim.8
  73.2 20.0 %all_to_all.21.refs_0_ = bf16[4,15,128,128]{3,2,1,0:T(8,128)(2,1)S(1)} all-to-all(bf16[4,15,128,128]{3,2,1,0:T(8,128)(2,1)S(1)} %broadcast_in_dim.8), channel_id=1, replica_groups={{0,32,64,96},{128,160,192,224},{256,288,320,352},{384,416,448,480},{1,1..., dimensions={0} | all-to-all | bytes 3932160 | tf_op jit(solution)/shard_map/all_to_all | solution.py:99
  93.2 5.0 %collective-permute-start.2 = (bf16[4,15,128,128]{3,2,1,0:T(8,128)(2,1)S(1)}, bf16[4,15,128,128]{3,2,1,0:T(8,128)(2,1)S(1)}, u32[]{:S(2)}, u32[]{:S(2)}) collective-permute-start(bf16[4,15,128,128]{3,2,1,0:T(8,128)(2,1)S(1)} %all_to_all.21.refs_0_), channel_id=1, source_target_pairs={{0,128},{1,33},{2,130},{3,35},{4,132},{5,37},{6,134},{7,39},{8,136... | collective-permute-start | bytes 5898248 | tf_op jit(solution)/shard_map/ppermute | solution.py:95
  98.2 1.9 collective-permute-start
  100.1 1.9 collective-permute-start.4
  102.0 18.3 %collective-permute-done.2.refs_4_ = bf16[4,15,128,128]{3,2,1,0:T(8,128)(2,1)S(1)} collective-permute-done((bf16[4,15,128,128]{3,2,1,0:T(8,128)(2,1)S(1)}, bf16[4,15,128,128]{3,2,1,0:T(8,128)(2,1)S(1)}, u32[]{:S(2)}, u32[]{:S(2)}) %collective-permute-start.2) | collective-permute-done | bytes 1966112 | tf_op jit(solution)/shard_map/ppermute | solution.py:95
  120.4 5.6 %collective-permute-start.3 = (bf16[2,15,128,128]{3,2,1,0:T(8,128)(2,1)S(1)}, bf16[2,15,128,128]{3,2,1,0:T(8,128)(2,1)S(1)}, u32[]{:S(2)}, u32[]{:S(2)}) collective-permute-start(bf16[2,15,128,128]{3,2,1,0:T(8,128)(2,1)S(1)} %slice.67), channel_id=1, source_target_pairs={{0,128},{1,33},{2,130},{3,35},{4,132},{5,37},{6,134},{7,39},{8,136... | collective-permute-start | bytes 2949128 | tf_op jit(solution)/shard_map/ppermute | solution.py:95
  126.1 1.9 collective-permute-start.1
  128.1 1.9 collective-permute-start.8
  130.0 2.4 %collective-permute-start.5 = (bf16[4,15,128,128]{3,2,1,0:T(8,128)(2,1)S(1)}, bf16[4,15,128,128]{3,2,1,0:T(8,128)(2,1)}, u32[]{:S(2)}, u32[]{:S(2)}) collective-permute-start(bf16[4,15,128,128]{3,2,1,0:T(8,128)(2,1)S(1)} %collective-permute-done.refs_1_), channel_id=1, source_target_pairs={{0,1},{1,0},{2,3},{3,2},{4,5},{5,4},{6,7},{7,6},{8,9},{9,8},{10,11... | collective-permute-start | bytes 5898248 | tf_op jit(solution)/shard_map/ppermute | solution.py:95
  132.4 5.2 %collective-permute-done.3.refs_3_ = bf16[2,15,128,128]{3,2,1,0:T(8,128)(2,1)S(1)} collective-permute-done((bf16[2,15,128,128]{3,2,1,0:T(8,128)(2,1)S(1)}, bf16[2,15,128,128]{3,2,1,0:T(8,128)(2,1)S(1)}, u32[]{:S(2)}, u32[]{:S(2)}) %collective-permute-start.3) | collective-permute-done | bytes 983072 | tf_op jit(solution)/shard_map/ppermute | solution.py:95
  137.6 1.9 collective-permute-start.7
  139.5 3.8 %collective-permute-done.1.refs_2_ = bf16[2,15,128,128]{3,2,1,0:T(8,128)(2,1)S(1)} collective-permute-done((bf16[2,15,128,128]{3,2,1,0:T(8,128)(2,1)S(1)}, bf16[2,15,128,128]{3,2,1,0:T(8,128)(2,1)S(1)}, u32[]{:S(2)}, u32[]{:S(2)}) %collective-permute-start.1) | collective-permute-done | bytes 983072 | tf_op jit(solution)/shard_map/ppermute | solution.py:95
  143.3 1.9 collective-permute-start.6
  145.3 2.5 %collective-permute-done.6.refs_7_ = bf16[2,15,128,128]{3,2,1,0:T(8,128)(2,1)S(1)} collective-permute-done((bf16[2,15,128,128]{3,2,1,0:T(8,128)(2,1)S(1)}, bf16[2,15,128,128]{3,2,1,0:T(8,128)(2,1)S(1)}, u32[]{:S(2)}, u32[]{:S(2)}) %collective-permute-start.6) | collective-permute-done | bytes 983072 | tf_op jit(solution)/shard_map/ppermute | solution.py:95
  147.8 1.1 copy-done.8
  148.9 14.7 %shard_map.69 = bf16[16,48,128]{2,1,0:T(8,128)(2,1)} custom-call(s32[8,6]{1,0:T(8,128)} %pattern.3, bf16[4,15,128,128]{3,2,1,0:T(8,128)(2,1)} %copy-done, bf16[4,15,128,128]{3,2,1,0:T(8,128)(2,1)} %copy-done.2, bf16[2,15,128,128]{3,2,1,0:T(8,128)(2,1)} %copy-done.6, bf16[2,15,128,128]{3,2,1,0:T(8,128)(2,1)} %copy-done.5, ...), custom_call_target="tpu_custom_call" | custom-call | tf_op jit(solution)/shard_map/pallas_call | solution.py:256
  163.6 20.2 %all_to_all.22.got = bf16[16,48,128]{2,1,0:T(8,128)(2,1)} all-to-all(bf16[16,48,128]{2,1,0:T(8,128)(2,1)} %shard_map.69), channel_id=1, replica_groups={{0,2,4,6,8,10,12,14,16,18,20,22,24,26,28,30},{1,3,5,7,9,11,13,15,17,19,..., dimensions={0} | all-to-all | bytes 393216 | tf_op jit(solution)/shard_map/all_to_all | solution.py:328
  183.8 1.8 shard_map.70
  (36 shorter events, 0.4 us)
Async XLA Ops:
  7.2 141.7 %all-gather.3.cloned.1.call-start = ((), (), s32[]{:S(2)}) async-start(), calls=%async_computation.4 | async-start | bytes 10813440 | tf_op jit(solution)/shard_map/all_gather | solution.py:303
  9.4 63.2 %copy-start.9 = (bf16[128,128]{1,0:T(8,128)(2,1)S(1)}, bf16[128,128]{1,0:T(8,128)(2,1)}, u32[]{:S(2)}) copy-start(bf16[128,128]{1,0:T(8,128)(2,1)} %get-tuple-element.6) | copy-start | bytes 98308
  9.4 34.6 %all-to-all-start = ((bf16[8,128,128]{2,1,0:T(8,128)(2,1)}), bf16[8,128,128]{2,1,0:T(8,128)(2,1)S(1)}, u32[]{:S(2)}, u32[]{:S(2)}) async-start(bf16[8,128,128]{2,1,0:T(8,128)(2,1)} %get-tuple-element.5), calls=%async_computation | async-start | bytes 524288 | tf_op jit(solution)/shard_map/all_to_all | solution.py:99
  93.1 55.7 %copy-start = (bf16[4,15,128,128]{3,2,1,0:T(8,128)(2,1)}, bf16[4,15,128,128]{3,2,1,0:T(8,128)(2,1)S(1)}, u32[]{:S(2)}) copy-start(bf16[4,15,128,128]{3,2,1,0:T(8,128)(2,1)S(1)} %all_to_all.21.refs_0_) | copy-start | bytes 5898244
  93.2 27.2 %collective-permute-start.2 = (bf16[4,15,128,128]{3,2,1,0:T(8,128)(2,1)S(1)}, bf16[4,15,128,128]{3,2,1,0:T(8,128)(2,1)S(1)}, u32[]{:S(2)}, u32[]{:S(2)}) collective-permute-start(bf16[4,15,128,128]{3,2,1,0:T(8,128)(2,1)S(1)} %all_to_all.21.refs_0_), channel_id=1, source_target_pairs={{0,128},{1,33},{2,130},{3,35},{4,132},{5,37},{6,134},{7,39},{8,136... | collective-permute-start | bytes 5898248 | tf_op jit(solution)/shard_map/ppermute | solution.py:95
  98.2 27.8 %collective-permute-start = (bf16[4,15,128,128]{3,2,1,0:T(8,128)(2,1)S(1)}, bf16[4,15,128,128]{3,2,1,0:T(8,128)(2,1)S(1)}, u32[]{:S(2)}, u32[]{:S(2)}) collective-permute-start(bf16[4,15,128,128]{3,2,1,0:T(8,128)(2,1)S(1)} %all_to_all.21.refs_0_), channel_id=1, source_target_pairs={{0,384},{1,97},{2,386},{3,99},{4,388},{5,101},{6,390},{7,103},{8,3... | collective-permute-start | bytes 5898248 | tf_op jit(solution)/shard_map/ppermute | solution.py:95
  100.1 45.1 %collective-permute-start.4 = (bf16[4,15,128,128]{3,2,1,0:T(8,128)(2,1)S(1)}, bf16[4,15,128,128]{3,2,1,0:T(8,128)(2,1)S(1)}, u32[]{:S(2)}, u32[]{:S(2)}) collective-permute-start(bf16[4,15,128,128]{3,2,1,0:T(8,128)(2,1)S(1)} %all_to_all.21.refs_0_), channel_id=1, source_target_pairs={{0,1},{1,0},{2,3},{3,2},{4,5},{5,4},{6,7},{7,6},{8,9},{9,8},{10,11... | collective-permute-start | bytes 5898248 | tf_op jit(solution)/shard_map/ppermute | solution.py:95
  120.3 25.0 %copy-start.1 = (bf16[4,15,128,128]{3,2,1,0:T(8,128)(2,1)}, bf16[4,15,128,128]{3,2,1,0:T(8,128)(2,1)S(1)}, u32[]{:S(2)}) copy-start(bf16[4,15,128,128]{3,2,1,0:T(8,128)(2,1)S(1)} %collective-permute-done.2.refs_4_) | copy-start | bytes 5898244
  120.4 17.2 %collective-permute-start.3 = (bf16[2,15,128,128]{3,2,1,0:T(8,128)(2,1)S(1)}, bf16[2,15,128,128]{3,2,1,0:T(8,128)(2,1)S(1)}, u32[]{:S(2)}, u32[]{:S(2)}) collective-permute-start(bf16[2,15,128,128]{3,2,1,0:T(8,128)(2,1)S(1)} %slice.67), channel_id=1, source_target_pairs={{0,128},{1,33},{2,130},{3,35},{4,132},{5,37},{6,134},{7,39},{8,136... | collective-permute-start | bytes 2949128 | tf_op jit(solution)/shard_map/ppermute | solution.py:95
  126.0 19.3 %copy-start.2 = (bf16[4,15,128,128]{3,2,1,0:T(8,128)(2,1)}, bf16[4,15,128,128]{3,2,1,0:T(8,128)(2,1)S(1)}, u32[]{:S(2)}) copy-start(bf16[4,15,128,128]{3,2,1,0:T(8,128)(2,1)S(1)} %collective-permute-done.refs_1_) | copy-start | bytes 5898244
  126.1 17.2 %collective-permute-start.1 = (bf16[2,15,128,128]{3,2,1,0:T(8,128)(2,1)S(1)}, bf16[2,15,128,128]{3,2,1,0:T(8,128)(2,1)S(1)}, u32[]{:S(2)}, u32[]{:S(2)}) collective-permute-start(bf16[2,15,128,128]{3,2,1,0:T(8,128)(2,1)S(1)} %slice.66), channel_id=1, source_target_pairs={{0,384},{1,97},{2,386},{3,99},{4,388},{5,101},{6,390},{7,103},{8,3... | collective-permute-start | bytes 2949128 | tf_op jit(solution)/shard_map/ppermute | solution.py:95
  128.1 17.2 %collective-permute-start.8 = (bf16[4,15,128,128]{3,2,1,0:T(8,128)(2,1)S(1)}, bf16[4,15,128,128]{3,2,1,0:T(8,128)(2,1)S(1)}, u32[]{:S(2)}, u32[]{:S(2)}) collective-permute-start(bf16[4,15,128,128]{3,2,1,0:T(8,128)(2,1)S(1)} %collective-permute-done.2.refs_4_), channel_id=1, source_target_pairs={{0,1},{1,0},{2,3},{3,2},{4,5},{5,4},{6,7},{7,6},{8,9},{9,8},{10,11... | collective-permute-start | bytes 5898248 | tf_op jit(solution)/shard_map/ppermute | solution.py:95
  130.0 18.9 %collective-permute-start.5 = (bf16[4,15,128,128]{3,2,1,0:T(8,128)(2,1)S(1)}, bf16[4,15,128,128]{3,2,1,0:T(8,128)(2,1)}, u32[]{:S(2)}, u32[]{:S(2)}) collective-permute-start(bf16[4,15,128,128]{3,2,1,0:T(8,128)(2,1)S(1)} %collective-permute-done.refs_1_), channel_id=1, source_target_pairs={{0,1},{1,0},{2,3},{3,2},{4,5},{5,4},{6,7},{7,6},{8,9},{9,8},{10,11... | collective-permute-start | bytes 5898248 | tf_op jit(solution)/shard_map/ppermute | solution.py:95
  137.6 11.3 %copy-start.5 = (bf16[2,15,128,128]{3,2,1,0:T(8,128)(2,1)}, bf16[2,15,128,128]{3,2,1,0:T(8,128)(2,1)S(1)}, u32[]{:S(2)}) copy-start(bf16[2,15,128,128]{3,2,1,0:T(8,128)(2,1)S(1)} %collective-permute-done.3.refs_3_) | copy-start | bytes 2949124
  137.6 7.7 %collective-permute-start.7 = (bf16[2,15,128,128]{3,2,1,0:T(8,128)(2,1)S(1)}, bf16[2,15,128,128]{3,2,1,0:T(8,128)(2,1)S(1)}, u32[]{:S(2)}, u32[]{:S(2)}) collective-permute-start(bf16[2,15,128,128]{3,2,1,0:T(8,128)(2,1)S(1)} %collective-permute-done.3.refs_3_), channel_id=1, source_target_pairs={{0,1},{1,0},{2,3},{3,2},{4,5},{5,4},{6,7},{7,6},{8,9},{9,8},{10,11... | collective-permute-start | bytes 2949128 | tf_op jit(solution)/shard_map/ppermute | solution.py:95
  143.3 4.5 %copy-start.6 = (bf16[2,15,128,128]{3,2,1,0:T(8,128)(2,1)}, bf16[2,15,128,128]{3,2,1,0:T(8,128)(2,1)S(1)}, u32[]{:S(2)}) copy-start(bf16[2,15,128,128]{3,2,1,0:T(8,128)(2,1)S(1)} %collective-permute-done.1.refs_2_) | copy-start | bytes 2949124
  143.3 4.4 %collective-permute-start.6 = (bf16[2,15,128,128]{3,2,1,0:T(8,128)(2,1)S(1)}, bf16[2,15,128,128]{3,2,1,0:T(8,128)(2,1)S(1)}, u32[]{:S(2)}, u32[]{:S(2)}) collective-permute-start(bf16[2,15,128,128]{3,2,1,0:T(8,128)(2,1)S(1)} %collective-permute-done.1.refs_2_), channel_id=1, source_target_pairs={{0,1},{1,0},{2,3},{3,2},{4,5},{5,4},{6,7},{7,6},{8,9},{9,8},{10,11... | collective-permute-start | bytes 2949128 | tf_op jit(solution)/shard_map/ppermute | solution.py:95
  145.3 2.5 %copy-start.3 = (bf16[4,15,128,128]{3,2,1,0:T(8,128)(2,1)}, bf16[4,15,128,128]{3,2,1,0:T(8,128)(2,1)S(1)}, u32[]{:S(2)}) copy-start(bf16[4,15,128,128]{3,2,1,0:T(8,128)(2,1)S(1)} %collective-permute-done.4.refs_5_) | copy-start | bytes 5898244
  145.3 2.5 %copy-start.7 = (bf16[2,15,128,128]{3,2,1,0:T(8,128)(2,1)}, bf16[2,15,128,128]{3,2,1,0:T(8,128)(2,1)S(1)}, u32[]{:S(2)}) copy-start(bf16[2,15,128,128]{3,2,1,0:T(8,128)(2,1)S(1)} %collective-permute-done.7.refs_8_) | copy-start | bytes 2949124
  145.3 2.5 %copy-start.4 = (bf16[4,15,128,128]{3,2,1,0:T(8,128)(2,1)}, bf16[4,15,128,128]{3,2,1,0:T(8,128)(2,1)S(1)}, u32[]{:S(2)}) copy-start(bf16[4,15,128,128]{3,2,1,0:T(8,128)(2,1)S(1)} %collective-permute-done.8.refs_9_) | copy-start | bytes 5898244
  147.8 1.1 copy-start.8
Sparse Core Ops, SparseCore 0:
  10.1 102.8 all-gather.2

commit v4 on v3

--- a/solution.py
+++ b/solution.py
@@ -300,7 +300,6 @@
     y, _, _, _ = coordinates()
     groups = [[NC * i + k for i in range(NZ)] for k in range(NC)]
     blob, send, btile = prep(pattern, offdiag, inverse, rhs_own)
-    blobs = lax.all_gather(blob, "col")
     got = exchange(send, stride_groups())
     low = y < 2
     last = jnp.where(low, jnp.where(y == 0, got[5], got[2]), jnp.where(y == 2, got[0], got[7]))
@@ -313,6 +312,8 @@
         ]
     )
     line = exchange(jnp.broadcast_to(quad[None], (4, 4, TILE, TILE)), near_groups())
+    blob, line = lax.optimization_barrier((blob, line))
+    blobs = lax.all_gather(blob, "col")
     chunk = jnp.concatenate(
         [line[:, 0], line[:, 2], line[:2, 3], btile[None], line[:, 1]], axis=0
     )

time: 194 us -> 187 us (0.964)
  blocking collectives: 68.6 us -> 60.9 us
    all_to_all x2, blocking collectives: 48.4 us -> 38.4 us  [exchange(): lax.all_to_all(value, AXES, 0, 0, tiled=True, axis_index_groups=groups)]
    all_to_all x1, blocking collectives: 20.2 us -> 22.6 us  [local(): lax.all_to_all(packed, 'col', 0, 0, tiled=True, axis_index_groups=groups)]
  transfers between devices with their start and end apart: 11 -> 11, of which waited for: 5 -> 6; matrix products, arithmetic and copies ran while one was open for 0% -> 0% of each run, Pallas kernels for 0% -> 0%
where the time goes in v4:
time: 187 us; the launch traced here: 185 us
  blocking collectives  60.9 us (33%)
  waiting for transfers between devices  46.6 us (25%)
  starting transfers between devices  42.2 us (23%)
  Pallas kernels  18.8 us (10%)
  between operations  14.3 us (8%)
  local copies, waits for them, and re-layouts  1.91 us (1%)
    all_to_all x2, blocking collectives, exchange(): lax.all_to_all(value, AXES, 0, 0, tiled=True, axis_index_groups=groups)  38.4 us
    ppermute x9, waiting for transfers between devices, move(): return lax.ppermute(value, AXES, pairs)  29.7 us
    ppermute x9, starting transfers between devices, move(): return lax.ppermute(value, AXES, pairs)  24.3 us
    all_to_all x1, blocking collectives, local(): lax.all_to_all(packed, 'col', 0, 0, tiled=True, axis_index_groups=groups)  22.6 us
    all_to_all x1, starting transfers between devices, exchange(): lax.all_to_all(value, AXES, 0, 0, tiled=True, axis_index_groups=groups)  17.9 us
    all_to_all x1, waiting for transfers between devices, exchange(): lax.all_to_all(value, AXES, 0, 0, tiled=True, axis_index_groups=groups)  16.5 us
    pallas_call x1, Pallas kernels, solve(): pl.pallas_call(solve_kernel, out_shape=jax.ShapeDtypeStruct((NZ, RZ + RZ...  14.7 us
  transfers between devices with their start and end apart: 11, of which 6 were waited for; matrix products, arithmetic and copies ran while one was open for 0% of the time, Pallas kernels for 0%

profile of v4, /device:TPU:24, one launch (start us, length us, event | category | flops | bytes accessed | tf_op | source)
XLA Modules:
  0.0 184.8 jit_solution(9827117964127733385)
XLA Ops:
  7.2 2.3 %shard_map.68 = (bf16[1280,128]{1,0:T(8,128)(2,1)}, bf16[8,128,128]{2,1,0:T(8,128)(2,1)}, bf16[128,128]{1,0:T(8,128)(2,1)}) custom-call(s32[8,6]{1,0:T(8,128)} %pattern.3, bf16[768,128]{1,0:T(8,128)(2,1)} %off.1, bf16[128,512]{1,0:T(8,128)(2,1)} %inv.1, f32[2,128,512]{2,1,0:T(8,128)} %rhs.1), custom_call_target="tpu_custom_call" | custom-call | tf_op jit(solution)/shard_map/pallas_call | solution.py:139
  9.4 17.9 %all-to-all-start = ((bf16[8,128,128]{2,1,0:T(8,128)(2,1)}), bf16[8,128,128]{2,1,0:T(8,128)(2,1)S(1)}, u32[]{:S(2)}, u32[]{:S(2)}) async-start(bf16[8,128,128]{2,1,0:T(8,128)(2,1)} %get-tuple-element.8), calls=%async_computation | async-start | bytes 524288 | tf_op jit(solution)/shard_map/all_to_all | solution.py:99
  27.3 16.5 %all-to-all-done = bf16[8,128,128]{2,1,0:T(8,128)(2,1)S(1)} async-done(((bf16[8,128,128]{2,1,0:T(8,128)(2,1)}), bf16[8,128,128]{2,1,0:T(8,128)(2,1)S(1)}, u32[]{:S(2)}, u32[]{:S(2)}) %all-to-all-start) | async-done | bytes 262176 | tf_op jit(solution)/shard_map/all_to_all | solution.py:99
  44.0 18.5 %all_to_all.20 = bf16[4,4,128,128]{3,2,1,0:T(8,128)(2,1)S(1)} all-to-all(bf16[4,4,128,128]{3,2,1,0:T(8,128)(2,1)S(1)} %broadcast_in_dim.6), channel_id=1, replica_groups={{0,2,4,6},{8,10,12,14},{16,18,20,22},{24,26,28,30},{1,3,5,7},{9,11,13,1..., dimensions={0} | all-to-all | bytes 1048576 | tf_op jit(solution)/shard_map/all_to_all | solution.py:99
  62.6 0.5 broadcast_in_dim.8
  63.1 19.9 %all_to_all.21.refs_0_ = bf16[4,15,128,128]{3,2,1,0:T(8,128)(2,1)S(1)} all-to-all(bf16[4,15,128,128]{3,2,1,0:T(8,128)(2,1)S(1)} %broadcast_in_dim.8), channel_id=1, replica_groups={{0,32,64,96},{128,160,192,224},{256,288,320,352},{384,416,448,480},{1,1..., dimensions={0} | all-to-all | bytes 3932160 | tf_op jit(solution)/shard_map/all_to_all | solution.py:99
  83.0 4.8 %collective-permute-start.2 = (bf16[4,15,128,128]{3,2,1,0:T(8,128)(2,1)S(1)}, bf16[4,15,128,128]{3,2,1,0:T(8,128)(2,1)S(1)}, u32[]{:S(2)}, u32[]{:S(2)}) collective-permute-start(bf16[4,15,128,128]{3,2,1,0:T(8,128)(2,1)S(1)} %all_to_all.21.refs_0_), channel_id=1, source_target_pairs={{0,128},{1,33},{2,130},{3,35},{4,132},{5,37},{6,134},{7,39},{8,136... | collective-permute-start | bytes 5898248 | tf_op jit(solution)/shard_map/ppermute | solution.py:95
  87.8 1.9 %collective-permute-start = (bf16[4,15,128,128]{3,2,1,0:T(8,128)(2,1)S(1)}, bf16[4,15,128,128]{3,2,1,0:T(8,128)(2,1)S(1)}, u32[]{:S(2)}, u32[]{:S(2)}) collective-permute-start(bf16[4,15,128,128]{3,2,1,0:T(8,128)(2,1)S(1)} %all_to_all.21.refs_0_), channel_id=1, source_target_pairs={{0,384},{1,97},{2,386},{3,99},{4,388},{5,101},{6,390},{7,103},{8,3... | collective-permute-start | bytes 5898248 | tf_op jit(solution)/shard_map/ppermute | solution.py:95
  89.7 1.9 %collective-permute-start.4 = (bf16[4,15,128,128]{3,2,1,0:T(8,128)(2,1)S(1)}, bf16[4,15,128,128]{3,2,1,0:T(8,128)(2,1)S(1)}, u32[]{:S(2)}, u32[]{:S(2)}) collective-permute-start(bf16[4,15,128,128]{3,2,1,0:T(8,128)(2,1)S(1)} %all_to_all.21.refs_0_), channel_id=1, source_target_pairs={{0,1},{1,0},{2,3},{3,2},{4,5},{5,4},{6,7},{7,6},{8,9},{9,8},{10,11... | collective-permute-start | bytes 5898248 | tf_op jit(solution)/shard_map/ppermute | solution.py:95
  91.6 18.3 %collective-permute-done.2.refs_4_ = bf16[4,15,128,128]{3,2,1,0:T(8,128)(2,1)S(1)} collective-permute-done((bf16[4,15,128,128]{3,2,1,0:T(8,128)(2,1)S(1)}, bf16[4,15,128,128]{3,2,1,0:T(8,128)(2,1)S(1)}, u32[]{:S(2)}, u32[]{:S(2)}) %collective-permute-start.2) | collective-permute-done | bytes 1966112 | tf_op jit(solution)/shard_map/ppermute | solution.py:95
  110.0 5.6 %collective-permute-start.3 = (bf16[2,15,128,128]{3,2,1,0:T(8,128)(2,1)S(1)}, bf16[2,15,128,128]{3,2,1,0:T(8,128)(2,1)S(1)}, u32[]{:S(2)}, u32[]{:S(2)}) collective-permute-start(bf16[2,15,128,128]{3,2,1,0:T(8,128)(2,1)S(1)} %slice.66), channel_id=1, source_target_pairs={{0,128},{1,33},{2,130},{3,35},{4,132},{5,37},{6,134},{7,39},{8,136... | collective-permute-start | bytes 2949128 | tf_op jit(solution)/shard_map/ppermute | solution.py:95
  115.7 1.9 %collective-permute-start.1 = (bf16[2,15,128,128]{3,2,1,0:T(8,128)(2,1)S(1)}, bf16[2,15,128,128]{3,2,1,0:T(8,128)(2,1)S(1)}, u32[]{:S(2)}, u32[]{:S(2)}) collective-permute-start(bf16[2,15,128,128]{3,2,1,0:T(8,128)(2,1)S(1)} %slice.65), channel_id=1, source_target_pairs={{0,384},{1,97},{2,386},{3,99},{4,388},{5,101},{6,390},{7,103},{8,3... | collective-permute-start | bytes 2949128 | tf_op jit(solution)/shard_map/ppermute | solution.py:95
  117.7 1.9 %collective-permute-start.8 = (bf16[4,15,128,128]{3,2,1,0:T(8,128)(2,1)S(1)}, bf16[4,15,128,128]{3,2,1,0:T(8,128)(2,1)S(1)}, u32[]{:S(2)}, u32[]{:S(2)}) collective-permute-start(bf16[4,15,128,128]{3,2,1,0:T(8,128)(2,1)S(1)} %collective-permute-done.2.refs_4_), channel_id=1, source_target_pairs={{0,1},{1,0},{2,3},{3,2},{4,5},{5,4},{6,7},{7,6},{8,9},{9,8},{10,11... | collective-permute-start | bytes 5898248 | tf_op jit(solution)/shard_map/ppermute | solution.py:95
  119.6 2.4 %collective-permute-start.5 = (bf16[4,15,128,128]{3,2,1,0:T(8,128)(2,1)S(1)}, bf16[4,15,128,128]{3,2,1,0:T(8,128)(2,1)}, u32[]{:S(2)}, u32[]{:S(2)}) collective-permute-start(bf16[4,15,128,128]{3,2,1,0:T(8,128)(2,1)S(1)} %collective-permute-done.refs_1_), channel_id=1, source_target_pairs={{0,1},{1,0},{2,3},{3,2},{4,5},{5,4},{6,7},{7,6},{8,9},{9,8},{10,11... | collective-permute-start | bytes 5898248 | tf_op jit(solution)/shard_map/ppermute | solution.py:95
  122.0 5.2 %collective-permute-done.3.refs_3_ = bf16[2,15,128,128]{3,2,1,0:T(8,128)(2,1)S(1)} collective-permute-done((bf16[2,15,128,128]{3,2,1,0:T(8,128)(2,1)S(1)}, bf16[2,15,128,128]{3,2,1,0:T(8,128)(2,1)S(1)}, u32[]{:S(2)}, u32[]{:S(2)}) %collective-permute-start.3) | collective-permute-done | bytes 983072 | tf_op jit(solution)/shard_map/ppermute | solution.py:95
  127.2 1.9 %collective-permute-start.7 = (bf16[2,15,128,128]{3,2,1,0:T(8,128)(2,1)S(1)}, bf16[2,15,128,128]{3,2,1,0:T(8,128)(2,1)S(1)}, u32[]{:S(2)}, u32[]{:S(2)}) collective-permute-start(bf16[2,15,128,128]{3,2,1,0:T(8,128)(2,1)S(1)} %collective-permute-done.3.refs_3_), channel_id=1, source_target_pairs={{0,1},{1,0},{2,3},{3,2},{4,5},{5,4},{6,7},{7,6},{8,9},{9,8},{10,11... | collective-permute-start | bytes 2949128 | tf_op jit(solution)/shard_map/ppermute | solution.py:95
  129.1 3.8 %collective-permute-done.1.refs_2_ = bf16[2,15,128,128]{3,2,1,0:T(8,128)(2,1)S(1)} collective-permute-done((bf16[2,15,128,128]{3,2,1,0:T(8,128)(2,1)S(1)}, bf16[2,15,128,128]{3,2,1,0:T(8,128)(2,1)S(1)}, u32[]{:S(2)}, u32[]{:S(2)}) %collective-permute-start.1) | collective-permute-done | bytes 983072 | tf_op jit(solution)/shard_map/ppermute | solution.py:95
  132.9 1.9 %collective-permute-start.6 = (bf16[2,15,128,128]{3,2,1,0:T(8,128)(2,1)S(1)}, bf16[2,15,128,128]{3,2,1,0:T(8,128)(2,1)S(1)}, u32[]{:S(2)}, u32[]{:S(2)}) collective-permute-start(bf16[2,15,128,128]{3,2,1,0:T(8,128)(2,1)S(1)} %collective-permute-done.1.refs_2_), channel_id=1, source_target_pairs={{0,1},{1,0},{2,3},{3,2},{4,5},{5,4},{6,7},{7,6},{8,9},{9,8},{10,11... | collective-permute-start | bytes 2949128 | tf_op jit(solution)/shard_map/ppermute | solution.py:95
  134.9 2.5 %collective-permute-done.6.refs_7_ = bf16[2,15,128,128]{3,2,1,0:T(8,128)(2,1)S(1)} collective-permute-done((bf16[2,15,128,128]{3,2,1,0:T(8,128)(2,1)S(1)}, bf16[2,15,128,128]{3,2,1,0:T(8,128)(2,1)S(1)}, u32[]{:S(2)}, u32[]{:S(2)}) %collective-permute-start.6) | collective-permute-done | bytes 983072 | tf_op jit(solution)/shard_map/ppermute | solution.py:95
  137.4 1.1 copy-done.8
  138.5 0.3 all-gather.3.cloned.1.call-done
  138.8 14.7 %shard_map.69 = bf16[16,48,128]{2,1,0:T(8,128)(2,1)} custom-call(s32[8,6]{1,0:T(8,128)} %pattern.3, bf16[4,15,128,128]{3,2,1,0:T(8,128)(2,1)} %copy-done, bf16[4,15,128,128]{3,2,1,0:T(8,128)(2,1)} %copy-done.2, bf16[2,15,128,128]{3,2,1,0:T(8,128)(2,1)} %copy-done.6, bf16[2,15,128,128]{3,2,1,0:T(8,128)(2,1)} %copy-done.5, ...), custom_call_target="tpu_custom_call" | custom-call | tf_op jit(solution)/shard_map/pallas_call | solution.py:256
  153.5 22.6 %all_to_all.22.got = bf16[16,48,128]{2,1,0:T(8,128)(2,1)} all-to-all(bf16[16,48,128]{2,1,0:T(8,128)(2,1)} %shard_map.69), channel_id=1, replica_groups={{0,2,4,6,8,10,12,14,16,18,20,22,24,26,28,30},{1,3,5,7,9,11,13,15,17,19,..., dimensions={0} | all-to-all | bytes 393216 | tf_op jit(solution)/shard_map/all_to_all | solution.py:329
  176.1 1.8 shard_map.70
  (36 shorter events, 0.5 us)
Async XLA Ops:
  9.4 53.1 %copy-start.9 = (bf16[128,128]{1,0:T(8,128)(2,1)S(1)}, bf16[128,128]{1,0:T(8,128)(2,1)}, u32[]{:S(2)}) copy-start(bf16[128,128]{1,0:T(8,128)(2,1)} %get-tuple-element.10) | copy-start | bytes 98308
  9.4 34.4 %all-to-all-start = ((bf16[8,128,128]{2,1,0:T(8,128)(2,1)}), bf16[8,128,128]{2,1,0:T(8,128)(2,1)S(1)}, u32[]{:S(2)}, u32[]{:S(2)}) async-start(bf16[8,128,128]{2,1,0:T(8,128)(2,1)} %get-tuple-element.8), calls=%async_computation | async-start | bytes 524288 | tf_op jit(solution)/shard_map/all_to_all | solution.py:99
  27.3 111.5 %all-gather.3.cloned.1.call-start = ((), (), s32[]{:S(2)}) async-start(), calls=%async_computation.4 | async-start | bytes 10813440 | tf_op jit(solution)/shard_map/all_gather | solution.py:316
  83.0 55.8 %copy-start = (bf16[4,15,128,128]{3,2,1,0:T(8,128)(2,1)}, bf16[4,15,128,128]{3,2,1,0:T(8,128)(2,1)S(1)}, u32[]{:S(2)}) copy-start(bf16[4,15,128,128]{3,2,1,0:T(8,128)(2,1)S(1)} %all_to_all.21.refs_0_) | copy-start | bytes 5898244
  83.0 26.9 %collective-permute-start.2 = (bf16[4,15,128,128]{3,2,1,0:T(8,128)(2,1)S(1)}, bf16[4,15,128,128]{3,2,1,0:T(8,128)(2,1)S(1)}, u32[]{:S(2)}, u32[]{:S(2)}) collective-permute-start(bf16[4,15,128,128]{3,2,1,0:T(8,128)(2,1)S(1)} %all_to_all.21.refs_0_), channel_id=1, source_target_pairs={{0,128},{1,33},{2,130},{3,35},{4,132},{5,37},{6,134},{7,39},{8,136... | collective-permute-start | bytes 5898248 | tf_op jit(solution)/shard_map/ppermute | solution.py:95
  87.8 27.8 %collective-permute-start = (bf16[4,15,128,128]{3,2,1,0:T(8,128)(2,1)S(1)}, bf16[4,15,128,128]{3,2,1,0:T(8,128)(2,1)S(1)}, u32[]{:S(2)}, u32[]{:S(2)}) collective-permute-start(bf16[4,15,128,128]{3,2,1,0:T(8,128)(2,1)S(1)} %all_to_all.21.refs_0_), channel_id=1, source_target_pairs={{0,384},{1,97},{2,386},{3,99},{4,388},{5,101},{6,390},{7,103},{8,3... | collective-permute-start | bytes 5898248 | tf_op jit(solution)/shard_map/ppermute | solution.py:95
  89.7 45.1 %collective-permute-start.4 = (bf16[4,15,128,128]{3,2,1,0:T(8,128)(2,1)S(1)}, bf16[4,15,128,128]{3,2,1,0:T(8,128)(2,1)S(1)}, u32[]{:S(2)}, u32[]{:S(2)}) collective-permute-start(bf16[4,15,128,128]{3,2,1,0:T(8,128)(2,1)S(1)} %all_to_all.21.refs_0_), channel_id=1, source_target_pairs={{0,1},{1,0},{2,3},{3,2},{4,5},{5,4},{6,7},{7,6},{8,9},{9,8},{10,11... | collective-permute-start | bytes 5898248 | tf_op jit(solution)/shard_map/ppermute | solution.py:95
  109.9 25.0 %copy-start.1 = (bf16[4,15,128,128]{3,2,1,0:T(8,128)(2,1)}, bf16[4,15,128,128]{3,2,1,0:T(8,128)(2,1)S(1)}, u32[]{:S(2)}) copy-start(bf16[4,15,128,128]{3,2,1,0:T(8,128)(2,1)S(1)} %collective-permute-done.2.refs_4_) | copy-start | bytes 5898244
  110.0 17.2 %collective-permute-start.3 = (bf16[2,15,128,128]{3,2,1,0:T(8,128)(2,1)S(1)}, bf16[2,15,128,128]{3,2,1,0:T(8,128)(2,1)S(1)}, u32[]{:S(2)}, u32[]{:S(2)}) collective-permute-start(bf16[2,15,128,128]{3,2,1,0:T(8,128)(2,1)S(1)} %slice.66), channel_id=1, source_target_pairs={{0,128},{1,33},{2,130},{3,35},{4,132},{5,37},{6,134},{7,39},{8,136... | collective-permute-start | bytes 2949128 | tf_op jit(solution)/shard_map/ppermute | solution.py:95
  115.6 19.3 %copy-start.2 = (bf16[4,15,128,128]{3,2,1,0:T(8,128)(2,1)}, bf16[4,15,128,128]{3,2,1,0:T(8,128)(2,1)S(1)}, u32[]{:S(2)}) copy-start(bf16[4,15,128,128]{3,2,1,0:T(8,128)(2,1)S(1)} %collective-permute-done.refs_1_) | copy-start | bytes 5898244
  115.7 17.2 %collective-permute-start.1 = (bf16[2,15,128,128]{3,2,1,0:T(8,128)(2,1)S(1)}, bf16[2,15,128,128]{3,2,1,0:T(8,128)(2,1)S(1)}, u32[]{:S(2)}, u32[]{:S(2)}) collective-permute-start(bf16[2,15,128,128]{3,2,1,0:T(8,128)(2,1)S(1)} %slice.65), channel_id=1, source_target_pairs={{0,384},{1,97},{2,386},{3,99},{4,388},{5,101},{6,390},{7,103},{8,3... | collective-permute-start | bytes 2949128 | tf_op jit(solution)/shard_map/ppermute | solution.py:95
  117.7 17.2 %collective-permute-start.8 = (bf16[4,15,128,128]{3,2,1,0:T(8,128)(2,1)S(1)}, bf16[4,15,128,128]{3,2,1,0:T(8,128)(2,1)S(1)}, u32[]{:S(2)}, u32[]{:S(2)}) collective-permute-start(bf16[4,15,128,128]{3,2,1,0:T(8,128)(2,1)S(1)} %collective-permute-done.2.refs_4_), channel_id=1, source_target_pairs={{0,1},{1,0},{2,3},{3,2},{4,5},{5,4},{6,7},{7,6},{8,9},{9,8},{10,11... | collective-permute-start | bytes 5898248 | tf_op jit(solution)/shard_map/ppermute | solution.py:95
  119.6 18.9 %collective-permute-start.5 = (bf16[4,15,128,128]{3,2,1,0:T(8,128)(2,1)S(1)}, bf16[4,15,128,128]{3,2,1,0:T(8,128)(2,1)}, u32[]{:S(2)}, u32[]{:S(2)}) collective-permute-start(bf16[4,15,128,128]{3,2,1,0:T(8,128)(2,1)S(1)} %collective-permute-done.refs_1_), channel_id=1, source_target_pairs={{0,1},{1,0},{2,3},{3,2},{4,5},{5,4},{6,7},{7,6},{8,9},{9,8},{10,11... | collective-permute-start | bytes 5898248 | tf_op jit(solution)/shard_map/ppermute | solution.py:95
  127.2 11.6 %copy-start.5 = (bf16[2,15,128,128]{3,2,1,0:T(8,128)(2,1)}, bf16[2,15,128,128]{3,2,1,0:T(8,128)(2,1)S(1)}, u32[]{:S(2)}) copy-start(bf16[2,15,128,128]{3,2,1,0:T(8,128)(2,1)S(1)} %collective-permute-done.3.refs_3_) | copy-start | bytes 2949124
  127.2 7.7 %collective-permute-start.7 = (bf16[2,15,128,128]{3,2,1,0:T(8,128)(2,1)S(1)}, bf16[2,15,128,128]{3,2,1,0:T(8,128)(2,1)S(1)}, u32[]{:S(2)}, u32[]{:S(2)}) collective-permute-start(bf16[2,15,128,128]{3,2,1,0:T(8,128)(2,1)S(1)} %collective-permute-done.3.refs_3_), channel_id=1, source_target_pairs={{0,1},{1,0},{2,3},{3,2},{4,5},{5,4},{6,7},{7,6},{8,9},{9,8},{10,11... | collective-permute-start | bytes 2949128 | tf_op jit(solution)/shard_map/ppermute | solution.py:95
  132.9 4.5 %copy-start.6 = (bf16[2,15,128,128]{3,2,1,0:T(8,128)(2,1)}, bf16[2,15,128,128]{3,2,1,0:T(8,128)(2,1)S(1)}, u32[]{:S(2)}) copy-start(bf16[2,15,128,128]{3,2,1,0:T(8,128)(2,1)S(1)} %collective-permute-done.1.refs_2_) | copy-start | bytes 2949124
  132.9 4.4 %collective-permute-start.6 = (bf16[2,15,128,128]{3,2,1,0:T(8,128)(2,1)S(1)}, bf16[2,15,128,128]{3,2,1,0:T(8,128)(2,1)S(1)}, u32[]{:S(2)}, u32[]{:S(2)}) collective-permute-start(bf16[2,15,128,128]{3,2,1,0:T(8,128)(2,1)S(1)} %collective-permute-done.1.refs_2_), channel_id=1, source_target_pairs={{0,1},{1,0},{2,3},{3,2},{4,5},{5,4},{6,7},{7,6},{8,9},{9,8},{10,11... | collective-permute-start | bytes 2949128 | tf_op jit(solution)/shard_map/ppermute | solution.py:95
  134.9 2.5 %copy-start.3 = (bf16[4,15,128,128]{3,2,1,0:T(8,128)(2,1)}, bf16[4,15,128,128]{3,2,1,0:T(8,128)(2,1)S(1)}, u32[]{:S(2)}) copy-start(bf16[4,15,128,128]{3,2,1,0:T(8,128)(2,1)S(1)} %collective-permute-done.4.refs_5_) | copy-start | bytes 5898244
  134.9 2.5 %copy-start.7 = (bf16[2,15,128,128]{3,2,1,0:T(8,128)(2,1)}, bf16[2,15,128,128]{3,2,1,0:T(8,128)(2,1)S(1)}, u32[]{:S(2)}) copy-start(bf16[2,15,128,128]{3,2,1,0:T(8,128)(2,1)S(1)} %collective-permute-done.7.refs_8_) | copy-start | bytes 2949124
  134.9 2.5 %copy-start.4 = (bf16[4,15,128,128]{3,2,1,0:T(8,128)(2,1)}, bf16[4,15,128,128]{3,2,1,0:T(8,128)(2,1)S(1)}, u32[]{:S(2)}) copy-start(bf16[4,15,128,128]{3,2,1,0:T(8,128)(2,1)S(1)} %collective-permute-done.8.refs_9_) | copy-start | bytes 5898244
  137.4 1.1 copy-start.8
Sparse Core Ops, SparseCore 0:
  62.6 76.1 all-gather.2

commit v5 on v4

--- a/solution.py
+++ b/solution.py
@@ -15,8 +15,8 @@
 RHS = 512
 RZ = RHS // NZ
 CHUNK = 15
-EARLY = 11
-RHS_AT = 10
+RHS_AT = 6
+WAVES = ((0, 7), (7, 4), (11, 4))
 INV0 = NZ_DEV * TILE
 BLOB = INV0 + TPS * TILE
 BLOCKS = NZ_DEV + TPS
@@ -38,17 +38,16 @@
 
 
 def home(slot, y, z):
+    first, second, third, fourth = (0, 1, 7, 8), (11, 12, 13, 14), (2, 3, 9, 10), (4, 5)
     if slot == 0:
         if y == 1:
-            return 2, 8 + z
-        return 3 - y, 4 + z
-    if z < 4:
-        return y, z
+            return 2, fourth[z]
+        return 3 - y, (third + fourth)[z]
     if z < 8:
-        return y, 7 + z
+        return y, (first + second)[z]
     if y == 1:
-        return y, z
-    return y, z - 4
+        return y, fourth[z - 8]
+    return y, (third + fourth)[z - 8]
 
 
 def stride_groups():
@@ -108,11 +107,8 @@
     return row >> 2, row & 3, col >> 1, col & 1
 
 
-def prep_kernel(pattern, off, inv, rhs, blob, send, btile, flat):
+def pick_kernel(pattern, off, send):
     y, _, z, _ = coordinates()
-    blob[:INV0] = off[...]
-    for j in range(TPS):
-        blob[INV0 + j * TILE : INV0 + (j + 1) * TILE] = inv[:, j * TILE : (j + 1) * TILE]
     tiles = []
     for slot in range(OWN):
         tile = jnp.zeros((TILE, TILE), F32)
@@ -124,6 +120,24 @@
         tile = jnp.where((y >> 1) == half, tiles[1], tiles[0]).astype(BF)
         for q in range(4):
             send[half * 4 + q] = tile
+
+
+def pick(pattern, off):
+    vm = pl.BlockSpec(memory_space=pltpu.VMEM)
+    return pl.pallas_call(
+        pick_kernel,
+        out_shape=jax.ShapeDtypeStruct((8, TILE, TILE), BF),
+        in_specs=[pl.BlockSpec(memory_space=pltpu.SMEM), vm],
+        out_specs=vm,
+        compiler_params=pltpu.CompilerParams(vmem_limit_bytes=VMEM),
+    )(pattern, off)
+
+
+def prep_kernel(off, inv, rhs, blob, btile, flat):
+    _, _, z, _ = coordinates()
+    blob[:INV0] = off[...]
+    for j in range(TPS):
+        blob[INV0 + j * TILE : INV0 + (j + 1) * TILE] = inv[:, j * TILE : (j + 1) * TILE]
     start = pl.multiple_of(z * RZ, RZ)
     for slot in range(OWN):
         flat[...] = rhs[slot].T
@@ -133,21 +147,20 @@
         btile[slot * 2 * RZ + RZ : (slot + 1) * 2 * RZ] = (part - high.astype(F32)).astype(BF)
 
 
-def prep(pattern, off, inv, rhs):
-    tile = jax.ShapeDtypeStruct((TILE, TILE), BF)
+def prep(off, inv, rhs):
     vm = pl.BlockSpec(memory_space=pltpu.VMEM)
     return pl.pallas_call(
         prep_kernel,
         out_shape=(
             jax.ShapeDtypeStruct((BLOB, TILE), BF),
-            jax.ShapeDtypeStruct((8, TILE, TILE), BF),
-            tile,
+            jax.ShapeDtypeStruct((TILE, TILE), BF),
         ),
-        in_specs=[pl.BlockSpec(memory_space=pltpu.SMEM), vm, vm, vm],
-        out_specs=(vm, vm, vm),
+        in_specs=[vm, vm, vm],
+        out_specs=(vm, vm),
         scratch_shapes=[pltpu.VMEM((RHS, TILE), F32)],
         compiler_params=pltpu.CompilerParams(vmem_limit_bytes=VMEM),
-    )(pattern, off, inv, rhs)
+        cost_estimate=pl.CostEstimate(flops=1 << 20, bytes_accessed=4 << 20, transcendentals=0),
+    )(off, inv, rhs)
 
 
 PIECES = ((0, 4), (4, 4), (8, 2), (10, 2), (12, 4))
@@ -155,7 +168,7 @@
 
 def solve_kernel(pattern, *refs):
     pieces = refs[:10]
-    blobs, out, factor, invs, rows_ext, upd, ext, sol, early, late, isems, esems = refs[10:]
+    blobs, out, factor, invs, rows_ext, upd, ext, sol, *wsems, isems, esems = refs[10:]
     my_y, my_x, _, core = coordinates()
 
     def load(first, count, sems):
@@ -169,8 +182,7 @@
             for p, (at, blocks) in enumerate(PIECES)
         ]
 
-    first_loads = load(0, EARLY, early)
-    last_loads = load(EARLY, CHUNK - EARLY, late)
+    waves = [load(first, count, sems) for (first, count), sems in zip(WAVES, wsems)]
     inv_loads, ext_loads = [], []
     for s in range(SUPER):
         four = pl.ds(s * TPS, TPS)
@@ -184,15 +196,13 @@
                 blobs.at[four, pl.ds(0, NZ_DEV), :, core], rows_ext.at[four], esems.at[s]
             )
         )
-    for c in first_loads[:5] + inv_loads[:1] + first_loads[5:] + inv_loads[1:2] + last_loads:
-        c.start()
-    for c in inv_loads[2:] + ext_loads:
+    for wave, inv_load in zip(waves, inv_loads):
+        for c in wave + [inv_load]:
+            c.start()
+    for c in inv_loads[len(WAVES) :] + ext_loads:
         c.start()
     upd[...] = jnp.zeros_like(upd)
     ext[...] = jnp.zeros_like(ext)
-    for c in first_loads:
-        c.wait()
-
     def position(parity, y, x):
         if parity == 0:
             return ((y - my_y) & 3) * 4 + x
@@ -210,10 +220,10 @@
         return high + low
 
     for s in range(SUPER):
+        if s < len(WAVES):
+            for c in waves[s]:
+                c.wait()
         inv_loads[s].wait()
-        if s == 2:
-            for c in last_loads:
-                c.wait()
         current = jnp.concatenate(
             [(rhs_tile(t) - upd[t]).astype(BF) for t in range(s * TPS, (s + 1) * TPS)], axis=1
         )
@@ -227,13 +237,18 @@
             sol[c] = x_i
             solved.append(x_i)
         x_s = jnp.concatenate(solved, axis=1)
-        for t in range((s + 1) * TPS, SUPER * TPS):
-            slot, y, x = t // 16, t % 16 // NX, t % NX
-            parts = []
-            for j in range(TPS):
-                at_y, place = home(slot, y, 2 * s + j // 2)
-                parts.append(block(j % 2, at_y, x, place))
-            upd[t] += nt(x_s, jnp.concatenate(parts, axis=1))
+        for t in range((s + 1) * TPS, SUPER * TPS, 2):
+            rows = []
+            for n in range(2):
+                slot, y, x = (t + n) // 16, (t + n) % 16 // NX, (t + n) % NX
+                parts = []
+                for j in range(TPS):
+                    at_y, place = home(slot, y, 2 * s + j // 2)
+                    parts.append(block(j % 2, at_y, x, place))
+                rows.append(jnp.concatenate(parts, axis=1))
+            more = nt(x_s, jnp.concatenate(rows, axis=0))
+            for n in range(2):
+                upd[t + n] += more[:, n * TILE : (n + 1) * TILE]
     for s in range(SUPER):
         ext_loads[s].wait()
         x_s = jnp.concatenate([sol[s * TPS + j] for j in range(TPS)], axis=1)
@@ -267,6 +282,7 @@
             pltpu.VMEM((SUPER * TPS, RZ, TILE), BF),
             pltpu.SemaphoreType.DMA((10,)),
             pltpu.SemaphoreType.DMA((10,)),
+            pltpu.SemaphoreType.DMA((10,)),
             pltpu.SemaphoreType.DMA((SUPER,)),
             pltpu.SemaphoreType.DMA((SUPER,)),
         ],
@@ -299,8 +315,8 @@
 def local(rhs_own, inverse, offdiag, pattern, rhs_ext):
     y, _, _, _ = coordinates()
     groups = [[NC * i + k for i in range(NZ)] for k in range(NC)]
-    blob, send, btile = prep(pattern, offdiag, inverse, rhs_own)
-    got = exchange(send, stride_groups())
+    got = exchange(pick(pattern, offdiag), stride_groups())
+    blob, btile = prep(offdiag, inverse, rhs_own)
     low = y < 2
     last = jnp.where(low, jnp.where(y == 0, got[5], got[2]), jnp.where(y == 2, got[0], got[7]))
     quad = jnp.stack(
@@ -311,11 +327,20 @@
             last,
         ]
     )
-    line = exchange(jnp.broadcast_to(quad[None], (4, 4, TILE, TILE)), near_groups())
+    line = lax.all_gather(quad, AXES, axis_index_groups=near_groups())
     blob, line = lax.optimization_barrier((blob, line))
     blobs = lax.all_gather(blob, "col")
     chunk = jnp.concatenate(
-        [line[:, 0], line[:, 2], line[:2, 3], btile[None], line[:, 1]], axis=0
+        [
+            line[:2, 0],
+            line[:2, 2],
+            line[:2, 3],
+            btile[None],
+            line[2:, 0],
+            line[2:, 2],
+            line[:, 1],
+        ],
+        axis=0,
     )
     four = jnp.broadcast_to(chunk[None], (4, CHUNK, TILE, TILE))
     first = exchange(four, first_groups())

time: 187 us -> 185 us (0.989)
  waiting for transfers between devices: 46.6 us -> 44.2 us
    all_gather x0 -> x1, blocking collectives: none -> 18.5 us  [local(): line = lax.all_gather(quad, AXES, axis_index_groups=near_groups())]
    all_to_all x2 -> x1, blocking collectives: 38.4 us -> 20.9 us  [exchange(): lax.all_to_all(value, AXES, 0, 0, tiled=True, axis_index_groups=groups)]
    all_to_all x1, blocking collectives: 22.6 us -> 20.3 us  [local(): lax.all_to_all(packed, 'col', 0, 0, tiled=True, axis_index_groups=groups)]
    all_to_all x1, waiting for transfers between devices: 16.5 us -> 14.4 us  [exchange(): lax.all_to_all(value, AXES, 0, 0, tiled=True, axis_index_groups=groups)]
  transfers between devices with their start and end apart: 11 -> 11, of which waited for: 6 -> 5; matrix products, arithmetic and copies ran while one was open for 0% -> 0% of each run, Pallas kernels for 0% -> 1%
where the time goes in v5:
time: 185 us; the launch traced here: 183 us
  blocking collectives  59.7 us (32%)
  waiting for transfers between devices  44.2 us (24%)
  starting transfers between devices  43.2 us (23%)
  Pallas kernels  19.6 us (11%)
  between operations  14.3 us (8%)
    ppermute x9, waiting for transfers between devices, move(): return lax.ppermute(value, AXES, pairs)  29.7 us
    ppermute x9, starting transfers between devices, move(): return lax.ppermute(value, AXES, pairs)  25.4 us
    all_to_all x1, blocking collectives, exchange(): lax.all_to_all(value, AXES, 0, 0, tiled=True, axis_index_groups=groups)  20.9 us
    all_to_all x1, blocking collectives, local(): lax.all_to_all(packed, 'col', 0, 0, tiled=True, axis_index_groups=groups)  20.3 us
    all_gather x1, blocking collectives, local(): line = lax.all_gather(quad, AXES, axis_index_groups=near_groups())  18.5 us
    all_to_all x1, starting transfers between devices, exchange(): lax.all_to_all(value, AXES, 0, 0, tiled=True, axis_index_groups=groups)  17.8 us
    all_to_all x1, waiting for transfers between devices, exchange(): lax.all_to_all(value, AXES, 0, 0, tiled=True, axis_index_groups=groups)  14.4 us
    pallas_call x1, Pallas kernels, solve(): pl.pallas_call(solve_kernel, out_shape=jax.ShapeDtypeStruct((NZ, RZ + RZ...  14 us
  transfers between devices with their start and end apart: 11, of which 5 were waited for; matrix products, arithmetic and copies ran while one was open for 0% of the time, Pallas kernels for 1%

profile of v5, /device:TPU:24, one launch (start us, length us, event | category | flops | bytes accessed | tf_op | source)
XLA Modules:
  0.0 182.9 jit_solution(12675291739672208605)
XLA Ops:
  7.2 1.7 shard_map.69
  8.9 17.8 %all-to-all-start = ((bf16[8,128,128]{2,1,0:T(8,128)(2,1)}), bf16[8,128,128]{2,1,0:T(8,128)(2,1)S(1)}, u32[]{:S(2)}, u32[]{:S(2)}) async-start(bf16[8,128,128]{2,1,0:T(8,128)(2,1)} %shard_map.69), calls=%async_computation | async-start | bytes 524288 | tf_op jit(solution)/shard_map/all_to_all | solution.py:98
  26.6 2.1 %shard_map.68 = (bf16[1280,128]{1,0:T(8,128)(2,1)}, bf16[128,128]{1,0:T(8,128)(2,1)}) custom-call(bf16[768,128]{1,0:T(8,128)(2,1)} %off.3, bf16[128,512]{1,0:T(8,128)(2,1)} %inv.1, f32[2,128,512]{2,1,0:T(8,128)} %rhs.1), custom_call_target="tpu_custom_call" | custom-call | flops 1048576 | bytes 4194304 | tf_op jit(solution)/shard_map/pallas_call | solution.py:152
  28.7 14.4 %all-to-all-done = bf16[8,128,128]{2,1,0:T(8,128)(2,1)S(1)} async-done(((bf16[8,128,128]{2,1,0:T(8,128)(2,1)}), bf16[8,128,128]{2,1,0:T(8,128)(2,1)S(1)}, u32[]{:S(2)}, u32[]{:S(2)}) %all-to-all-start) | async-done | bytes 262176 | tf_op jit(solution)/shard_map/all_to_all | solution.py:98
  43.2 18.5 %all-gather = bf16[16,128,128]{2,1,0:T(8,128)(2,1)S(1)} all-gather(bf16[4,128,128]{2,1,0:T(8,128)(2,1)S(1)} %pad_maximum_fusion), channel_id=2, replica_groups={{0,2,4,6},{8,10,12,14},{16,18,20,22},{24,26,28,30},{1,3,5,7},{9,11,13,1..., dimensions={0}, use_global_device_ids=true | all-gather | bytes 655360 | tf_op jit(solution)/shard_map/all_gather | solution.py:330
  61.9 0.5 broadcast_in_dim.10
  62.3 20.9 %all_to_all.15.refs_0_ = bf16[4,15,128,128]{3,2,1,0:T(8,128)(2,1)S(1)} all-to-all(bf16[4,15,128,128]{3,2,1,0:T(8,128)(2,1)S(1)} %broadcast_in_dim.10), channel_id=1, replica_groups={{0,32,64,96},{128,160,192,224},{256,288,320,352},{384,416,448,480},{1,1..., dimensions={0} | all-to-all | bytes 3932160 | tf_op jit(solution)/shard_map/all_to_all | solution.py:98
  83.3 5.9 %collective-permute-start.2 = (bf16[4,15,128,128]{3,2,1,0:T(8,128)(2,1)S(1)}, bf16[4,15,128,128]{3,2,1,0:T(8,128)(2,1)S(1)}, u32[]{:S(2)}, u32[]{:S(2)}) collective-permute-start(bf16[4,15,128,128]{3,2,1,0:T(8,128)(2,1)S(1)} %all_to_all.15.refs_0_), channel_id=1, source_target_pairs={{0,128},{1,33},{2,130},{3,35},{4,132},{5,37},{6,134},{7,39},{8,136... | collective-permute-start | bytes 5898248 | tf_op jit(solution)/shard_map/ppermute | solution.py:94
  89.2 1.9 %collective-permute-start = (bf16[4,15,128,128]{3,2,1,0:T(8,128)(2,1)S(1)}, bf16[4,15,128,128]{3,2,1,0:T(8,128)(2,1)S(1)}, u32[]{:S(2)}, u32[]{:S(2)}) collective-permute-start(bf16[4,15,128,128]{3,2,1,0:T(8,128)(2,1)S(1)} %all_to_all.15.refs_0_), channel_id=1, source_target_pairs={{0,384},{1,97},{2,386},{3,99},{4,388},{5,101},{6,390},{7,103},{8,3... | collective-permute-start | bytes 5898248 | tf_op jit(solution)/shard_map/ppermute | solution.py:94
  91.1 1.9 %collective-permute-start.4 = (bf16[4,15,128,128]{3,2,1,0:T(8,128)(2,1)S(1)}, bf16[4,15,128,128]{3,2,1,0:T(8,128)(2,1)S(1)}, u32[]{:S(2)}, u32[]{:S(2)}) collective-permute-start(bf16[4,15,128,128]{3,2,1,0:T(8,128)(2,1)S(1)} %all_to_all.15.refs_0_), channel_id=1, source_target_pairs={{0,1},{1,0},{2,3},{3,2},{4,5},{5,4},{6,7},{7,6},{8,9},{9,8},{10,11... | collective-permute-start | bytes 5898248 | tf_op jit(solution)/shard_map/ppermute | solution.py:94
  93.0 18.3 %collective-permute-done.2.refs_4_ = bf16[4,15,128,128]{3,2,1,0:T(8,128)(2,1)S(1)} collective-permute-done((bf16[4,15,128,128]{3,2,1,0:T(8,128)(2,1)S(1)}, bf16[4,15,128,128]{3,2,1,0:T(8,128)(2,1)S(1)}, u32[]{:S(2)}, u32[]{:S(2)}) %collective-permute-start.2) | collective-permute-done | bytes 1966112 | tf_op jit(solution)/shard_map/ppermute | solution.py:94
  111.4 5.6 %collective-permute-start.3 = (bf16[2,15,128,128]{3,2,1,0:T(8,128)(2,1)S(1)}, bf16[2,15,128,128]{3,2,1,0:T(8,128)(2,1)S(1)}, u32[]{:S(2)}, u32[]{:S(2)}) collective-permute-start(bf16[2,15,128,128]{3,2,1,0:T(8,128)(2,1)S(1)} %slice.77), channel_id=1, source_target_pairs={{0,128},{1,33},{2,130},{3,35},{4,132},{5,37},{6,134},{7,39},{8,136... | collective-permute-start | bytes 2949128 | tf_op jit(solution)/shard_map/ppermute | solution.py:94
  117.1 1.9 %collective-permute-start.1 = (bf16[2,15,128,128]{3,2,1,0:T(8,128)(2,1)S(1)}, bf16[2,15,128,128]{3,2,1,0:T(8,128)(2,1)S(1)}, u32[]{:S(2)}, u32[]{:S(2)}) collective-permute-start(bf16[2,15,128,128]{3,2,1,0:T(8,128)(2,1)S(1)} %slice.76), channel_id=1, source_target_pairs={{0,384},{1,97},{2,386},{3,99},{4,388},{5,101},{6,390},{7,103},{8,3... | collective-permute-start | bytes 2949128 | tf_op jit(solution)/shard_map/ppermute | solution.py:94
  119.1 1.9 %collective-permute-start.8 = (bf16[4,15,128,128]{3,2,1,0:T(8,128)(2,1)S(1)}, bf16[4,15,128,128]{3,2,1,0:T(8,128)(2,1)S(1)}, u32[]{:S(2)}, u32[]{:S(2)}) collective-permute-start(bf16[4,15,128,128]{3,2,1,0:T(8,128)(2,1)S(1)} %collective-permute-done.2.refs_4_), channel_id=1, source_target_pairs={{0,1},{1,0},{2,3},{3,2},{4,5},{5,4},{6,7},{7,6},{8,9},{9,8},{10,11... | collective-permute-start | bytes 5898248 | tf_op jit(solution)/shard_map/ppermute | solution.py:94
  121.0 2.4 %collective-permute-start.5 = (bf16[4,15,128,128]{3,2,1,0:T(8,128)(2,1)S(1)}, bf16[4,15,128,128]{3,2,1,0:T(8,128)(2,1)}, u32[]{:S(2)}, u32[]{:S(2)}) collective-permute-start(bf16[4,15,128,128]{3,2,1,0:T(8,128)(2,1)S(1)} %collective-permute-done.refs_1_), channel_id=1, source_target_pairs={{0,1},{1,0},{2,3},{3,2},{4,5},{5,4},{6,7},{7,6},{8,9},{9,8},{10,11... | collective-permute-start | bytes 5898248 | tf_op jit(solution)/shard_map/ppermute | solution.py:94
  123.4 5.2 %collective-permute-done.3.refs_3_ = bf16[2,15,128,128]{3,2,1,0:T(8,128)(2,1)S(1)} collective-permute-done((bf16[2,15,128,128]{3,2,1,0:T(8,128)(2,1)S(1)}, bf16[2,15,128,128]{3,2,1,0:T(8,128)(2,1)S(1)}, u32[]{:S(2)}, u32[]{:S(2)}) %collective-permute-start.3) | collective-permute-done | bytes 983072 | tf_op jit(solution)/shard_map/ppermute | solution.py:94
  128.6 1.9 %collective-permute-start.7 = (bf16[2,15,128,128]{3,2,1,0:T(8,128)(2,1)S(1)}, bf16[2,15,128,128]{3,2,1,0:T(8,128)(2,1)S(1)}, u32[]{:S(2)}, u32[]{:S(2)}) collective-permute-start(bf16[2,15,128,128]{3,2,1,0:T(8,128)(2,1)S(1)} %collective-permute-done.3.refs_3_), channel_id=1, source_target_pairs={{0,1},{1,0},{2,3},{3,2},{4,5},{5,4},{6,7},{7,6},{8,9},{9,8},{10,11... | collective-permute-start | bytes 2949128 | tf_op jit(solution)/shard_map/ppermute | solution.py:94
  130.5 3.8 %collective-permute-done.1.refs_2_ = bf16[2,15,128,128]{3,2,1,0:T(8,128)(2,1)S(1)} collective-permute-done((bf16[2,15,128,128]{3,2,1,0:T(8,128)(2,1)S(1)}, bf16[2,15,128,128]{3,2,1,0:T(8,128)(2,1)S(1)}, u32[]{:S(2)}, u32[]{:S(2)}) %collective-permute-start.1) | collective-permute-done | bytes 983072 | tf_op jit(solution)/shard_map/ppermute | solution.py:94
  134.3 1.9 %collective-permute-start.6 = (bf16[2,15,128,128]{3,2,1,0:T(8,128)(2,1)S(1)}, bf16[2,15,128,128]{3,2,1,0:T(8,128)(2,1)S(1)}, u32[]{:S(2)}, u32[]{:S(2)}) collective-permute-start(bf16[2,15,128,128]{3,2,1,0:T(8,128)(2,1)S(1)} %collective-permute-done.1.refs_2_), channel_id=1, source_target_pairs={{0,1},{1,0},{2,3},{3,2},{4,5},{5,4},{6,7},{7,6},{8,9},{9,8},{10,11... | collective-permute-start | bytes 2949128 | tf_op jit(solution)/shard_map/ppermute | solution.py:94
  136.3 2.5 %collective-permute-done.6.refs_7_ = bf16[2,15,128,128]{3,2,1,0:T(8,128)(2,1)S(1)} collective-permute-done((bf16[2,15,128,128]{3,2,1,0:T(8,128)(2,1)S(1)}, bf16[2,15,128,128]{3,2,1,0:T(8,128)(2,1)S(1)}, u32[]{:S(2)}, u32[]{:S(2)}) %collective-permute-start.6) | collective-permute-done | bytes 983072 | tf_op jit(solution)/shard_map/ppermute | solution.py:94
  138.8 1.1 copy-done.8
  139.9 14.0 %shard_map.70 = bf16[16,48,128]{2,1,0:T(8,128)(2,1)} custom-call(s32[8,6]{1,0:T(8,128)} %pattern.3, bf16[4,15,128,128]{3,2,1,0:T(8,128)(2,1)} %copy-done, bf16[4,15,128,128]{3,2,1,0:T(8,128)(2,1)} %copy-done.2, bf16[2,15,128,128]{3,2,1,0:T(8,128)(2,1)} %copy-done.6, bf16[2,15,128,128]{3,2,1,0:T(8,128)(2,1)} %copy-done.5, ...), custom_call_target="tpu_custom_call" | custom-call | tf_op jit(solution)/shard_map/pallas_call | solution.py:271
  153.9 20.3 %all_to_all.16.got = bf16[16,48,128]{2,1,0:T(8,128)(2,1)} all-to-all(bf16[16,48,128]{2,1,0:T(8,128)(2,1)} %shard_map.70), channel_id=1, replica_groups={{0,2,4,6,8,10,12,14,16,18,20,22,24,26,28,30},{1,3,5,7,9,11,13,15,17,19,..., dimensions={0} | all-to-all | bytes 393216 | tf_op jit(solution)/shard_map/all_to_all | solution.py:354
  174.2 1.8 %shard_map.71 = (bf16[128,512]{1,0:T(8,128)(2,1)}, f32[32,512]{1,0:T(8,128)}) custom-call(bf16[16,48,128]{2,1,0:T(8,128)(2,1)} %all_to_all.16.got, f32[32,512]{1,0:T(8,128)} %rhs_ext.1), custom_call_target="tpu_custom_call" | custom-call | tf_op jit(solution)/shard_map/pallas_call | solution.py:305
  (38 shorter events, 0.4 us)
Async XLA Ops:
  8.9 34.3 %all-to-all-start = ((bf16[8,128,128]{2,1,0:T(8,128)(2,1)}), bf16[8,128,128]{2,1,0:T(8,128)(2,1)S(1)}, u32[]{:S(2)}, u32[]{:S(2)}) async-start(bf16[8,128,128]{2,1,0:T(8,128)(2,1)} %shard_map.69), calls=%async_computation | async-start | bytes 524288 | tf_op jit(solution)/shard_map/all_to_all | solution.py:98
  26.6 113.2 %all-gather.4.cloned.1.call-start = ((), (), s32[]{:S(2)}) async-start(), calls=%async_computation.3 | async-start | bytes 10813440 | tf_op jit(solution)/shard_map/all_gather | solution.py:332
  28.7 33.0 %copy-start.9 = (bf16[128,128]{1,0:T(8,128)(2,1)S(1)}, bf16[128,128]{1,0:T(8,128)(2,1)}, u32[]{:S(2)}) copy-start(bf16[128,128]{1,0:T(8,128)(2,1)} %get-tuple-element.8) | copy-start | bytes 98308
  83.3 56.6 %copy-start = (bf16[4,15,128,128]{3,2,1,0:T(8,128)(2,1)}, bf16[4,15,128,128]{3,2,1,0:T(8,128)(2,1)S(1)}, u32[]{:S(2)}) copy-start(bf16[4,15,128,128]{3,2,1,0:T(8,128)(2,1)S(1)} %all_to_all.15.refs_0_) | copy-start | bytes 5898244
  83.3 28.0 %collective-permute-start.2 = (bf16[4,15,128,128]{3,2,1,0:T(8,128)(2,1)S(1)}, bf16[4,15,128,128]{3,2,1,0:T(8,128)(2,1)S(1)}, u32[]{:S(2)}, u32[]{:S(2)}) collective-permute-start(bf16[4,15,128,128]{3,2,1,0:T(8,128)(2,1)S(1)} %all_to_all.15.refs_0_), channel_id=1, source_target_pairs={{0,128},{1,33},{2,130},{3,35},{4,132},{5,37},{6,134},{7,39},{8,136... | collective-permute-start | bytes 5898248 | tf_op jit(solution)/shard_map/ppermute | solution.py:94
  89.2 27.8 %collective-permute-start = (bf16[4,15,128,128]{3,2,1,0:T(8,128)(2,1)S(1)}, bf16[4,15,128,128]{3,2,1,0:T(8,128)(2,1)S(1)}, u32[]{:S(2)}, u32[]{:S(2)}) collective-permute-start(bf16[4,15,128,128]{3,2,1,0:T(8,128)(2,1)S(1)} %all_to_all.15.refs_0_), channel_id=1, source_target_pairs={{0,384},{1,97},{2,386},{3,99},{4,388},{5,101},{6,390},{7,103},{8,3... | collective-permute-start | bytes 5898248 | tf_op jit(solution)/shard_map/ppermute | solution.py:94
  91.1 45.1 %collective-permute-start.4 = (bf16[4,15,128,128]{3,2,1,0:T(8,128)(2,1)S(1)}, bf16[4,15,128,128]{3,2,1,0:T(8,128)(2,1)S(1)}, u32[]{:S(2)}, u32[]{:S(2)}) collective-permute-start(bf16[4,15,128,128]{3,2,1,0:T(8,128)(2,1)S(1)} %all_to_all.15.refs_0_), channel_id=1, source_target_pairs={{0,1},{1,0},{2,3},{3,2},{4,5},{5,4},{6,7},{7,6},{8,9},{9,8},{10,11... | collective-permute-start | bytes 5898248 | tf_op jit(solution)/shard_map/ppermute | solution.py:94
  111.3 25.0 %copy-start.1 = (bf16[4,15,128,128]{3,2,1,0:T(8,128)(2,1)}, bf16[4,15,128,128]{3,2,1,0:T(8,128)(2,1)S(1)}, u32[]{:S(2)}) copy-start(bf16[4,15,128,128]{3,2,1,0:T(8,128)(2,1)S(1)} %collective-permute-done.2.refs_4_) | copy-start | bytes 5898244
  111.4 17.2 %collective-permute-start.3 = (bf16[2,15,128,128]{3,2,1,0:T(8,128)(2,1)S(1)}, bf16[2,15,128,128]{3,2,1,0:T(8,128)(2,1)S(1)}, u32[]{:S(2)}, u32[]{:S(2)}) collective-permute-start(bf16[2,15,128,128]{3,2,1,0:T(8,128)(2,1)S(1)} %slice.77), channel_id=1, source_target_pairs={{0,128},{1,33},{2,130},{3,35},{4,132},{5,37},{6,134},{7,39},{8,136... | collective-permute-start | bytes 2949128 | tf_op jit(solution)/shard_map/ppermute | solution.py:94
  117.0 19.3 %copy-start.2 = (bf16[4,15,128,128]{3,2,1,0:T(8,128)(2,1)}, bf16[4,15,128,128]{3,2,1,0:T(8,128)(2,1)S(1)}, u32[]{:S(2)}) copy-start(bf16[4,15,128,128]{3,2,1,0:T(8,128)(2,1)S(1)} %collective-permute-done.refs_1_) | copy-start | bytes 5898244
  117.1 17.2 %collective-permute-start.1 = (bf16[2,15,128,128]{3,2,1,0:T(8,128)(2,1)S(1)}, bf16[2,15,128,128]{3,2,1,0:T(8,128)(2,1)S(1)}, u32[]{:S(2)}, u32[]{:S(2)}) collective-permute-start(bf16[2,15,128,128]{3,2,1,0:T(8,128)(2,1)S(1)} %slice.76), channel_id=1, source_target_pairs={{0,384},{1,97},{2,386},{3,99},{4,388},{5,101},{6,390},{7,103},{8,3... | collective-permute-start | bytes 2949128 | tf_op jit(solution)/shard_map/ppermute | solution.py:94
  119.1 17.2 %collective-permute-start.8 = (bf16[4,15,128,128]{3,2,1,0:T(8,128)(2,1)S(1)}, bf16[4,15,128,128]{3,2,1,0:T(8,128)(2,1)S(1)}, u32[]{:S(2)}, u32[]{:S(2)}) collective-permute-start(bf16[4,15,128,128]{3,2,1,0:T(8,128)(2,1)S(1)} %collective-permute-done.2.refs_4_), channel_id=1, source_target_pairs={{0,1},{1,0},{2,3},{3,2},{4,5},{5,4},{6,7},{7,6},{8,9},{9,8},{10,11... | collective-permute-start | bytes 5898248 | tf_op jit(solution)/shard_map/ppermute | solution.py:94
  121.0 18.9 %collective-permute-start.5 = (bf16[4,15,128,128]{3,2,1,0:T(8,128)(2,1)S(1)}, bf16[4,15,128,128]{3,2,1,0:T(8,128)(2,1)}, u32[]{:S(2)}, u32[]{:S(2)}) collective-permute-start(bf16[4,15,128,128]{3,2,1,0:T(8,128)(2,1)S(1)} %collective-permute-done.refs_1_), channel_id=1, source_target_pairs={{0,1},{1,0},{2,3},{3,2},{4,5},{5,4},{6,7},{7,6},{8,9},{9,8},{10,11... | collective-permute-start | bytes 5898248 | tf_op jit(solution)/shard_map/ppermute | solution.py:94
  128.6 11.3 %copy-start.5 = (bf16[2,15,128,128]{3,2,1,0:T(8,128)(2,1)}, bf16[2,15,128,128]{3,2,1,0:T(8,128)(2,1)S(1)}, u32[]{:S(2)}) copy-start(bf16[2,15,128,128]{3,2,1,0:T(8,128)(2,1)S(1)} %collective-permute-done.3.refs_3_) | copy-start | bytes 2949124
  128.6 7.7 %collective-permute-start.7 = (bf16[2,15,128,128]{3,2,1,0:T(8,128)(2,1)S(1)}, bf16[2,15,128,128]{3,2,1,0:T(8,128)(2,1)S(1)}, u32[]{:S(2)}, u32[]{:S(2)}) collective-permute-start(bf16[2,15,128,128]{3,2,1,0:T(8,128)(2,1)S(1)} %collective-permute-done.3.refs_3_), channel_id=1, source_target_pairs={{0,1},{1,0},{2,3},{3,2},{4,5},{5,4},{6,7},{7,6},{8,9},{9,8},{10,11... | collective-permute-start | bytes 2949128 | tf_op jit(solution)/shard_map/ppermute | solution.py:94
  134.3 4.5 %copy-start.6 = (bf16[2,15,128,128]{3,2,1,0:T(8,128)(2,1)}, bf16[2,15,128,128]{3,2,1,0:T(8,128)(2,1)S(1)}, u32[]{:S(2)}) copy-start(bf16[2,15,128,128]{3,2,1,0:T(8,128)(2,1)S(1)} %collective-permute-done.1.refs_2_) | copy-start | bytes 2949124
  134.3 4.4 %collective-permute-start.6 = (bf16[2,15,128,128]{3,2,1,0:T(8,128)(2,1)S(1)}, bf16[2,15,128,128]{3,2,1,0:T(8,128)(2,1)S(1)}, u32[]{:S(2)}, u32[]{:S(2)}) collective-permute-start(bf16[2,15,128,128]{3,2,1,0:T(8,128)(2,1)S(1)} %collective-permute-done.1.refs_2_), channel_id=1, source_target_pairs={{0,1},{1,0},{2,3},{3,2},{4,5},{5,4},{6,7},{7,6},{8,9},{9,8},{10,11... | collective-permute-start | bytes 2949128 | tf_op jit(solution)/shard_map/ppermute | solution.py:94
  136.3 2.5 %copy-start.3 = (bf16[4,15,128,128]{3,2,1,0:T(8,128)(2,1)}, bf16[4,15,128,128]{3,2,1,0:T(8,128)(2,1)S(1)}, u32[]{:S(2)}) copy-start(bf16[4,15,128,128]{3,2,1,0:T(8,128)(2,1)S(1)} %collective-permute-done.4.refs_5_) | copy-start | bytes 5898244
  136.3 2.5 %copy-start.7 = (bf16[2,15,128,128]{3,2,1,0:T(8,128)(2,1)}, bf16[2,15,128,128]{3,2,1,0:T(8,128)(2,1)S(1)}, u32[]{:S(2)}) copy-start(bf16[2,15,128,128]{3,2,1,0:T(8,128)(2,1)S(1)} %collective-permute-done.7.refs_8_) | copy-start | bytes 2949124
  136.3 2.5 %copy-start.4 = (bf16[4,15,128,128]{3,2,1,0:T(8,128)(2,1)}, bf16[4,15,128,128]{3,2,1,0:T(8,128)(2,1)S(1)}, u32[]{:S(2)}) copy-start(bf16[4,15,128,128]{3,2,1,0:T(8,128)(2,1)S(1)} %collective-permute-done.8.refs_9_) | copy-start | bytes 5898244
  138.8 1.1 copy-start.8
Sparse Core Ops, SparseCore 0:
  61.8 75.6 all-gather.3

commit v6 on v5

--- a/solution.py
+++ b/solution.py
@@ -183,12 +183,20 @@
         ]
 
     waves = [load(first, count, sems) for (first, count), sems in zip(WAVES, wsems)]
-    inv_loads, ext_loads = [], []
+    inv_loads, inv_lows, ext_loads = [], [], []
     for s in range(SUPER):
         four = pl.ds(s * TPS, TPS)
         inv_loads.append(
             pltpu.make_async_copy(
-                blobs.at[four, pl.ds(NZ_DEV, TPS)], invs.at[four], isems.at[s]
+                blobs.at[four, pl.ds(NZ_DEV, 2)], invs.at[four, pl.ds(0, 2)], isems.at[2 * s]
+            )
+        )
+        lower = pl.ds(s * TPS + 2, 2)
+        inv_lows.append(
+            pltpu.make_async_copy(
+                blobs.at[lower, pl.ds(NZ_DEV + 2, 2)],
+                invs.at[lower, pl.ds(2, 2)],
+                isems.at[2 * s + 1],
             )
         )
         ext_loads.append(
@@ -196,10 +204,10 @@
                 blobs.at[four, pl.ds(0, NZ_DEV), :, core], rows_ext.at[four], esems.at[s]
             )
         )
-    for wave, inv_load in zip(waves, inv_loads):
-        for c in wave + [inv_load]:
+    for wave, inv_load, inv_low in zip(waves, inv_loads, inv_lows):
+        for c in wave + [inv_load, inv_low]:
             c.start()
-    for c in inv_loads[len(WAVES) :] + ext_loads:
+    for c in inv_loads[len(WAVES) :] + inv_lows[len(WAVES) :] + ext_loads:
         c.start()
     upd[...] = jnp.zeros_like(upd)
     ext[...] = jnp.zeros_like(ext)
@@ -224,6 +232,7 @@
             for c in waves[s]:
                 c.wait()
         inv_loads[s].wait()
+        inv_lows[s].wait()
         current = jnp.concatenate(
             [(rhs_tile(t) - upd[t]).astype(BF) for t in range(s * TPS, (s + 1) * TPS)], axis=1
         )
@@ -283,7 +292,7 @@
             pltpu.SemaphoreType.DMA((10,)),
             pltpu.SemaphoreType.DMA((10,)),
             pltpu.SemaphoreType.DMA((10,)),
-            pltpu.SemaphoreType.DMA((SUPER,)),
+            pltpu.SemaphoreType.DMA((2 * SUPER,)),
             pltpu.SemaphoreType.DMA((SUPER,)),
         ],
         compiler_params=pltpu.CompilerParams(vmem_limit_bytes=VMEM),

time: 185 us -> 184 us (level)
  no operation moved by 1% of the time
where the time goes in v6:
time: 184 us; the launch traced here: 182 us
  blocking collectives  59.7 us (32%)
  waiting for transfers between devices  44.2 us (24%)
  starting transfers between devices  43.2 us (23%)
  Pallas kernels  19.2 us (10%)
  between operations  14.3 us (8%)
    ppermute x9, waiting for transfers between devices, move(): return lax.ppermute(value, AXES, pairs)  29.7 us
    ppermute x9, starting transfers between devices, move(): return lax.ppermute(value, AXES, pairs)  25.4 us
    all_to_all x1, blocking collectives, exchange(): lax.all_to_all(value, AXES, 0, 0, tiled=True, axis_index_groups=groups)  20.9 us
    all_to_all x1, blocking collectives, local(): lax.all_to_all(packed, 'col', 0, 0, tiled=True, axis_index_groups=groups)  20.3 us
    all_gather x1, blocking collectives, local(): line = lax.all_gather(quad, AXES, axis_index_groups=near_groups())  18.5 us
    all_to_all x1, starting transfers between devices, exchange(): lax.all_to_all(value, AXES, 0, 0, tiled=True, axis_index_groups=groups)  17.8 us
    all_to_all x1, waiting for transfers between devices, exchange(): lax.all_to_all(value, AXES, 0, 0, tiled=True, axis_index_groups=groups)  14.4 us
    pallas_call x1, Pallas kernels, solve(): pl.pallas_call(solve_kernel, out_shape=jax.ShapeDtypeStruct((NZ, RZ + RZ...  13.5 us
  transfers between devices with their start and end apart: 11, of which 5 were waited for; matrix products, arithmetic and copies ran while one was open for 0% of the time, Pallas kernels for 1%

profile of v6, /device:TPU:24, one launch (start us, length us, event | category | flops | bytes accessed | tf_op | source)
XLA Modules:
  0.0 182.4 jit_solution(517570467150709318)
XLA Ops:
  7.2 1.7 shard_map.69
  8.9 17.8 %all-to-all-start = ((bf16[8,128,128]{2,1,0:T(8,128)(2,1)}), bf16[8,128,128]{2,1,0:T(8,128)(2,1)S(1)}, u32[]{:S(2)}, u32[]{:S(2)}) async-start(bf16[8,128,128]{2,1,0:T(8,128)(2,1)} %shard_map.69), calls=%async_computation | async-start | bytes 524288 | tf_op jit(solution)/shard_map/all_to_all | solution.py:98
  26.6 2.1 %shard_map.68 = (bf16[1280,128]{1,0:T(8,128)(2,1)}, bf16[128,128]{1,0:T(8,128)(2,1)}) custom-call(bf16[768,128]{1,0:T(8,128)(2,1)} %off.3, bf16[128,512]{1,0:T(8,128)(2,1)} %inv.1, f32[2,128,512]{2,1,0:T(8,128)} %rhs.1), custom_call_target="tpu_custom_call" | custom-call | flops 1048576 | bytes 4194304 | tf_op jit(solution)/shard_map/pallas_call | solution.py:152
  28.7 14.4 %all-to-all-done = bf16[8,128,128]{2,1,0:T(8,128)(2,1)S(1)} async-done(((bf16[8,128,128]{2,1,0:T(8,128)(2,1)}), bf16[8,128,128]{2,1,0:T(8,128)(2,1)S(1)}, u32[]{:S(2)}, u32[]{:S(2)}) %all-to-all-start) | async-done | bytes 262176 | tf_op jit(solution)/shard_map/all_to_all | solution.py:98
  43.2 18.5 %all-gather = bf16[16,128,128]{2,1,0:T(8,128)(2,1)S(1)} all-gather(bf16[4,128,128]{2,1,0:T(8,128)(2,1)S(1)} %pad_maximum_fusion), channel_id=2, replica_groups={{0,2,4,6},{8,10,12,14},{16,18,20,22},{24,26,28,30},{1,3,5,7},{9,11,13,1..., dimensions={0}, use_global_device_ids=true | all-gather | bytes 655360 | tf_op jit(solution)/shard_map/all_gather | solution.py:339
  61.9 0.5 broadcast_in_dim.10
  62.3 20.9 %all_to_all.15.refs_0_ = bf16[4,15,128,128]{3,2,1,0:T(8,128)(2,1)S(1)} all-to-all(bf16[4,15,128,128]{3,2,1,0:T(8,128)(2,1)S(1)} %broadcast_in_dim.10), channel_id=1, replica_groups={{0,32,64,96},{128,160,192,224},{256,288,320,352},{384,416,448,480},{1,1..., dimensions={0} | all-to-all | bytes 3932160 | tf_op jit(solution)/shard_map/all_to_all | solution.py:98
  83.3 5.9 %collective-permute-start.2 = (bf16[4,15,128,128]{3,2,1,0:T(8,128)(2,1)S(1)}, bf16[4,15,128,128]{3,2,1,0:T(8,128)(2,1)S(1)}, u32[]{:S(2)}, u32[]{:S(2)}) collective-permute-start(bf16[4,15,128,128]{3,2,1,0:T(8,128)(2,1)S(1)} %all_to_all.15.refs_0_), channel_id=1, source_target_pairs={{0,128},{1,33},{2,130},{3,35},{4,132},{5,37},{6,134},{7,39},{8,136... | collective-permute-start | bytes 5898248 | tf_op jit(solution)/shard_map/ppermute | solution.py:94
  89.2 1.9 %collective-permute-start = (bf16[4,15,128,128]{3,2,1,0:T(8,128)(2,1)S(1)}, bf16[4,15,128,128]{3,2,1,0:T(8,128)(2,1)S(1)}, u32[]{:S(2)}, u32[]{:S(2)}) collective-permute-start(bf16[4,15,128,128]{3,2,1,0:T(8,128)(2,1)S(1)} %all_to_all.15.refs_0_), channel_id=1, source_target_pairs={{0,384},{1,97},{2,386},{3,99},{4,388},{5,101},{6,390},{7,103},{8,3... | collective-permute-start | bytes 5898248 | tf_op jit(solution)/shard_map/ppermute | solution.py:94
  91.1 1.9 %collective-permute-start.4 = (bf16[4,15,128,128]{3,2,1,0:T(8,128)(2,1)S(1)}, bf16[4,15,128,128]{3,2,1,0:T(8,128)(2,1)S(1)}, u32[]{:S(2)}, u32[]{:S(2)}) collective-permute-start(bf16[4,15,128,128]{3,2,1,0:T(8,128)(2,1)S(1)} %all_to_all.15.refs_0_), channel_id=1, source_target_pairs={{0,1},{1,0},{2,3},{3,2},{4,5},{5,4},{6,7},{7,6},{8,9},{9,8},{10,11... | collective-permute-start | bytes 5898248 | tf_op jit(solution)/shard_map/ppermute | solution.py:94
  93.0 18.3 %collective-permute-done.2.refs_4_ = bf16[4,15,128,128]{3,2,1,0:T(8,128)(2,1)S(1)} collective-permute-done((bf16[4,15,128,128]{3,2,1,0:T(8,128)(2,1)S(1)}, bf16[4,15,128,128]{3,2,1,0:T(8,128)(2,1)S(1)}, u32[]{:S(2)}, u32[]{:S(2)}) %collective-permute-start.2) | collective-permute-done | bytes 1966112 | tf_op jit(solution)/shard_map/ppermute | solution.py:94
  111.4 5.6 %collective-permute-start.3 = (bf16[2,15,128,128]{3,2,1,0:T(8,128)(2,1)S(1)}, bf16[2,15,128,128]{3,2,1,0:T(8,128)(2,1)S(1)}, u32[]{:S(2)}, u32[]{:S(2)}) collective-permute-start(bf16[2,15,128,128]{3,2,1,0:T(8,128)(2,1)S(1)} %slice.77), channel_id=1, source_target_pairs={{0,128},{1,33},{2,130},{3,35},{4,132},{5,37},{6,134},{7,39},{8,136... | collective-permute-start | bytes 2949128 | tf_op jit(solution)/shard_map/ppermute | solution.py:94
  117.1 1.9 %collective-permute-start.1 = (bf16[2,15,128,128]{3,2,1,0:T(8,128)(2,1)S(1)}, bf16[2,15,128,128]{3,2,1,0:T(8,128)(2,1)S(1)}, u32[]{:S(2)}, u32[]{:S(2)}) collective-permute-start(bf16[2,15,128,128]{3,2,1,0:T(8,128)(2,1)S(1)} %slice.76), channel_id=1, source_target_pairs={{0,384},{1,97},{2,386},{3,99},{4,388},{5,101},{6,390},{7,103},{8,3... | collective-permute-start | bytes 2949128 | tf_op jit(solution)/shard_map/ppermute | solution.py:94
  119.1 1.9 %collective-permute-start.8 = (bf16[4,15,128,128]{3,2,1,0:T(8,128)(2,1)S(1)}, bf16[4,15,128,128]{3,2,1,0:T(8,128)(2,1)S(1)}, u32[]{:S(2)}, u32[]{:S(2)}) collective-permute-start(bf16[4,15,128,128]{3,2,1,0:T(8,128)(2,1)S(1)} %collective-permute-done.2.refs_4_), channel_id=1, source_target_pairs={{0,1},{1,0},{2,3},{3,2},{4,5},{5,4},{6,7},{7,6},{8,9},{9,8},{10,11... | collective-permute-start | bytes 5898248 | tf_op jit(solution)/shard_map/ppermute | solution.py:94
  121.0 2.4 %collective-permute-start.5 = (bf16[4,15,128,128]{3,2,1,0:T(8,128)(2,1)S(1)}, bf16[4,15,128,128]{3,2,1,0:T(8,128)(2,1)}, u32[]{:S(2)}, u32[]{:S(2)}) collective-permute-start(bf16[4,15,128,128]{3,2,1,0:T(8,128)(2,1)S(1)} %collective-permute-done.refs_1_), channel_id=1, source_target_pairs={{0,1},{1,0},{2,3},{3,2},{4,5},{5,4},{6,7},{7,6},{8,9},{9,8},{10,11... | collective-permute-start | bytes 5898248 | tf_op jit(solution)/shard_map/ppermute | solution.py:94
  123.4 5.2 %collective-permute-done.3.refs_3_ = bf16[2,15,128,128]{3,2,1,0:T(8,128)(2,1)S(1)} collective-permute-done((bf16[2,15,128,128]{3,2,1,0:T(8,128)(2,1)S(1)}, bf16[2,15,128,128]{3,2,1,0:T(8,128)(2,1)S(1)}, u32[]{:S(2)}, u32[]{:S(2)}) %collective-permute-start.3) | collective-permute-done | bytes 983072 | tf_op jit(solution)/shard_map/ppermute | solution.py:94
  128.6 1.9 %collective-permute-start.7 = (bf16[2,15,128,128]{3,2,1,0:T(8,128)(2,1)S(1)}, bf16[2,15,128,128]{3,2,1,0:T(8,128)(2,1)S(1)}, u32[]{:S(2)}, u32[]{:S(2)}) collective-permute-start(bf16[2,15,128,128]{3,2,1,0:T(8,128)(2,1)S(1)} %collective-permute-done.3.refs_3_), channel_id=1, source_target_pairs={{0,1},{1,0},{2,3},{3,2},{4,5},{5,4},{6,7},{7,6},{8,9},{9,8},{10,11... | collective-permute-start | bytes 2949128 | tf_op jit(solution)/shard_map/ppermute | solution.py:94
  130.5 3.8 %collective-permute-done.1.refs_2_ = bf16[2,15,128,128]{3,2,1,0:T(8,128)(2,1)S(1)} collective-permute-done((bf16[2,15,128,128]{3,2,1,0:T(8,128)(2,1)S(1)}, bf16[2,15,128,128]{3,2,1,0:T(8,128)(2,1)S(1)}, u32[]{:S(2)}, u32[]{:S(2)}) %collective-permute-start.1) | collective-permute-done | bytes 983072 | tf_op jit(solution)/shard_map/ppermute | solution.py:94
  134.3 1.9 %collective-permute-start.6 = (bf16[2,15,128,128]{3,2,1,0:T(8,128)(2,1)S(1)}, bf16[2,15,128,128]{3,2,1,0:T(8,128)(2,1)S(1)}, u32[]{:S(2)}, u32[]{:S(2)}) collective-permute-start(bf16[2,15,128,128]{3,2,1,0:T(8,128)(2,1)S(1)} %collective-permute-done.1.refs_2_), channel_id=1, source_target_pairs={{0,1},{1,0},{2,3},{3,2},{4,5},{5,4},{6,7},{7,6},{8,9},{9,8},{10,11... | collective-permute-start | bytes 2949128 | tf_op jit(solution)/shard_map/ppermute | solution.py:94
  136.3 2.5 %collective-permute-done.6.refs_7_ = bf16[2,15,128,128]{3,2,1,0:T(8,128)(2,1)S(1)} collective-permute-done((bf16[2,15,128,128]{3,2,1,0:T(8,128)(2,1)S(1)}, bf16[2,15,128,128]{3,2,1,0:T(8,128)(2,1)S(1)}, u32[]{:S(2)}, u32[]{:S(2)}) %collective-permute-start.6) | collective-permute-done | bytes 983072 | tf_op jit(solution)/shard_map/ppermute | solution.py:94
  138.8 1.1 copy-done.8
  139.9 13.5 %shard_map.70 = bf16[16,48,128]{2,1,0:T(8,128)(2,1)} custom-call(s32[8,6]{1,0:T(8,128)} %pattern.3, bf16[4,15,128,128]{3,2,1,0:T(8,128)(2,1)} %copy-done, bf16[4,15,128,128]{3,2,1,0:T(8,128)(2,1)} %copy-done.2, bf16[2,15,128,128]{3,2,1,0:T(8,128)(2,1)} %copy-done.6, bf16[2,15,128,128]{3,2,1,0:T(8,128)(2,1)} %copy-done.5, ...), custom_call_target="tpu_custom_call" | custom-call | tf_op jit(solution)/shard_map/pallas_call | solution.py:280
  153.4 20.3 %all_to_all.16.got = bf16[16,48,128]{2,1,0:T(8,128)(2,1)} all-to-all(bf16[16,48,128]{2,1,0:T(8,128)(2,1)} %shard_map.70), channel_id=1, replica_groups={{0,2,4,6,8,10,12,14,16,18,20,22,24,26,28,30},{1,3,5,7,9,11,13,15,17,19,..., dimensions={0} | all-to-all | bytes 393216 | tf_op jit(solution)/shard_map/all_to_all | solution.py:363
  173.7 1.8 %shard_map.71 = (bf16[128,512]{1,0:T(8,128)(2,1)}, f32[32,512]{1,0:T(8,128)}) custom-call(bf16[16,48,128]{2,1,0:T(8,128)(2,1)} %all_to_all.16.got, f32[32,512]{1,0:T(8,128)} %rhs_ext.1), custom_call_target="tpu_custom_call" | custom-call | tf_op jit(solution)/shard_map/pallas_call | solution.py:314
  (38 shorter events, 0.4 us)
Async XLA Ops:
  8.9 34.3 %all-to-all-start = ((bf16[8,128,128]{2,1,0:T(8,128)(2,1)}), bf16[8,128,128]{2,1,0:T(8,128)(2,1)S(1)}, u32[]{:S(2)}, u32[]{:S(2)}) async-start(bf16[8,128,128]{2,1,0:T(8,128)(2,1)} %shard_map.69), calls=%async_computation | async-start | bytes 524288 | tf_op jit(solution)/shard_map/all_to_all | solution.py:98
  26.6 113.2 %all-gather.4.cloned.1.call-start = ((), (), s32[]{:S(2)}) async-start(), calls=%async_computation.3 | async-start | bytes 10813440 | tf_op jit(solution)/shard_map/all_gather | solution.py:341
  28.7 33.0 %copy-start.9 = (bf16[128,128]{1,0:T(8,128)(2,1)S(1)}, bf16[128,128]{1,0:T(8,128)(2,1)}, u32[]{:S(2)}) copy-start(bf16[128,128]{1,0:T(8,128)(2,1)} %get-tuple-element.8) | copy-start | bytes 98308
  83.3 56.6 %copy-start = (bf16[4,15,128,128]{3,2,1,0:T(8,128)(2,1)}, bf16[4,15,128,128]{3,2,1,0:T(8,128)(2,1)S(1)}, u32[]{:S(2)}) copy-start(bf16[4,15,128,128]{3,2,1,0:T(8,128)(2,1)S(1)} %all_to_all.15.refs_0_) | copy-start | bytes 5898244
  83.3 28.0 %collective-permute-start.2 = (bf16[4,15,128,128]{3,2,1,0:T(8,128)(2,1)S(1)}, bf16[4,15,128,128]{3,2,1,0:T(8,128)(2,1)S(1)}, u32[]{:S(2)}, u32[]{:S(2)}) collective-permute-start(bf16[4,15,128,128]{3,2,1,0:T(8,128)(2,1)S(1)} %all_to_all.15.refs_0_), channel_id=1, source_target_pairs={{0,128},{1,33},{2,130},{3,35},{4,132},{5,37},{6,134},{7,39},{8,136... | collective-permute-start | bytes 5898248 | tf_op jit(solution)/shard_map/ppermute | solution.py:94
  89.2 27.8 %collective-permute-start = (bf16[4,15,128,128]{3,2,1,0:T(8,128)(2,1)S(1)}, bf16[4,15,128,128]{3,2,1,0:T(8,128)(2,1)S(1)}, u32[]{:S(2)}, u32[]{:S(2)}) collective-permute-start(bf16[4,15,128,128]{3,2,1,0:T(8,128)(2,1)S(1)} %all_to_all.15.refs_0_), channel_id=1, source_target_pairs={{0,384},{1,97},{2,386},{3,99},{4,388},{5,101},{6,390},{7,103},{8,3... | collective-permute-start | bytes 5898248 | tf_op jit(solution)/shard_map/ppermute | solution.py:94
  91.1 45.1 %collective-permute-start.4 = (bf16[4,15,128,128]{3,2,1,0:T(8,128)(2,1)S(1)}, bf16[4,15,128,128]{3,2,1,0:T(8,128)(2,1)S(1)}, u32[]{:S(2)}, u32[]{:S(2)}) collective-permute-start(bf16[4,15,128,128]{3,2,1,0:T(8,128)(2,1)S(1)} %all_to_all.15.refs_0_), channel_id=1, source_target_pairs={{0,1},{1,0},{2,3},{3,2},{4,5},{5,4},{6,7},{7,6},{8,9},{9,8},{10,11... | collective-permute-start | bytes 5898248 | tf_op jit(solution)/shard_map/ppermute | solution.py:94
  111.3 25.0 %copy-start.1 = (bf16[4,15,128,128]{3,2,1,0:T(8,128)(2,1)}, bf16[4,15,128,128]{3,2,1,0:T(8,128)(2,1)S(1)}, u32[]{:S(2)}) copy-start(bf16[4,15,128,128]{3,2,1,0:T(8,128)(2,1)S(1)} %collective-permute-done.2.refs_4_) | copy-start | bytes 5898244
  111.4 17.2 %collective-permute-start.3 = (bf16[2,15,128,128]{3,2,1,0:T(8,128)(2,1)S(1)}, bf16[2,15,128,128]{3,2,1,0:T(8,128)(2,1)S(1)}, u32[]{:S(2)}, u32[]{:S(2)}) collective-permute-start(bf16[2,15,128,128]{3,2,1,0:T(8,128)(2,1)S(1)} %slice.77), channel_id=1, source_target_pairs={{0,128},{1,33},{2,130},{3,35},{4,132},{5,37},{6,134},{7,39},{8,136... | collective-permute-start | bytes 2949128 | tf_op jit(solution)/shard_map/ppermute | solution.py:94
  117.0 19.3 %copy-start.2 = (bf16[4,15,128,128]{3,2,1,0:T(8,128)(2,1)}, bf16[4,15,128,128]{3,2,1,0:T(8,128)(2,1)S(1)}, u32[]{:S(2)}) copy-start(bf16[4,15,128,128]{3,2,1,0:T(8,128)(2,1)S(1)} %collective-permute-done.refs_1_) | copy-start | bytes 5898244
  117.1 17.2 %collective-permute-start.1 = (bf16[2,15,128,128]{3,2,1,0:T(8,128)(2,1)S(1)}, bf16[2,15,128,128]{3,2,1,0:T(8,128)(2,1)S(1)}, u32[]{:S(2)}, u32[]{:S(2)}) collective-permute-start(bf16[2,15,128,128]{3,2,1,0:T(8,128)(2,1)S(1)} %slice.76), channel_id=1, source_target_pairs={{0,384},{1,97},{2,386},{3,99},{4,388},{5,101},{6,390},{7,103},{8,3... | collective-permute-start | bytes 2949128 | tf_op jit(solution)/shard_map/ppermute | solution.py:94
  119.1 17.2 %collective-permute-start.8 = (bf16[4,15,128,128]{3,2,1,0:T(8,128)(2,1)S(1)}, bf16[4,15,128,128]{3,2,1,0:T(8,128)(2,1)S(1)}, u32[]{:S(2)}, u32[]{:S(2)}) collective-permute-start(bf16[4,15,128,128]{3,2,1,0:T(8,128)(2,1)S(1)} %collective-permute-done.2.refs_4_), channel_id=1, source_target_pairs={{0,1},{1,0},{2,3},{3,2},{4,5},{5,4},{6,7},{7,6},{8,9},{9,8},{10,11... | collective-permute-start | bytes 5898248 | tf_op jit(solution)/shard_map/ppermute | solution.py:94
  121.0 18.9 %collective-permute-start.5 = (bf16[4,15,128,128]{3,2,1,0:T(8,128)(2,1)S(1)}, bf16[4,15,128,128]{3,2,1,0:T(8,128)(2,1)}, u32[]{:S(2)}, u32[]{:S(2)}) collective-permute-start(bf16[4,15,128,128]{3,2,1,0:T(8,128)(2,1)S(1)} %collective-permute-done.refs_1_), channel_id=1, source_target_pairs={{0,1},{1,0},{2,3},{3,2},{4,5},{5,4},{6,7},{7,6},{8,9},{9,8},{10,11... | collective-permute-start | bytes 5898248 | tf_op jit(solution)/shard_map/ppermute | solution.py:94
  128.6 11.3 %copy-start.5 = (bf16[2,15,128,128]{3,2,1,0:T(8,128)(2,1)}, bf16[2,15,128,128]{3,2,1,0:T(8,128)(2,1)S(1)}, u32[]{:S(2)}) copy-start(bf16[2,15,128,128]{3,2,1,0:T(8,128)(2,1)S(1)} %collective-permute-done.3.refs_3_) | copy-start | bytes 2949124
  128.6 7.7 %collective-permute-start.7 = (bf16[2,15,128,128]{3,2,1,0:T(8,128)(2,1)S(1)}, bf16[2,15,128,128]{3,2,1,0:T(8,128)(2,1)S(1)}, u32[]{:S(2)}, u32[]{:S(2)}) collective-permute-start(bf16[2,15,128,128]{3,2,1,0:T(8,128)(2,1)S(1)} %collective-permute-done.3.refs_3_), channel_id=1, source_target_pairs={{0,1},{1,0},{2,3},{3,2},{4,5},{5,4},{6,7},{7,6},{8,9},{9,8},{10,11... | collective-permute-start | bytes 2949128 | tf_op jit(solution)/shard_map/ppermute | solution.py:94
  134.3 4.5 %copy-start.6 = (bf16[2,15,128,128]{3,2,1,0:T(8,128)(2,1)}, bf16[2,15,128,128]{3,2,1,0:T(8,128)(2,1)S(1)}, u32[]{:S(2)}) copy-start(bf16[2,15,128,128]{3,2,1,0:T(8,128)(2,1)S(1)} %collective-permute-done.1.refs_2_) | copy-start | bytes 2949124
  134.3 4.4 %collective-permute-start.6 = (bf16[2,15,128,128]{3,2,1,0:T(8,128)(2,1)S(1)}, bf16[2,15,128,128]{3,2,1,0:T(8,128)(2,1)S(1)}, u32[]{:S(2)}, u32[]{:S(2)}) collective-permute-start(bf16[2,15,128,128]{3,2,1,0:T(8,128)(2,1)S(1)} %collective-permute-done.1.refs_2_), channel_id=1, source_target_pairs={{0,1},{1,0},{2,3},{3,2},{4,5},{5,4},{6,7},{7,6},{8,9},{9,8},{10,11... | collective-permute-start | bytes 2949128 | tf_op jit(solution)/shard_map/ppermute | solution.py:94
  136.3 2.5 %copy-start.3 = (bf16[4,15,128,128]{3,2,1,0:T(8,128)(2,1)}, bf16[4,15,128,128]{3,2,1,0:T(8,128)(2,1)S(1)}, u32[]{:S(2)}) copy-start(bf16[4,15,128,128]{3,2,1,0:T(8,128)(2,1)S(1)} %collective-permute-done.4.refs_5_) | copy-start | bytes 5898244
  136.3 2.5 %copy-start.7 = (bf16[2,15,128,128]{3,2,1,0:T(8,128)(2,1)}, bf16[2,15,128,128]{3,2,1,0:T(8,128)(2,1)S(1)}, u32[]{:S(2)}) copy-start(bf16[2,15,128,128]{3,2,1,0:T(8,128)(2,1)S(1)} %collective-permute-done.7.refs_8_) | copy-start | bytes 2949124
  136.3 2.5 %copy-start.4 = (bf16[4,15,128,128]{3,2,1,0:T(8,128)(2,1)}, bf16[4,15,128,128]{3,2,1,0:T(8,128)(2,1)S(1)}, u32[]{:S(2)}) copy-start(bf16[4,15,128,128]{3,2,1,0:T(8,128)(2,1)S(1)} %collective-permute-done.8.refs_9_) | copy-start | bytes 5898244
  138.8 1.1 copy-start.8
Sparse Core Ops, SparseCore 0:
  61.8 75.6 all-gather.3

commit v7 on v6

--- a/solution.py
+++ b/solution.py
@@ -168,7 +168,7 @@
 
 def solve_kernel(pattern, *refs):
     pieces = refs[:10]
-    blobs, out, factor, invs, rows_ext, upd, ext, sol, *wsems, isems, esems = refs[10:]
+    blobs, out, factor, invs, rows_ext, upd, ext, sol, *wsems, isems, esem = refs[10:]
     my_y, my_x, _, core = coordinates()
 
     def load(first, count, sems):
@@ -183,7 +183,10 @@
         ]
 
     waves = [load(first, count, sems) for (first, count), sems in zip(WAVES, wsems)]
-    inv_loads, inv_lows, ext_loads = [], [], []
+    ext_load = pltpu.make_async_copy(
+        blobs.at[:, pl.ds(0, NZ_DEV), :, core], rows_ext, esem
+    )
+    inv_loads, inv_lows = [], []
     for s in range(SUPER):
         four = pl.ds(s * TPS, TPS)
         inv_loads.append(
@@ -199,15 +202,10 @@
                 isems.at[2 * s + 1],
             )
         )
-        ext_loads.append(
-            pltpu.make_async_copy(
-                blobs.at[four, pl.ds(0, NZ_DEV), :, core], rows_ext.at[four], esems.at[s]
-            )
-        )
     for wave, inv_load, inv_low in zip(waves, inv_loads, inv_lows):
         for c in wave + [inv_load, inv_low]:
             c.start()
-    for c in inv_loads[len(WAVES) :] + inv_lows[len(WAVES) :] + ext_loads:
+    for c in inv_loads[len(WAVES) :] + inv_lows[len(WAVES) :] + [ext_load]:
         c.start()
     upd[...] = jnp.zeros_like(upd)
     ext[...] = jnp.zeros_like(ext)
@@ -258,8 +256,8 @@
             more = nt(x_s, jnp.concatenate(rows, axis=0))
             for n in range(2):
                 upd[t + n] += more[:, n * TILE : (n + 1) * TILE]
+    ext_load.wait()
     for s in range(SUPER):
-        ext_loads[s].wait()
         x_s = jnp.concatenate([sol[s * TPS + j] for j in range(TPS)], axis=1)
         for k in range(NZ_DEV):
             rows = jnp.concatenate(
@@ -293,7 +291,7 @@
             pltpu.SemaphoreType.DMA((10,)),
             pltpu.SemaphoreType.DMA((10,)),
             pltpu.SemaphoreType.DMA((2 * SUPER,)),
-            pltpu.SemaphoreType.DMA((SUPER,)),
+            pltpu.SemaphoreType.DMA,
         ],
         compiler_params=pltpu.CompilerParams(vmem_limit_bytes=VMEM),
     )(pattern, *pieces, blobs)

time: 184 us -> 183 us (level)
  no operation moved by 1% of the time
where the time goes in v7:
time: 183 us; the launch traced here: 181 us
  blocking collectives  59.7 us (33%)
  waiting for transfers between devices  44.2 us (24%)
  starting transfers between devices  43.2 us (24%)
  Pallas kernels  18.2 us (10%)
  between operations  14.3 us (8%)
  local copies, waits for them, and re-layouts  1.83 us (1%)
    ppermute x9, waiting for transfers between devices, move(): return lax.ppermute(value, AXES, pairs)  29.7 us
    ppermute x9, starting transfers between devices, move(): return lax.ppermute(value, AXES, pairs)  25.4 us
    all_to_all x1, blocking collectives, exchange(): lax.all_to_all(value, AXES, 0, 0, tiled=True, axis_index_groups=groups)  20.9 us
    all_to_all x1, blocking collectives, local(): lax.all_to_all(packed, 'col', 0, 0, tiled=True, axis_index_groups=groups)  20.3 us
    all_gather x1, blocking collectives, local(): line = lax.all_gather(quad, AXES, axis_index_groups=near_groups())  18.5 us
    all_to_all x1, starting transfers between devices, exchange(): lax.all_to_all(value, AXES, 0, 0, tiled=True, axis_index_groups=groups)  17.8 us
    all_to_all x1, waiting for transfers between devices, exchange(): lax.all_to_all(value, AXES, 0, 0, tiled=True, axis_index_groups=groups)  14.4 us
    pallas_call x1, Pallas kernels, solve(): pl.pallas_call(solve_kernel, out_shape=jax.ShapeDtypeStruct((NZ, RZ + RZ...  12.5 us
  transfers between devices with their start and end apart: 11, of which 5 were waited for; matrix products, arithmetic and copies ran while one was open for 0% of the time, Pallas kernels for 1%

profile of v7, /device:TPU:24, one launch (start us, length us, event | category | flops | bytes accessed | tf_op | source)
XLA Modules:
  0.0 181.4 jit_solution(11157142178292441173)
XLA Ops:
  7.2 1.7 shard_map.69
  8.9 17.8 %all-to-all-start = ((bf16[8,128,128]{2,1,0:T(8,128)(2,1)}), bf16[8,128,128]{2,1,0:T(8,128)(2,1)S(1)}, u32[]{:S(2)}, u32[]{:S(2)}) async-start(bf16[8,128,128]{2,1,0:T(8,128)(2,1)} %shard_map.69), calls=%async_computation | async-start | bytes 524288 | tf_op jit(solution)/shard_map/all_to_all | solution.py:98
  26.6 2.1 %shard_map.68 = (bf16[1280,128]{1,0:T(8,128)(2,1)}, bf16[128,128]{1,0:T(8,128)(2,1)}) custom-call(bf16[768,128]{1,0:T(8,128)(2,1)} %off.3, bf16[128,512]{1,0:T(8,128)(2,1)} %inv.1, f32[2,128,512]{2,1,0:T(8,128)} %rhs.1), custom_call_target="tpu_custom_call" | custom-call | flops 1048576 | bytes 4194304 | tf_op jit(solution)/shard_map/pallas_call | solution.py:152
  28.7 14.4 %all-to-all-done = bf16[8,128,128]{2,1,0:T(8,128)(2,1)S(1)} async-done(((bf16[8,128,128]{2,1,0:T(8,128)(2,1)}), bf16[8,128,128]{2,1,0:T(8,128)(2,1)S(1)}, u32[]{:S(2)}, u32[]{:S(2)}) %all-to-all-start) | async-done | bytes 262176 | tf_op jit(solution)/shard_map/all_to_all | solution.py:98
  43.2 18.5 %all-gather = bf16[16,128,128]{2,1,0:T(8,128)(2,1)S(1)} all-gather(bf16[4,128,128]{2,1,0:T(8,128)(2,1)S(1)} %pad_maximum_fusion), channel_id=2, replica_groups={{0,2,4,6},{8,10,12,14},{16,18,20,22},{24,26,28,30},{1,3,5,7},{9,11,13,1..., dimensions={0}, use_global_device_ids=true | all-gather | bytes 655360 | tf_op jit(solution)/shard_map/all_gather | solution.py:337
  61.9 0.5 broadcast_in_dim.10
  62.3 20.9 %all_to_all.15.refs_0_ = bf16[4,15,128,128]{3,2,1,0:T(8,128)(2,1)S(1)} all-to-all(bf16[4,15,128,128]{3,2,1,0:T(8,128)(2,1)S(1)} %broadcast_in_dim.10), channel_id=1, replica_groups={{0,32,64,96},{128,160,192,224},{256,288,320,352},{384,416,448,480},{1,1..., dimensions={0} | all-to-all | bytes 3932160 | tf_op jit(solution)/shard_map/all_to_all | solution.py:98
  83.3 5.9 %collective-permute-start.2 = (bf16[4,15,128,128]{3,2,1,0:T(8,128)(2,1)S(1)}, bf16[4,15,128,128]{3,2,1,0:T(8,128)(2,1)S(1)}, u32[]{:S(2)}, u32[]{:S(2)}) collective-permute-start(bf16[4,15,128,128]{3,2,1,0:T(8,128)(2,1)S(1)} %all_to_all.15.refs_0_), channel_id=1, source_target_pairs={{0,128},{1,33},{2,130},{3,35},{4,132},{5,37},{6,134},{7,39},{8,136... | collective-permute-start | bytes 5898248 | tf_op jit(solution)/shard_map/ppermute | solution.py:94
  89.2 1.9 %collective-permute-start = (bf16[4,15,128,128]{3,2,1,0:T(8,128)(2,1)S(1)}, bf16[4,15,128,128]{3,2,1,0:T(8,128)(2,1)S(1)}, u32[]{:S(2)}, u32[]{:S(2)}) collective-permute-start(bf16[4,15,128,128]{3,2,1,0:T(8,128)(2,1)S(1)} %all_to_all.15.refs_0_), channel_id=1, source_target_pairs={{0,384},{1,97},{2,386},{3,99},{4,388},{5,101},{6,390},{7,103},{8,3... | collective-permute-start | bytes 5898248 | tf_op jit(solution)/shard_map/ppermute | solution.py:94
  91.1 1.9 %collective-permute-start.4 = (bf16[4,15,128,128]{3,2,1,0:T(8,128)(2,1)S(1)}, bf16[4,15,128,128]{3,2,1,0:T(8,128)(2,1)S(1)}, u32[]{:S(2)}, u32[]{:S(2)}) collective-permute-start(bf16[4,15,128,128]{3,2,1,0:T(8,128)(2,1)S(1)} %all_to_all.15.refs_0_), channel_id=1, source_target_pairs={{0,1},{1,0},{2,3},{3,2},{4,5},{5,4},{6,7},{7,6},{8,9},{9,8},{10,11... | collective-permute-start | bytes 5898248 | tf_op jit(solution)/shard_map/ppermute | solution.py:94
  93.0 18.3 %collective-permute-done.2.refs_4_ = bf16[4,15,128,128]{3,2,1,0:T(8,128)(2,1)S(1)} collective-permute-done((bf16[4,15,128,128]{3,2,1,0:T(8,128)(2,1)S(1)}, bf16[4,15,128,128]{3,2,1,0:T(8,128)(2,1)S(1)}, u32[]{:S(2)}, u32[]{:S(2)}) %collective-permute-start.2) | collective-permute-done | bytes 1966112 | tf_op jit(solution)/shard_map/ppermute | solution.py:94
  111.4 5.6 %collective-permute-start.3 = (bf16[2,15,128,128]{3,2,1,0:T(8,128)(2,1)S(1)}, bf16[2,15,128,128]{3,2,1,0:T(8,128)(2,1)S(1)}, u32[]{:S(2)}, u32[]{:S(2)}) collective-permute-start(bf16[2,15,128,128]{3,2,1,0:T(8,128)(2,1)S(1)} %slice.77), channel_id=1, source_target_pairs={{0,128},{1,33},{2,130},{3,35},{4,132},{5,37},{6,134},{7,39},{8,136... | collective-permute-start | bytes 2949128 | tf_op jit(solution)/shard_map/ppermute | solution.py:94
  117.1 1.9 %collective-permute-start.1 = (bf16[2,15,128,128]{3,2,1,0:T(8,128)(2,1)S(1)}, bf16[2,15,128,128]{3,2,1,0:T(8,128)(2,1)S(1)}, u32[]{:S(2)}, u32[]{:S(2)}) collective-permute-start(bf16[2,15,128,128]{3,2,1,0:T(8,128)(2,1)S(1)} %slice.76), channel_id=1, source_target_pairs={{0,384},{1,97},{2,386},{3,99},{4,388},{5,101},{6,390},{7,103},{8,3... | collective-permute-start | bytes 2949128 | tf_op jit(solution)/shard_map/ppermute | solution.py:94
  119.1 1.9 %collective-permute-start.8 = (bf16[4,15,128,128]{3,2,1,0:T(8,128)(2,1)S(1)}, bf16[4,15,128,128]{3,2,1,0:T(8,128)(2,1)S(1)}, u32[]{:S(2)}, u32[]{:S(2)}) collective-permute-start(bf16[4,15,128,128]{3,2,1,0:T(8,128)(2,1)S(1)} %collective-permute-done.2.refs_4_), channel_id=1, source_target_pairs={{0,1},{1,0},{2,3},{3,2},{4,5},{5,4},{6,7},{7,6},{8,9},{9,8},{10,11... | collective-permute-start | bytes 5898248 | tf_op jit(solution)/shard_map/ppermute | solution.py:94
  121.0 2.4 %collective-permute-start.5 = (bf16[4,15,128,128]{3,2,1,0:T(8,128)(2,1)S(1)}, bf16[4,15,128,128]{3,2,1,0:T(8,128)(2,1)}, u32[]{:S(2)}, u32[]{:S(2)}) collective-permute-start(bf16[4,15,128,128]{3,2,1,0:T(8,128)(2,1)S(1)} %collective-permute-done.refs_1_), channel_id=1, source_target_pairs={{0,1},{1,0},{2,3},{3,2},{4,5},{5,4},{6,7},{7,6},{8,9},{9,8},{10,11... | collective-permute-start | bytes 5898248 | tf_op jit(solution)/shard_map/ppermute | solution.py:94
  123.4 5.2 %collective-permute-done.3.refs_3_ = bf16[2,15,128,128]{3,2,1,0:T(8,128)(2,1)S(1)} collective-permute-done((bf16[2,15,128,128]{3,2,1,0:T(8,128)(2,1)S(1)}, bf16[2,15,128,128]{3,2,1,0:T(8,128)(2,1)S(1)}, u32[]{:S(2)}, u32[]{:S(2)}) %collective-permute-start.3) | collective-permute-done | bytes 983072 | tf_op jit(solution)/shard_map/ppermute | solution.py:94
  128.6 1.9 %collective-permute-start.7 = (bf16[2,15,128,128]{3,2,1,0:T(8,128)(2,1)S(1)}, bf16[2,15,128,128]{3,2,1,0:T(8,128)(2,1)S(1)}, u32[]{:S(2)}, u32[]{:S(2)}) collective-permute-start(bf16[2,15,128,128]{3,2,1,0:T(8,128)(2,1)S(1)} %collective-permute-done.3.refs_3_), channel_id=1, source_target_pairs={{0,1},{1,0},{2,3},{3,2},{4,5},{5,4},{6,7},{7,6},{8,9},{9,8},{10,11... | collective-permute-start | bytes 2949128 | tf_op jit(solution)/shard_map/ppermute | solution.py:94
  130.5 3.8 %collective-permute-done.1.refs_2_ = bf16[2,15,128,128]{3,2,1,0:T(8,128)(2,1)S(1)} collective-permute-done((bf16[2,15,128,128]{3,2,1,0:T(8,128)(2,1)S(1)}, bf16[2,15,128,128]{3,2,1,0:T(8,128)(2,1)S(1)}, u32[]{:S(2)}, u32[]{:S(2)}) %collective-permute-start.1) | collective-permute-done | bytes 983072 | tf_op jit(solution)/shard_map/ppermute | solution.py:94
  134.3 1.9 %collective-permute-start.6 = (bf16[2,15,128,128]{3,2,1,0:T(8,128)(2,1)S(1)}, bf16[2,15,128,128]{3,2,1,0:T(8,128)(2,1)S(1)}, u32[]{:S(2)}, u32[]{:S(2)}) collective-permute-start(bf16[2,15,128,128]{3,2,1,0:T(8,128)(2,1)S(1)} %collective-permute-done.1.refs_2_), channel_id=1, source_target_pairs={{0,1},{1,0},{2,3},{3,2},{4,5},{5,4},{6,7},{7,6},{8,9},{9,8},{10,11... | collective-permute-start | bytes 2949128 | tf_op jit(solution)/shard_map/ppermute | solution.py:94
  136.3 2.5 %collective-permute-done.6.refs_7_ = bf16[2,15,128,128]{3,2,1,0:T(8,128)(2,1)S(1)} collective-permute-done((bf16[2,15,128,128]{3,2,1,0:T(8,128)(2,1)S(1)}, bf16[2,15,128,128]{3,2,1,0:T(8,128)(2,1)S(1)}, u32[]{:S(2)}, u32[]{:S(2)}) %collective-permute-start.6) | collective-permute-done | bytes 983072 | tf_op jit(solution)/shard_map/ppermute | solution.py:94
  138.8 1.1 copy-done.8
  139.9 12.5 %shard_map.70 = bf16[16,48,128]{2,1,0:T(8,128)(2,1)} custom-call(s32[8,6]{1,0:T(8,128)} %pattern.3, bf16[4,15,128,128]{3,2,1,0:T(8,128)(2,1)} %copy-done, bf16[4,15,128,128]{3,2,1,0:T(8,128)(2,1)} %copy-done.2, bf16[2,15,128,128]{3,2,1,0:T(8,128)(2,1)} %copy-done.6, bf16[2,15,128,128]{3,2,1,0:T(8,128)(2,1)} %copy-done.5, ...), custom_call_target="tpu_custom_call" | custom-call | tf_op jit(solution)/shard_map/pallas_call | solution.py:278
  152.4 20.3 %all_to_all.16.got = bf16[16,48,128]{2,1,0:T(8,128)(2,1)} all-to-all(bf16[16,48,128]{2,1,0:T(8,128)(2,1)} %shard_map.70), channel_id=1, replica_groups={{0,2,4,6,8,10,12,14,16,18,20,22,24,26,28,30},{1,3,5,7,9,11,13,15,17,19,..., dimensions={0} | all-to-all | bytes 393216 | tf_op jit(solution)/shard_map/all_to_all | solution.py:361
  172.8 1.8 %shard_map.71 = (bf16[128,512]{1,0:T(8,128)(2,1)}, f32[32,512]{1,0:T(8,128)}) custom-call(bf16[16,48,128]{2,1,0:T(8,128)(2,1)} %all_to_all.16.got, f32[32,512]{1,0:T(8,128)} %rhs_ext.1), custom_call_target="tpu_custom_call" | custom-call | tf_op jit(solution)/shard_map/pallas_call | solution.py:312
  (38 shorter events, 0.4 us)
Async XLA Ops:
  8.9 34.3 %all-to-all-start = ((bf16[8,128,128]{2,1,0:T(8,128)(2,1)}), bf16[8,128,128]{2,1,0:T(8,128)(2,1)S(1)}, u32[]{:S(2)}, u32[]{:S(2)}) async-start(bf16[8,128,128]{2,1,0:T(8,128)(2,1)} %shard_map.69), calls=%async_computation | async-start | bytes 524288 | tf_op jit(solution)/shard_map/all_to_all | solution.py:98
  26.6 113.2 %all-gather.4.cloned.1.call-start = ((), (), s32[]{:S(2)}) async-start(), calls=%async_computation.3 | async-start | bytes 10813440 | tf_op jit(solution)/shard_map/all_gather | solution.py:339
  28.7 33.0 %copy-start.9 = (bf16[128,128]{1,0:T(8,128)(2,1)S(1)}, bf16[128,128]{1,0:T(8,128)(2,1)}, u32[]{:S(2)}) copy-start(bf16[128,128]{1,0:T(8,128)(2,1)} %get-tuple-element.8) | copy-start | bytes 98308
  83.3 56.6 %copy-start = (bf16[4,15,128,128]{3,2,1,0:T(8,128)(2,1)}, bf16[4,15,128,128]{3,2,1,0:T(8,128)(2,1)S(1)}, u32[]{:S(2)}) copy-start(bf16[4,15,128,128]{3,2,1,0:T(8,128)(2,1)S(1)} %all_to_all.15.refs_0_) | copy-start | bytes 5898244
  83.3 28.0 %collective-permute-start.2 = (bf16[4,15,128,128]{3,2,1,0:T(8,128)(2,1)S(1)}, bf16[4,15,128,128]{3,2,1,0:T(8,128)(2,1)S(1)}, u32[]{:S(2)}, u32[]{:S(2)}) collective-permute-start(bf16[4,15,128,128]{3,2,1,0:T(8,128)(2,1)S(1)} %all_to_all.15.refs_0_), channel_id=1, source_target_pairs={{0,128},{1,33},{2,130},{3,35},{4,132},{5,37},{6,134},{7,39},{8,136... | collective-permute-start | bytes 5898248 | tf_op jit(solution)/shard_map/ppermute | solution.py:94
  89.2 27.8 %collective-permute-start = (bf16[4,15,128,128]{3,2,1,0:T(8,128)(2,1)S(1)}, bf16[4,15,128,128]{3,2,1,0:T(8,128)(2,1)S(1)}, u32[]{:S(2)}, u32[]{:S(2)}) collective-permute-start(bf16[4,15,128,128]{3,2,1,0:T(8,128)(2,1)S(1)} %all_to_all.15.refs_0_), channel_id=1, source_target_pairs={{0,384},{1,97},{2,386},{3,99},{4,388},{5,101},{6,390},{7,103},{8,3... | collective-permute-start | bytes 5898248 | tf_op jit(solution)/shard_map/ppermute | solution.py:94
  91.1 45.1 %collective-permute-start.4 = (bf16[4,15,128,128]{3,2,1,0:T(8,128)(2,1)S(1)}, bf16[4,15,128,128]{3,2,1,0:T(8,128)(2,1)S(1)}, u32[]{:S(2)}, u32[]{:S(2)}) collective-permute-start(bf16[4,15,128,128]{3,2,1,0:T(8,128)(2,1)S(1)} %all_to_all.15.refs_0_), channel_id=1, source_target_pairs={{0,1},{1,0},{2,3},{3,2},{4,5},{5,4},{6,7},{7,6},{8,9},{9,8},{10,11... | collective-permute-start | bytes 5898248 | tf_op jit(solution)/shard_map/ppermute | solution.py:94
  111.3 25.0 %copy-start.1 = (bf16[4,15,128,128]{3,2,1,0:T(8,128)(2,1)}, bf16[4,15,128,128]{3,2,1,0:T(8,128)(2,1)S(1)}, u32[]{:S(2)}) copy-start(bf16[4,15,128,128]{3,2,1,0:T(8,128)(2,1)S(1)} %collective-permute-done.2.refs_4_) | copy-start | bytes 5898244
  111.4 17.2 %collective-permute-start.3 = (bf16[2,15,128,128]{3,2,1,0:T(8,128)(2,1)S(1)}, bf16[2,15,128,128]{3,2,1,0:T(8,128)(2,1)S(1)}, u32[]{:S(2)}, u32[]{:S(2)}) collective-permute-start(bf16[2,15,128,128]{3,2,1,0:T(8,128)(2,1)S(1)} %slice.77), channel_id=1, source_target_pairs={{0,128},{1,33},{2,130},{3,35},{4,132},{5,37},{6,134},{7,39},{8,136... | collective-permute-start | bytes 2949128 | tf_op jit(solution)/shard_map/ppermute | solution.py:94
  117.0 19.3 %copy-start.2 = (bf16[4,15,128,128]{3,2,1,0:T(8,128)(2,1)}, bf16[4,15,128,128]{3,2,1,0:T(8,128)(2,1)S(1)}, u32[]{:S(2)}) copy-start(bf16[4,15,128,128]{3,2,1,0:T(8,128)(2,1)S(1)} %collective-permute-done.refs_1_) | copy-start | bytes 5898244
  117.1 17.2 %collective-permute-start.1 = (bf16[2,15,128,128]{3,2,1,0:T(8,128)(2,1)S(1)}, bf16[2,15,128,128]{3,2,1,0:T(8,128)(2,1)S(1)}, u32[]{:S(2)}, u32[]{:S(2)}) collective-permute-start(bf16[2,15,128,128]{3,2,1,0:T(8,128)(2,1)S(1)} %slice.76), channel_id=1, source_target_pairs={{0,384},{1,97},{2,386},{3,99},{4,388},{5,101},{6,390},{7,103},{8,3... | collective-permute-start | bytes 2949128 | tf_op jit(solution)/shard_map/ppermute | solution.py:94
  119.1 17.2 %collective-permute-start.8 = (bf16[4,15,128,128]{3,2,1,0:T(8,128)(2,1)S(1)}, bf16[4,15,128,128]{3,2,1,0:T(8,128)(2,1)S(1)}, u32[]{:S(2)}, u32[]{:S(2)}) collective-permute-start(bf16[4,15,128,128]{3,2,1,0:T(8,128)(2,1)S(1)} %collective-permute-done.2.refs_4_), channel_id=1, source_target_pairs={{0,1},{1,0},{2,3},{3,2},{4,5},{5,4},{6,7},{7,6},{8,9},{9,8},{10,11... | collective-permute-start | bytes 5898248 | tf_op jit(solution)/shard_map/ppermute | solution.py:94
  121.0 18.9 %collective-permute-start.5 = (bf16[4,15,128,128]{3,2,1,0:T(8,128)(2,1)S(1)}, bf16[4,15,128,128]{3,2,1,0:T(8,128)(2,1)}, u32[]{:S(2)}, u32[]{:S(2)}) collective-permute-start(bf16[4,15,128,128]{3,2,1,0:T(8,128)(2,1)S(1)} %collective-permute-done.refs_1_), channel_id=1, source_target_pairs={{0,1},{1,0},{2,3},{3,2},{4,5},{5,4},{6,7},{7,6},{8,9},{9,8},{10,11... | collective-permute-start | bytes 5898248 | tf_op jit(solution)/shard_map/ppermute | solution.py:94
  128.6 11.3 %copy-start.5 = (bf16[2,15,128,128]{3,2,1,0:T(8,128)(2,1)}, bf16[2,15,128,128]{3,2,1,0:T(8,128)(2,1)S(1)}, u32[]{:S(2)}) copy-start(bf16[2,15,128,128]{3,2,1,0:T(8,128)(2,1)S(1)} %collective-permute-done.3.refs_3_) | copy-start | bytes 2949124
  128.6 7.7 %collective-permute-start.7 = (bf16[2,15,128,128]{3,2,1,0:T(8,128)(2,1)S(1)}, bf16[2,15,128,128]{3,2,1,0:T(8,128)(2,1)S(1)}, u32[]{:S(2)}, u32[]{:S(2)}) collective-permute-start(bf16[2,15,128,128]{3,2,1,0:T(8,128)(2,1)S(1)} %collective-permute-done.3.refs_3_), channel_id=1, source_target_pairs={{0,1},{1,0},{2,3},{3,2},{4,5},{5,4},{6,7},{7,6},{8,9},{9,8},{10,11... | collective-permute-start | bytes 2949128 | tf_op jit(solution)/shard_map/ppermute | solution.py:94
  134.3 4.5 %copy-start.6 = (bf16[2,15,128,128]{3,2,1,0:T(8,128)(2,1)}, bf16[2,15,128,128]{3,2,1,0:T(8,128)(2,1)S(1)}, u32[]{:S(2)}) copy-start(bf16[2,15,128,128]{3,2,1,0:T(8,128)(2,1)S(1)} %collective-permute-done.1.refs_2_) | copy-start | bytes 2949124
  134.3 4.4 %collective-permute-start.6 = (bf16[2,15,128,128]{3,2,1,0:T(8,128)(2,1)S(1)}, bf16[2,15,128,128]{3,2,1,0:T(8,128)(2,1)S(1)}, u32[]{:S(2)}, u32[]{:S(2)}) collective-permute-start(bf16[2,15,128,128]{3,2,1,0:T(8,128)(2,1)S(1)} %collective-permute-done.1.refs_2_), channel_id=1, source_target_pairs={{0,1},{1,0},{2,3},{3,2},{4,5},{5,4},{6,7},{7,6},{8,9},{9,8},{10,11... | collective-permute-start | bytes 2949128 | tf_op jit(solution)/shard_map/ppermute | solution.py:94
  136.3 2.5 %copy-start.3 = (bf16[4,15,128,128]{3,2,1,0:T(8,128)(2,1)}, bf16[4,15,128,128]{3,2,1,0:T(8,128)(2,1)S(1)}, u32[]{:S(2)}) copy-start(bf16[4,15,128,128]{3,2,1,0:T(8,128)(2,1)S(1)} %collective-permute-done.4.refs_5_) | copy-start | bytes 5898244
  136.3 2.5 %copy-start.7 = (bf16[2,15,128,128]{3,2,1,0:T(8,128)(2,1)}, bf16[2,15,128,128]{3,2,1,0:T(8,128)(2,1)S(1)}, u32[]{:S(2)}) copy-start(bf16[2,15,128,128]{3,2,1,0:T(8,128)(2,1)S(1)} %collective-permute-done.7.refs_8_) | copy-start | bytes 2949124
  136.3 2.5 %copy-start.4 = (bf16[4,15,128,128]{3,2,1,0:T(8,128)(2,1)}, bf16[4,15,128,128]{3,2,1,0:T(8,128)(2,1)S(1)}, u32[]{:S(2)}) copy-start(bf16[4,15,128,128]{3,2,1,0:T(8,128)(2,1)S(1)} %collective-permute-done.8.refs_9_) | copy-start | bytes 5898244
  138.8 1.1 copy-start.8
Sparse Core Ops, SparseCore 0:
  61.8 75.6 all-gather.3
